TPU v7x, 256 devices: a whole 4x4x8 slice. The times are simulated.
256 devices in a mesh: leaf: 64 (over z, x, core), panel: 4 (over y).
Axes of the slice: x: 4, y: 4, z: 8, core: 2. Of those that a mesh axis runs over, the one named last changes fastest.
Arguments:
- rhs: bfloat16 [3, 64, 64, 1024], P(None, 'leaf', None, 'panel'), may hold values from -6 to 6
- inv_diag: bfloat16 [3, 64, 1024, 1024], P(None, 'leaf', 'panel'), as said below
- coupling: bfloat16 [2, 64, 1024, 512], P(None, 'leaf', None, 'panel'), may hold values from -0.1875 to 0.1875
- row_lists: int32 [2, 64, 512], replicated, may hold values from 0 to 1023, as said below
- parents: int32 [2, 64], replicated, may hold values from 0 to 63
- counts: int32 [2, 64], replicated, may hold values from 1 to 512, as said below
Outputs:
- forward_part: bfloat16 [3, 64, 64, 1024], P(None, 'leaf', None, 'panel')
- solution: bfloat16 [3, 64, 64, 1024], P(None, 'leaf', None, 'panel')
Inputs may be any that keep to these rules, and one draw needn't show every extreme that they name: `inv_diag`: each inverse diagonal block is lower triangular with a positive diagonal. `row_lists`: each slot's list names 512 different rows. `counts`: in every level some slot has all 512 columns live.
All inputs are finite; a program needn't handle non-finite values.
Results may differ from a plain program's by a relative error of at most 0.01.
Values may be sent and summed in bfloat16 or wider, within the bound.
No kernel may reach another device: no remote copies, remote signals or barrier semaphores. Data moves between devices by JAX's collectives and lax.ppermute only.
A program may use at most 64 MiB of HBM per device.

v0:
```python
import jax
import jax.numpy as jnp
from jax import lax
from jax.sharding import PartitionSpec as P


def add_into(total, flat_index, piece):
    count_here = piece.shape[0]
    rhs_cols = piece.shape[1]
    width_here = piece.shape[2]
    targets = total.shape[1]
    block_rows = max(1, min(count_here, (1 << 22) // (width_here * targets)))
    block_count = -(-count_here // block_rows)
    piece = piece.reshape(block_count, block_rows, rhs_cols, width_here)
    flat_index = flat_index.reshape(block_count, block_rows, width_here)
    target_ids = jnp.arange(targets, dtype=jnp.int32)

    def add_block(running, members):
        values, indices = members
        onehot = (indices[:, :, None] == target_ids[None, None, :]).astype(jnp.bfloat16)
        return (
            running + jnp.einsum("crj,cjt->rt", values, onehot, preferred_element_type=jnp.float32),
            None,
        )

    total, _ = lax.scan(add_block, total, (piece, flat_index))
    return total


def local(rhs, inv_diag, coupling, row_lists, parents, counts):
    levels = rhs.shape[0]
    local_slots = rhs.shape[1]
    rhs_cols = rhs.shape[2]
    quarter = rhs.shape[3]
    part_cols = coupling.shape[3]
    leaf_pos = lax.axis_index("leaf")
    panel_pos = lax.axis_index("panel")
    leaf_count = lax.axis_size("leaf")
    panel_count = lax.axis_size("panel")
    first_slot = leaf_pos * local_slots
    col_base = panel_pos * part_cols
    column_ids = col_base + jnp.arange(part_cols, dtype=jnp.int32)
    accum = jnp.zeros((local_slots, rhs_cols, quarter), jnp.float32)
    forward_levels = []
    for level in range(levels):
        resid_local = (rhs[level].astype(jnp.float32) - accum).astype(jnp.bfloat16)
        resid_whole = lax.all_gather(resid_local, "panel", axis=2, tiled=True)
        forward = jnp.einsum(
            "srw,svw->srv", resid_whole, inv_diag[level], preferred_element_type=jnp.float32
        ).astype(jnp.bfloat16)
        forward_levels.append(forward)
        if level < levels - 1:
            block_level = coupling[level]
            lists_level = row_lists[level]
            parent_level = parents[level]
            mine_counts = lax.dynamic_slice_in_dim(counts[level], first_slot, local_slots)
            update = jnp.einsum(
                "srw,swj->srj",
                lax.all_gather(forward, "panel", axis=2, tiled=True),
                block_level,
                preferred_element_type=jnp.float32,
            )
            alive = column_ids[None, None, :] < mine_counts[:, None, None]
            update = jnp.where(alive, update, 0.0).astype(jnp.bfloat16)
            lists_table = jnp.transpose(
                lists_level.reshape(leaf_count, local_slots, panel_count, part_cols), (0, 2, 1, 3)
            ).reshape(-1, part_cols)
            parent_table = jnp.broadcast_to(
                parent_level.reshape(leaf_count, 1, local_slots),
                (leaf_count, panel_count, local_slots),
            ).reshape(-1)
            target = parent_table - first_slot
            lower_edge = panel_pos * quarter
            valid = ((target >= 0) & (target < local_slots))[:, None]
            valid = valid & (lists_table >= lower_edge) & (lists_table < lower_edge + quarter)
            flat_index = jnp.where(
                valid, target[:, None] * quarter + lists_table - lower_edge, local_slots * quarter
            )
            folded = add_into(
                jnp.zeros((rhs_cols, local_slots * quarter), jnp.float32),
                flat_index,
                lax.all_gather(update, ("leaf", "panel"), axis=0, tiled=True),
            )
            accum = jnp.transpose(folded.reshape(rhs_cols, local_slots, quarter), (1, 0, 2))
    solved = [None] * levels
    for level in reversed(range(levels)):
        forward = forward_levels[level]
        if level == levels - 1:
            reduced = forward
        else:
            upper = solved[level + 1]
            mine_parents = lax.dynamic_slice_in_dim(parents[level], first_slot, local_slots)
            mine_counts = lax.dynamic_slice_in_dim(counts[level], first_slot, local_slots)
            mine_lists = lax.dynamic_slice(
                row_lists[level], (first_slot, col_base), (local_slots, part_cols)
            )
            piece = lax.all_gather(upper, "leaf", axis=0, tiled=True)
            row_here = jnp.arange(piece.shape[0], dtype=jnp.int32)
            match = (mine_parents[:, None] == row_here[None, :]).astype(jnp.bfloat16)
            chosen = jnp.einsum(
                "km,mrw->krw", match, piece, preferred_element_type=jnp.float32
            ).astype(jnp.bfloat16)
            chosen_whole = lax.all_gather(chosen, "panel", axis=2, tiled=True)
            picked = jnp.take_along_axis(chosen_whole, mine_lists[:, None, :], axis=2)
            alive = column_ids[None, None, :] < mine_counts[:, None, None]
            picked = jnp.where(alive, picked, jnp.zeros((), picked.dtype))
            back_partial = jnp.einsum(
                "srj,swj->srw", picked, coupling[level], preferred_element_type=jnp.float32
            )
            back_term = lax.psum_scatter(back_partial, "panel", scatter_dimension=2, tiled=True)
            reduced = (forward.astype(jnp.float32) - back_term).astype(jnp.bfloat16)
        solve_partial = jnp.einsum(
            "srv,svw->srw", reduced, inv_diag[level], preferred_element_type=jnp.float32
        )
        solved[level] = lax.psum_scatter(
            solve_partial, "panel", scatter_dimension=2, tiled=True
        ).astype(jnp.bfloat16)
    return (jnp.stack(forward_levels), jnp.stack(solved))


def solution(mesh):
    placed = (
        P(None, "leaf", None, "panel"),
        P(None, "leaf", "panel", None),
        P(None, "leaf", None, "panel"),
        P(),
        P(),
        P(),
    )
    return jax.shard_map(
        local,
        mesh=mesh,
        in_specs=placed,
        out_specs=(P(None, "leaf", None, "panel"), P(None, "leaf", None, "panel")),
        check_vma=False,
    )
```

profile of v0, /device:TPU:24, one launch (start us, length us, event | category | flops | bytes accessed | tf_op | source)
XLA Modules:
  0.0 640.2 jit_solution(11144560001103592362)
XLA Ops:
  8.7 12.0 %all-gather = bf16[1,1,64,1024]{3,2,1,0:T(8,128)(2,1)S(1)} all-gather(bf16[1,1,64,256]{3,2,1,0:T(8,128)(2,1)S(1)} %slice.53), channel_id=2, replica_groups=mesh['leaf'=64,'panel'=4] {'panel'}, dimensions={3}, use_global_device_ids=true | all-gather | bytes 163840 | tf_op jit(solution)/shard_map/all_gather | solution.py:47
  20.7 1.3 convolution_convert_fusion.2
  22.0 12.0 %all-gather.1 = bf16[64,1024]{1,0:T(8,128)(2,1)S(1)} all-gather(bf16[64,256]{1,0:T(8,128)(2,1)S(1)} %convolution_convert_fusion.2), channel_id=3, replica_groups=mesh['leaf'=64,'panel'=4] {'panel'}, dimensions={1}, use_global_device_ids=true | all-gather | bytes 163840 | tf_op jit(solution)/shard_map/all_gather | solution.py:59
  35.3 1.7 fusion.30
  40.9 113.7 %all-gather.18.cloned.1.call-done = bf16[16384,128]{1,0:T(8,128)(2,1)} async-done(((bf16[64,128]{1,0:T(8,128)(2,1)}), bf16[16384,128]{1,0:T(8,128)(2,1)}) %all-gather.18.cloned.1.call-update) | async-done | bytes 4194320 | tf_op jit(solution)/shard_map/all_gather | solution.py:82
  154.7 9.4 %while.22 = (s32[]{:T(128)}, f32[64,256]{1,0:T(8,128)S(1)}, bf16[2,128,64,128]{3,2,1,0:T(8,128)(2,1)}, s32[2,128,128]{2,1,0:T(8,128)S(1)}, s32[]{:T(128)}, /*index=5*/s32[]{:T(128)}) while((s32[]{:T(128)}, f32[64,256]{1,0:T(8,128)S(1)}, bf16[2,128,64,128]{3,2,1,0:T(8,128)(2,1)}, s32[2,128,128]{2,1,0:T(8,128)S(1)}, s32[]{:T(128)}, ...), condition=%wide.region_1.2_spmd.clone, body=%wide.region_0.1_spmd.clone.sunk | while | flops 541097984 | bytes 2424927 | solution.py:26
  154.7 4.7 fusion.103
  159.5 4.6 fusion.103
  164.1 12.1 %all-gather.3 = bf16[64,1024]{1,0:T(8,128)(2,1)S(1)} all-gather(bf16[64,256]{1,0:T(8,128)(2,1)S(1)} %fusion.56), channel_id=5, replica_groups=mesh['leaf'=64,'panel'=4] {'panel'}, dimensions={1}, use_global_device_ids=true | all-gather | bytes 163840 | tf_op jit(solution)/shard_map/all_gather | solution.py:47
  176.5 12.0 %all-gather.4 = bf16[64,1024]{1,0:T(8,128)(2,1)S(1)} all-gather(bf16[64,256]{1,0:T(8,128)(2,1)S(1)} %convolution_convert_fusion.1), channel_id=6, replica_groups=mesh['leaf'=64,'panel'=4] {'panel'}, dimensions={1}, use_global_device_ids=true | all-gather | bytes 163840 | tf_op jit(solution)/shard_map/all_gather | solution.py:59
  190.1 111.4 %all-gather.20.cloned.1.call-done = bf16[16384,128]{1,0:T(8,128)(2,1)} async-done(((bf16[64,128]{1,0:T(8,128)(2,1)}), bf16[16384,128]{1,0:T(8,128)(2,1)}) %all-gather.20.cloned.1.call-update) | async-done | bytes 4194320 | tf_op jit(solution)/shard_map/all_gather | solution.py:82
  301.5 9.2 %while.23 = (s32[]{:T(128)}, f32[64,256]{1,0:T(8,128)S(1)}, bf16[2,128,64,128]{3,2,1,0:T(8,128)(2,1)}, s32[2,128,128]{2,1,0:T(8,128)S(1)}, s32[]{:T(128)}, /*index=5*/s32[]{:T(128)}) while((s32[]{:T(128)}, f32[64,256]{1,0:T(8,128)S(1)}, bf16[2,128,64,128]{3,2,1,0:T(8,128)(2,1)}, s32[2,128,128]{2,1,0:T(8,128)S(1)}, s32[]{:T(128)}, ...), condition=%wide.region_3.4_spmd.clone, body=%wide.region_2.3_spmd.clone.sunk | while | flops 541097984 | bytes 2424927 | solution.py:26
  301.5 4.6 fusion.105
  306.2 4.6 fusion.105
  310.8 12.1 %all-gather.6 = bf16[64,1024]{1,0:T(8,128)(2,1)S(1)} all-gather(bf16[64,256]{1,0:T(8,128)(2,1)S(1)} %fusion.55), channel_id=8, replica_groups=mesh['leaf'=64,'panel'=4] {'panel'}, dimensions={1}, use_global_device_ids=true | all-gather | bytes 163840 | tf_op jit(solution)/shard_map/all_gather | solution.py:47
  324.2 18.5 %reduce-scatter.6.cloned.1.call-done = f32[1,64,256]{2,1,0:T(8,128)} async-done(((f32[1,64,1024]{2,1,0:T(8,128)}), f32[1,64,256]{2,1,0:T(8,128)}) %reduce-scatter.6.cloned.1.call-update) | async-done | bytes 65552 | tf_op jit(solution)/shard_map/reduce_scatter | solution.py:115
  342.7 1.5 convert_element_type.114
  344.9 80.2 %all-gather.14.cloned.1.call-done = bf16[64,64,256]{2,1,0:T(8,128)(2,1)} async-done(((bf16[1,64,256]{2,1,0:T(8,128)(2,1)}), bf16[64,64,256]{2,1,0:T(8,128)(2,1)}) %all-gather.14.cloned.1.call-update) | async-done | bytes 2097168 | tf_op jit(solution)/shard_map/all_gather | solution.py:97
  425.2 3.5 fusion.28
  428.7 12.6 %all-gather.7 = bf16[64,1024]{0,1:T(8,128)(2,1)S(1)} all-gather(bf16[64,256]{0,1:T(8,128)(2,1)S(1)} %bitcast.166), channel_id=9, replica_groups=mesh['leaf'=64,'panel'=4] {'panel'}, dimensions={1}, use_global_device_ids=true | all-gather | bytes 163840 | tf_op jit(solution)/shard_map/all_gather | solution.py:103
  442.0 1.0 convolution_bitcast_fusion.4
  443.1 18.8 %reduce-scatter.8.cloned.1.call-done = f32[1,64,256]{2,1,0:T(8,128)} async-done(((f32[1,64,1024]{2,1,0:T(8,128)}), f32[1,64,256]{2,1,0:T(8,128)}) %reduce-scatter.8.cloned.1.call-update) | async-done | bytes 65552 | tf_op jit(solution)/shard_map/reduce_scatter | solution.py:110
  462.0 1.8 convolution_bitcast_fusion.1
  463.8 23.5 %reduce-scatter.10.cloned.1.call-done = f32[1,64,256]{2,1,0:T(8,128)} async-done(((f32[1,64,1024]{2,1,0:T(8,128)}), f32[1,64,256]{2,1,0:T(8,128)}) %reduce-scatter.10.cloned.1.call-update) | async-done | bytes 65552 | tf_op jit(solution)/shard_map/reduce_scatter | solution.py:115
  487.3 1.5 convert_element_type.118
  489.5 80.4 %all-gather.16.cloned.1.call-done = bf16[64,64,256]{2,1,0:T(8,128)(2,1)} async-done(((bf16[1,64,256]{2,1,0:T(8,128)(2,1)}), bf16[64,64,256]{2,1,0:T(8,128)(2,1)}) %all-gather.16.cloned.1.call-update) | async-done | bytes 2097168 | tf_op jit(solution)/shard_map/all_gather | solution.py:97
  569.9 3.5 fusion.26
  573.5 12.6 %all-gather.8 = bf16[64,1024]{0,1:T(8,128)(2,1)S(1)} all-gather(bf16[64,256]{0,1:T(8,128)(2,1)S(1)} %bitcast.167), channel_id=10, replica_groups=mesh['leaf'=64,'panel'=4] {'panel'}, dimensions={1}, use_global_device_ids=true | all-gather | bytes 163840 | tf_op jit(solution)/shard_map/all_gather | solution.py:103
  586.8 1.0 convolution_bitcast_fusion.3
  587.9 18.8 %reduce-scatter.12.cloned.1.call-done = f32[1,64,256]{2,1,0:T(8,128)} async-done(((f32[1,64,1024]{2,1,0:T(8,128)}), f32[1,64,256]{2,1,0:T(8,128)}) %reduce-scatter.12.cloned.1.call-update) | async-done | bytes 65552 | tf_op jit(solution)/shard_map/reduce_scatter | solution.py:110
  606.8 1.8 convolution_bitcast_fusion
  609.2 23.0 %reduce-scatter.14.cloned.1.call-done = f32[1,64,256]{2,1,0:T(8,128)} async-done(((f32[1,64,1024]{2,1,0:T(8,128)}), f32[1,64,256]{2,1,0:T(8,128)}) %reduce-scatter.14.cloned.1.call-update) | async-done | bytes 65552 | tf_op jit(solution)/shard_map/reduce_scatter | solution.py:115
  (79 shorter events, 15.3 us)
Async XLA Ops:
  7.2 147.5 %all-gather.18.cloned.1.call-start = ((), (), s32[]{:S(2)}) async-start(), calls=%async_computation.12 | async-start | bytes 4210688 | tf_op jit(solution)/shard_map/all_gather | solution.py:82
  37.0 264.5 %all-gather.20.cloned.1.call-start = ((), (), s32[]{:S(2)}) async-start(), calls=%async_computation.13 | async-start | bytes 4210688 | tf_op jit(solution)/shard_map/all_gather | solution.py:82
  154.7 9.4 %copy-start.4 = (bf16[3,1,64,256]{3,2,1,0:T(8,128)(2,1)S(1)}, bf16[3,1,64,256]{3,2,1,0:T(8,128)(2,1)}, u32[]{:S(2)}) copy-start(bf16[3,1,64,256]{3,2,1,0:T(8,128)(2,1)} %param.12) | copy-start | bytes 294916
  154.7 21.6 %copy-start = (bf16[3,1,256,1024]{3,2,1,0:T(8,128)(2,1)S(1)}, bf16[3,1,256,1024]{3,2,1,0:T(8,128)(2,1)}, u32[]{:S(2)}) copy-start(bf16[3,1,256,1024]{3,2,1,0:T(8,128)(2,1)} %param.13) | copy-start | bytes 4718596
  154.7 33.8 %copy-start.1 = (bf16[2,1,1024,128]{3,2,1,0:T(8,128)(2,1)S(1)}, bf16[2,1,1024,128]{3,2,1,0:T(8,128)(2,1)}, u32[]{:S(2)}) copy-start(bf16[2,1,1024,128]{3,2,1,0:T(8,128)(2,1)} %param.14) | copy-start | bytes 1572868
  189.3 153.4 %reduce-scatter.6.cloned.1.call-start = ((), (), s32[]{:S(2)}) async-start(), calls=%async_computation.5 | async-start | bytes 327680 | tf_op jit(solution)/shard_map/reduce_scatter | solution.py:115
  324.2 101.0 %all-gather.14.cloned.1.call-start = ((), (), s32[]{:S(2)}) async-start(), calls=%async_computation.6 | async-start | bytes 2129920 | tf_op jit(solution)/shard_map/all_gather | solution.py:97
  344.2 117.8 %reduce-scatter.8.cloned.1.call-start = ((), (), s32[]{:S(2)}) async-start(), calls=%async_computation.7 | async-start | bytes 327680 | tf_op jit(solution)/shard_map/reduce_scatter | solution.py:110
  443.1 44.2 %reduce-scatter.10.cloned.1.call-start = ((), (), s32[]{:S(2)}) async-start(), calls=%async_computation.8 | async-start | bytes 327680 | tf_op jit(solution)/shard_map/reduce_scatter | solution.py:115
  463.8 106.1 %all-gather.16.cloned.1.call-start = ((), (), s32[]{:S(2)}) async-start(), calls=%async_computation.9 | async-start | bytes 2129920 | tf_op jit(solution)/shard_map/all_gather | solution.py:97
  488.8 118.0 %reduce-scatter.12.cloned.1.call-start = ((), (), s32[]{:S(2)}) async-start(), calls=%async_computation.10 | async-start | bytes 327680 | tf_op jit(solution)/shard_map/reduce_scatter | solution.py:110
  569.9 39.3 %copy-start.2 = (f32[1,64,256]{2,1,0:T(8,128)S(1)}, f32[1,64,256]{2,1,0:T(8,128)}, u32[]{:S(2)}) copy-start(f32[1,64,256]{2,1,0:T(8,128)} %reduce-scatter.6.cloned.1.call-done) | copy-start | bytes 196612
  569.9 39.3 %copy-start.3 = (f32[1,64,256]{2,1,0:T(8,128)S(1)}, f32[1,64,256]{2,1,0:T(8,128)}, u32[]{:S(2)}) copy-start(f32[1,64,256]{2,1,0:T(8,128)} %reduce-scatter.10.cloned.1.call-done) | copy-start | bytes 196612
  587.9 44.3 %reduce-scatter.14.cloned.1.call-start = ((), (), s32[]{:S(2)}) async-start(), calls=%async_computation.11 | async-start | bytes 327680 | tf_op jit(solution)/shard_map/reduce_scatter | solution.py:115
Sparse Core Ops, SparseCore 0:
  37.2 117.4 all-gather.17
  189.4 112.0 all-gather.19
  324.3 18.4 reduce-scatter.5
  346.3 78.7 all-gather.13
  443.2 18.7 reduce-scatter.7
  464.4 22.9 reduce-scatter.9
  491.0 78.7 all-gather.15
  588.0 18.7 reduce-scatter.11
  609.3 22.8 reduce-scatter.13
where the time goes:
time: 643 us; the launch traced here: 640 us
  waiting for transfers between devices  489 us (76%)
  blocking collectives  85.4 us (13%)
  matrix products  36.3 us (6%)
  between operations  14 us (2%)
  other arithmetic  8.3 us (1%)
  local copies, waits for them, and re-layouts  7.11 us (1%)
    all_gather x2, waiting for transfers between devices, local(): lax.all_gather(update, ('leaf', 'panel'), axis=0, tiled=True)  225 us
    all_gather x2, waiting for transfers between devices, local(): piece = lax.all_gather(upper, 'leaf', axis=0, tiled=True)  161 us
    reduce_scatter x3, waiting for transfers between devices, local(): lax.psum_scatter(solve_partial, 'panel', scatter_dimension=2, tiled=True)  65 us
    reduce_scatter x2, waiting for transfers between devices, local(): lax.psum_scatter(back_partial, 'panel', scatter_dimension=2, tiled=True)  37.7 us
    all_gather x3, blocking collectives, local(): resid_whole = lax.all_gather(resid_local, 'panel', axis=2, tiled=True)  36.3 us
    all_gather x2, blocking collectives, local(): chosen_whole = lax.all_gather(chosen, 'panel', axis=2, tiled=True)  25.2 us
    all_gather x2, blocking collectives, local(): lax.all_gather(forward, 'panel', axis=2, tiled=True)  24 us
    dot_general x4, matrix products, add_block(): jnp.einsum('crj,cjt->rt', values, onehot, preferred_element_type=jnp.floa...  18.5 us
  transfers between devices with their start and end apart: 9, of which 9 were waited for; matrix products, arithmetic and copies ran while one was open for 1% of the time, Pallas kernels for 0%

commit v1 on v0

v1 whole, which is shorter than its diff:
```python
import functools

import jax
import jax.numpy as jnp
from jax import lax
from jax.experimental import pallas as pl
from jax.experimental.pallas import tpu as pltpu
from jax.sharding import Mesh, PartitionSpec as P

BF = jnp.bfloat16
F32 = jnp.float32
VMEM = pl.BlockSpec(memory_space=pltpu.VMEM)
SMEM = pl.BlockSpec(memory_space=pltpu.SMEM)
PARAMS = pltpu.CompilerParams(vmem_limit_bytes=32 * 1024 * 1024)
NT = (((1,), (1,)), ((), ()))
NN = (((1,), (0,)), ((), ()))


def mul_t(a, b):
    return lax.dot_general(a, b, NT, preferred_element_type=F32)


def mul(a, b):
    return lax.dot_general(a, b, NN, preferred_element_type=F32)


def call(body, outs, *args, specs=None, scratch=()):
    specs = [VMEM] * len(args) if specs is None else specs
    return pl.pallas_call(
        body,
        out_shape=outs,
        in_specs=specs,
        out_specs=jax.tree.map(lambda _: VMEM, outs),
        scratch_shapes=list(scratch),
        compiler_params=PARAMS,
    )(*args)


def sds(*shape, dtype=BF):
    return jax.ShapeDtypeStruct(shape, dtype)


def first_body(panels, info, r0, r1, r2, r3, inv, send, mine):
    p = info[2]
    quarter = r0.shape[-1]
    total = None
    for k, ref in enumerate((r0, r1, r2, r3)):
        q = lax.rem(p + panels - k, panels)
        block = ref[0, 0] if k == 0 else ref[...]
        part = mul_t(block, inv[:, pl.ds(pl.multiple_of(q * quarter, quarter), quarter)])
        total = part if total is None else total + part
    f = total.astype(BF)
    mine[...] = f
    rows = f.shape[0] // panels
    for d in range(panels):
        send[d, 0] = f[d * rows : (d + 1) * rows]
        send[d, 1] = r0[1, 0, d * rows : (d + 1) * rows]
        send[d, 2] = r0[2, 0, d * rows : (d + 1) * rows]


def place(lists, count, rows):
    cols = lists.shape[-1]
    row = lax.broadcasted_iota(jnp.int32, (rows, cols), 0)
    col = lax.broadcasted_iota(jnp.int32, (rows, cols), 1)
    return jnp.where((row == lists) & (col < count), 1.0, 0.0).astype(BF)


def updated(panels, p, f, lists, count, blocks, scratch):
    width = blocks[0].shape[-1]
    for k, ref in enumerate(blocks):
        q = lax.rem(p + panels - k, panels)
        scratch[:, pl.ds(pl.multiple_of(q * width, width), width)] = mul(f, ref[...]).astype(BF)
    u = scratch[...]
    col = lax.broadcasted_iota(jnp.int32, u.shape, 1)
    u = jnp.where(col < count, u.astype(F32), 0.0).astype(BF)
    return mul_t(u, place(lists, count, 4 * u.shape[1] // 2)).astype(BF)


def whole(ref, index):
    return jnp.concatenate([ref[q, index] for q in range(ref.shape[0])], axis=1)


def up0_body(panels, info, got, lists, c0, c1, c2, c3, out, scratch):
    f = whole(got, 0)
    e = updated(panels, info[2], f, lists[...], info[3], (c0, c1, c2, c3), scratch)
    for d in range(out.shape[0]):
        out[d] = e


def summed(recv):
    total = recv[0].astype(F32)
    for j in range(1, recv.shape[0]):
        total = total + recv[j].astype(F32)
    return total


def forward(resid, inv):
    return jnp.concatenate([mul_t(resid, inv[q]) for q in range(inv.shape[0])], axis=1).astype(BF)


def backward(reduced, inv):
    rows = inv.shape[1]
    total = None
    for q in range(inv.shape[0]):
        part = mul(reduced[:, q * rows : (q + 1) * rows], inv[q])
        total = part if total is None else total + part
    return total.astype(BF)


def up1_body(panels, info, recv, got, inv, lists, c0, c1, c2, c3, fout, out, scratch):
    resid = (whole(got, 1).astype(F32) - summed(recv)).astype(BF)
    f = forward(resid, inv)
    fout[...] = f
    e = updated(panels, info[2], f, lists[...], info[4], (c0, c1, c2, c3), scratch)
    for d in range(out.shape[0]):
        out[d] = e


def top_body(recv, got, inv, fout, out):
    resid = (whole(got, 2).astype(F32) - summed(recv)).astype(BF)
    f = forward(resid, inv)
    fout[...] = f
    s = backward(f, inv)
    for d in range(out.shape[0]):
        out[d] = s


def fold_body(slots, blocks, out, acc):
    acc[...] = jnp.zeros_like(acc)
    for j in range(blocks.shape[0]):
        d = slots[j]
        acc[d] = acc[d] + blocks[j].astype(F32)
    for d in range(out.shape[0]):
        out[d] = acc[d].astype(BF)


def route_body(slots, blocks, out):
    for d in range(out.shape[0]):
        out[d] = blocks[slots[d]]


def solved(panels, p, f, above, lists, count, blocks, inv, scratch):
    scratch[...] = mul(above, place(lists, count, above.shape[1])).astype(BF)
    width = blocks[0].shape[-1]
    back = None
    for k, ref in enumerate(blocks):
        q = lax.rem(p + panels - k, panels)
        term = mul_t(scratch[:, pl.ds(pl.multiple_of(q * width, width), width)], ref[...])
        back = term if back is None else back + term
    reduced = (f.astype(F32) - back).astype(BF)
    return backward(reduced, inv)


def down1_body(panels, info, recv, f, inv, lists, c0, c1, c2, c3, out, scratch):
    s = solved(panels, info[2], f[...], recv[info[6]], lists[...], info[4], (c0, c1, c2, c3), inv, scratch)
    for d in range(out.shape[0]):
        out[d] = s


def down0_body(panels, info, recv, got, inv, lists, c0, c1, c2, c3, f1, f2, s2, s1, send, scratch):
    s = solved(panels, info[2], whole(got, 0), recv[info[5]], lists[...], info[3], (c0, c1, c2, c3), inv, scratch)
    quarter = send.shape[-1]
    for index, value in enumerate((f1[...], f2[...], s2[0], s1[0], s)):
        for d in range(panels):
            send[d, index] = value[:, d * quarter : (d + 1) * quarter]


def last_body(panels, got, mine, fwd, sol):
    rows = got.shape[2]
    fwd[0, 0] = mine[...]
    for q in range(panels):
        span = slice(q * rows, (q + 1) * rows)
        fwd[1, 0, span] = got[q, 0]
        fwd[2, 0, span] = got[q, 1]
        sol[2, 0, span] = got[q, 2]
        sol[1, 0, span] = got[q, 3]
        sol[0, 0, span] = got[q, 4]


def local(sizes, rhs, inv_diag, coupling, row_lists, parents, counts):
    nz, group, panels = sizes
    leaf = lax.axis_index("z") * group + lax.axis_index("x") * 2 + lax.axis_index("core")
    z = leaf // group
    lane = leaf % group
    panel = lax.axis_index("panel")
    width = inv_diag.shape[3]
    mid = (group, rhs.shape[2] // panels, width)
    rows = rhs.shape[2] // panels

    def spread(x):
        return [x] + [
            lax.ppermute(x, "panel", [(i, (i + k) % panels) for i in range(panels)])
            for k in range(1, panels)
        ]

    mine0, mine1 = parents[0, leaf], parents[1, leaf]
    info = jnp.stack(
        [z, lane, panel, counts[0, leaf], counts[1, leaf], mine0 % group, mine1 % group]
    ).astype(jnp.int32)
    lists0 = lax.dynamic_slice_in_dim(row_lists[0], leaf, 1, 0)
    lists1 = lax.dynamic_slice_in_dim(row_lists[1], leaf, 1, 0)
    table = parents.reshape(2, nz, group)
    column = lax.dynamic_index_in_dim(table, lane, 2, keepdims=False)
    fold_slots = jnp.where(column // group == z, column % group, group).astype(jnp.int32)
    plane = lax.dynamic_index_in_dim(table, z, 1, keepdims=False)
    route_slots = (plane // group).astype(jnp.int32)

    rest = spread(rhs[0, 0])[1:]
    c0 = spread(coupling[0, 0])
    c1 = spread(coupling[1, 0])
    inv1 = lax.all_gather(inv_diag[1, 0], "panel", axis=0)
    inv2 = lax.all_gather(inv_diag[2, 0], "panel", axis=0)
    inv0 = lax.all_gather(inv_diag[0, 0], "panel", axis=0)

    send, mine = call(
        functools.partial(first_body, panels),
        (sds(panels, 3, rows, rhs.shape[3]), sds(rhs.shape[2], rhs.shape[3])),
        info, rhs, *rest, inv_diag[0, 0],
        specs=[SMEM] + [VMEM] * 5,
    )
    got = lax.all_to_all(send, "panel", 0, 0)
    touched = pltpu.VMEM((rows, panels * coupling.shape[3]), BF)
    e = call(
        functools.partial(up0_body, panels), sds(*mid), info, got, lists0, *c0,
        specs=[SMEM] + [VMEM] * 6, scratch=[touched],
    )

    def go_up(e, level):
        e = lax.all_to_all(e, "z", 0, 0)
        e = call(
            fold_body, sds(*mid), fold_slots[level], e,
            specs=[SMEM, VMEM], scratch=[pltpu.VMEM((group + 1, *mid[1:]), F32)],
        )
        return lax.all_to_all(e, ("x", "core"), 0, 0)

    def go_down(s, level):
        s = lax.all_to_all(s, "z", 0, 0)
        s = call(route_body, sds(*mid), route_slots[level], s, specs=[SMEM, VMEM])
        return lax.all_to_all(s, ("x", "core"), 0, 0)

    f1, e = call(
        functools.partial(up1_body, panels), (sds(*mid[1:]), sds(*mid)),
        info, go_up(e, 0), got, inv1, lists1, *c1,
        specs=[SMEM] + [VMEM] * 8, scratch=[touched],
    )
    f2, s2 = call(top_body, (sds(*mid[1:]), sds(*mid)), go_up(e, 1), got, inv2)
    s1 = call(
        functools.partial(down1_body, panels), sds(*mid),
        info, go_down(s2, 1), f1, inv1, lists1, *c1,
        specs=[SMEM] + [VMEM] * 8, scratch=[touched],
    )
    send = call(
        functools.partial(down0_body, panels), sds(panels, 5, rows, rhs.shape[3]),
        info, go_down(s1, 0), got, inv0, lists0, *c0, f1, f2, s2, s1,
        specs=[SMEM] + [VMEM] * 12, scratch=[touched],
    )
    got = lax.all_to_all(send, "panel", 0, 0)
    return call(
        functools.partial(last_body, panels), (sds(*rhs.shape), sds(*rhs.shape)), got, mine
    )


def solution(mesh):
    leaves, panels = mesh.shape["leaf"], mesh.shape["panel"]
    group = 8
    nz = leaves // group
    inner = Mesh(mesh.devices.reshape(nz, group // 2, 2, panels), ("z", "x", "core", "panel"))
    leaf = ("z", "x", "core")
    placed = (
        P(None, leaf, None, "panel"),
        P(None, leaf, "panel", None),
        P(None, leaf, None, "panel"),
        P(),
        P(),
        P(),
    )
    return jax.shard_map(
        functools.partial(local, (nz, group, panels)),
        mesh=inner,
        in_specs=placed,
        out_specs=(P(None, leaf, None, "panel"), P(None, leaf, None, "panel")),
        check_vma=False,
    )
```

time: 643 us -> 206 us (0.32)
  waiting for transfers between devices: 489 us -> 58.9 us
  starting transfers between devices: 0.37 us -> 42 us
  matrix products: 36.3 us -> 0 us
  blocking collectives: 85.4 us -> 51.2 us
  Pallas kernels: 0 us -> 15.4 us
  local copies, waits for them, and re-layouts: 7.11 us -> 17.6 us
  other arithmetic: 8.3 us -> 0.62 us
    all_gather x4 -> x3, waiting for transfers between devices: 386 us -> 0.04 us  [the longest x1 0.02 us: local(): inv0 = lax.all_gather(inv_diag[0, 0], 'panel', axis=0)]
    reduce_scatter x5 -> x0, waiting for transfers between devices: 103 us -> none  [the longest x3 65 us: local(): lax.psum_scatter(solve_partial, 'panel', scatter_dimension=2, tiled=True)]
    all_gather x7 -> x0, blocking collectives: 85.4 us -> none  [the longest x3 36.3 us: local(): resid_whole = lax.all_gather(resid_local, 'panel', axis=2, tiled=True)]
    all_to_all x0 -> x6, waiting for transfers between devices: none -> 58.1 us  [the longest x1 15.7 us: local(): got = lax.all_to_all(send, 'panel', 0, 0)]
    all_to_all x0 -> x4, blocking collectives: none -> 51.2 us  [the longest x1 14.2 us: go_up(): e = lax.all_to_all(e, 'z', 0, 0)]
    dot_general x16 -> x0, matrix products: 36.3 us -> none  [the longest x4 18.5 us: add_block(): jnp.einsum('crj,cjt->rt', values, onehot, preferred_element_type=jnp.floa...]
    all_to_all x0 -> x6, starting transfers between devices: none -> 29.1 us  [the longest x1 9.95 us: go_up(): e = lax.all_to_all(e, 'z', 0, 0)]
    pallas_call x0 -> x11, Pallas kernels: none -> 15.4 us  [call(): pl.pallas_call(body, out_shape=outs, in_specs=specs, out_specs=jax.tree.m...]
  transfers between devices with their start and end apart: 9 -> 18, of which waited for: 9 -> 6; matrix products, arithmetic and copies ran while one was open for 1% -> 2% of each run, Pallas kernels for 0% -> 6%
where the time goes in v1:
time: 206 us; the launch traced here: 204 us
  waiting for transfers between devices  58.9 us (29%)
  blocking collectives  51.2 us (25%)
  starting transfers between devices  42 us (20%)
  between operations  17.9 us (9%)
  local copies, waits for them, and re-layouts  17.6 us (9%)
  Pallas kernels  15.4 us (7%)
    all_to_all x1, waiting for transfers between devices, local(): got = lax.all_to_all(send, 'panel', 0, 0)  15.7 us
    pallas_call x11, Pallas kernels, call(): pl.pallas_call(body, out_shape=outs, in_specs=specs, out_specs=jax.tree.m...  15.4 us
    all_to_all x2, waiting for transfers between devices, go_up(): return lax.all_to_all(e, ('x', 'core'), 0, 0)  14.9 us
    all_to_all x1, blocking collectives, go_up(): e = lax.all_to_all(e, 'z', 0, 0)  14.2 us
    all_to_all x1, blocking collectives, go_down(): s = lax.all_to_all(s, 'z', 0, 0)  14.2 us
    all_to_all x1, blocking collectives, local(): got = lax.all_to_all(send, 'panel', 0, 0)  12.8 us
    ppermute x9, starting transfers between devices, spread(): lax.ppermute(x, 'panel', [(i, (i + k) % panels) for i in range(panels)])  12.8 us
    unnamed x44, local copies, waits for them, and re-layouts  11.2 us
  transfers between devices with their start and end apart: 18, of which 6 were waited for; matrix products, arithmetic and copies ran while one was open for 2% of the time, Pallas kernels for 6%

profile of v1, /device:TPU:24, one launch (start us, length us, event | category | flops | bytes accessed | tf_op | source)
XLA Modules:
  0.0 203.6 jit_solution(7773144903371335447)
XLA Ops:
  7.2 2.7 %fusion = (bf16[1,1,256,1024]{3,2,1,0:T(8,128)(2,1)}, bf16[256,1024]{1,0:T(8,128)(2,1)S(1)}, bf16[1,1,256,1024]{3,2,1,0:T(8,128)(2,1)}, bf16[1,1,256,1024]{3,2,1,0:T(8,128)(2,1)}) fusion(bf16[3,1,256,1024]{3,2,1,0:T(8,128)(2,1)} %param.7), kind=kLoop, calls=%fused_computation.26 | loop fusion | bytes 3670016 | tf_op jit(solution)/shard_map/slice | solution.py:218
  10.8 2.0 collective-permute-start
  13.8 3.2 %collective-permute-start.3 = (bf16[1024,128]{1,0:T(8,128)(2,1)S(1)}, bf16[1024,128]{1,0:T(8,128)(2,1)S(1)}, u32[]{:S(2)}, u32[]{:S(2)}) collective-permute-start(bf16[1024,128]{1,0:T(8,128)(2,1)S(1)} %get-tuple-element.19.c0), channel_id=1, source_target_pairs={{0,1},{1,2},{2,3},{3,0},{4,5},{5,6},{6,7},{7,4},{8,9},{9,10},{10,1... | collective-permute-start | bytes 786440 | tf_op jit(solution)/shard_map/ppermute | solution.py:192
  17.0 1.5 collective-permute-start.4
  24.7 3.2 %collective-permute-start.6 = (bf16[1024,128]{1,0:T(8,128)(2,1)S(1)}, bf16[1024,128]{1,0:T(8,128)(2,1)S(1)}, u32[]{:S(2)}, u32[]{:S(2)}) collective-permute-start(bf16[1024,128]{1,0:T(8,128)(2,1)S(1)} %get-tuple-element.18.c0), channel_id=1, source_target_pairs={{0,1},{1,2},{2,3},{3,0},{4,5},{5,6},{6,7},{7,4},{8,9},{9,10},{10,1... | collective-permute-start | bytes 786440 | tf_op jit(solution)/shard_map/ppermute | solution.py:192
  28.8 1.5 shard_map.77
  30.9 4.5 %all-to-all-start = ((bf16[4,3,16,256]{3,2,1,0:T(8,128)(2,1)}), bf16[4,3,16,256]{3,2,1,0:T(8,128)(2,1)S(1)}, u32[]{:S(2)}, u32[]{:S(2)}) async-start(bf16[4,3,16,256]{3,2,1,0:T(8,128)(2,1)} %get-tuple-element.8), calls=%async_computation | async-start | bytes 196608 | tf_op jit(solution)/shard_map/all_to_all | solution.py:221
  36.4 15.7 %all-to-all-done.got = bf16[4,3,16,256]{3,2,1,0:T(8,128)(2,1)S(1)} async-done(((bf16[4,3,16,256]{3,2,1,0:T(8,128)(2,1)}), bf16[4,3,16,256]{3,2,1,0:T(8,128)(2,1)S(1)}, u32[]{:S(2)}, u32[]{:S(2)}) %all-to-all-start) | async-done | bytes 98336 | tf_op jit(solution)/shard_map/all_to_all | solution.py:221
  52.0 1.9 shard_map.78
  53.9 9.9 %all-to-all-start.1 = ((bf16[8,16,1024]{2,1,0:T(8,128)(2,1)}), bf16[8,16,1024]{2,1,0:T(8,128)(2,1)S(1)}, u32[]{:S(2)}, u32[]{:S(2)}) async-start(bf16[8,16,1024]{2,1,0:T(8,128)(2,1)} %shard_map.78), calls=%async_computation.1 | async-start | bytes 524288 | tf_op jit(solution)/shard_map/all_to_all | solution.py:229
  64.7 9.6 %all-to-all-done.1.blocks = bf16[8,16,1024]{2,1,0:T(8,128)(2,1)S(1)} async-done(((bf16[8,16,1024]{2,1,0:T(8,128)(2,1)}), bf16[8,16,1024]{2,1,0:T(8,128)(2,1)S(1)}, u32[]{:S(2)}, u32[]{:S(2)}) %all-to-all-start.1) | async-done | bytes 262176 | tf_op jit(solution)/shard_map/all_to_all | solution.py:229
  74.3 1.4 shard_map.79
  75.7 4.4 %all-to-all-start.2 = ((bf16[8,16,1024]{2,1,0:T(8,128)(2,1)}), bf16[8,16,1024]{2,1,0:T(8,128)(2,1)S(1)}, u32[]{:S(2)}, u32[]{:S(2)}) async-start(bf16[8,16,1024]{2,1,0:T(8,128)(2,1)} %shard_map.79), calls=%async_computation.2 | async-start | bytes 524288 | tf_op jit(solution)/shard_map/all_to_all | solution.py:234
  80.2 7.5 %all-to-all-done.2.recv = bf16[8,16,1024]{2,1,0:T(8,128)(2,1)S(1)} async-done(((bf16[8,16,1024]{2,1,0:T(8,128)(2,1)}), bf16[8,16,1024]{2,1,0:T(8,128)(2,1)S(1)}, u32[]{:S(2)}, u32[]{:S(2)}) %all-to-all-start.2) | async-done | bytes 262176 | tf_op jit(solution)/shard_map/all_to_all | solution.py:234
  87.6 1.6 copy-done
  89.2 1.8 shard_map.80
  91.0 14.2 %all_to_all.50.blocks = bf16[8,16,1024]{2,1,0:T(8,128)(2,1)S(1)} all-to-all(bf16[8,16,1024]{2,1,0:T(8,128)(2,1)S(1)} %get-tuple-element.9), channel_id=1, replica_groups=mesh['z'=8,'x'=4,'core'=2,'panel'=4] {'z'}, dimensions={0} | all-to-all | bytes 524288 | tf_op jit(solution)/shard_map/all_to_all | solution.py:229
  105.3 1.4 shard_map.81
  106.7 3.4 %all-to-all-start.4 = ((bf16[8,16,1024]{2,1,0:T(8,128)(2,1)}), bf16[8,16,1024]{2,1,0:T(8,128)(2,1)S(1)}, u32[]{:S(2)}, u32[]{:S(2)}) async-start(bf16[8,16,1024]{2,1,0:T(8,128)(2,1)} %shard_map.81), calls=%async_computation.4 | async-start | bytes 524288 | tf_op jit(solution)/shard_map/all_to_all | solution.py:234
  110.1 7.4 %all-to-all-done.4.recv = bf16[8,16,1024]{2,1,0:T(8,128)(2,1)S(1)} async-done(((bf16[8,16,1024]{2,1,0:T(8,128)(2,1)}), bf16[8,16,1024]{2,1,0:T(8,128)(2,1)S(1)}, u32[]{:S(2)}, u32[]{:S(2)}) %all-to-all-start.4) | async-done | bytes 262176 | tf_op jit(solution)/shard_map/all_to_all | solution.py:234
  117.6 1.6 copy-done.2
  119.2 1.6 shard_map.82
  121.4 3.4 %all-to-all-start.5 = ((bf16[8,16,1024]{2,1,0:T(8,128)(2,1)}), bf16[8,16,1024]{2,1,0:T(8,128)(2,1)S(1)}, u32[]{:S(2)}, u32[]{:S(2)}) async-start(bf16[8,16,1024]{2,1,0:T(8,128)(2,1)} %get-tuple-element.10.s2), calls=%async_computation.5 | async-start | bytes 524288 | tf_op jit(solution)/shard_map/all_to_all | solution.py:237
  126.1 10.5 %all-to-all-done.5.blocks = bf16[8,16,1024]{2,1,0:T(8,128)(2,1)S(1)} async-done(((bf16[8,16,1024]{2,1,0:T(8,128)(2,1)}), bf16[8,16,1024]{2,1,0:T(8,128)(2,1)S(1)}, u32[]{:S(2)}, u32[]{:S(2)}) %all-to-all-start.5) | async-done | bytes 262176 | tf_op jit(solution)/shard_map/all_to_all | solution.py:237
  137.8 9.9 %all_to_all.51.recv = bf16[8,16,1024]{2,1,0:T(8,128)(2,1)S(1)} all-to-all(bf16[8,16,1024]{2,1,0:T(8,128)(2,1)S(1)} %shard_map.83), channel_id=1, replica_groups=mesh['z'=8,'x'=4,'core'=2,'panel'=4] {'x','core'}, dimensions={0} | all-to-all | bytes 524288 | tf_op jit(solution)/shard_map/all_to_all | solution.py:239
  150.6 1.5 shard_map.84.s1
  152.1 14.2 %all_to_all.52.blocks = bf16[8,16,1024]{2,1,0:T(8,128)(2,1)S(1)} all-to-all(bf16[8,16,1024]{2,1,0:T(8,128)(2,1)S(1)} %shard_map.84.s1), channel_id=1, replica_groups=mesh['z'=8,'x'=4,'core'=2,'panel'=4] {'z'}, dimensions={0} | all-to-all | bytes 524288 | tf_op jit(solution)/shard_map/all_to_all | solution.py:237
  167.5 3.4 %all-to-all-start.8 = ((bf16[8,16,1024]{2,1,0:T(8,128)(2,1)}), bf16[8,16,1024]{2,1,0:T(8,128)(2,1)S(1)}, u32[]{:S(2)}, u32[]{:S(2)}) async-start(bf16[8,16,1024]{2,1,0:T(8,128)(2,1)} %shard_map.85), calls=%async_computation.8 | async-start | bytes 524288 | tf_op jit(solution)/shard_map/all_to_all | solution.py:239
  171.0 7.4 %all-to-all-done.8.recv = bf16[8,16,1024]{2,1,0:T(8,128)(2,1)S(1)} async-done(((bf16[8,16,1024]{2,1,0:T(8,128)(2,1)}), bf16[8,16,1024]{2,1,0:T(8,128)(2,1)S(1)}, u32[]{:S(2)}, u32[]{:S(2)}) %all-to-all-start.8) | async-done | bytes 262176 | tf_op jit(solution)/shard_map/all_to_all | solution.py:239
  178.4 1.6 copy-done.3
  181.7 1.9 shard_map.86
  183.6 12.8 %all_to_all.53.got = bf16[4,5,16,256]{3,2,1,0:T(8,128)(2,1)S(1)} all-to-all(bf16[4,5,16,256]{3,2,1,0:T(8,128)(2,1)S(1)} %shard_map.86), channel_id=1, replica_groups=mesh['z'=8,'x'=4,'core'=2,'panel'=4] {'panel'}, dimensions={0} | all-to-all | bytes 327680 | tf_op jit(solution)/shard_map/all_to_all | solution.py:257
  (80 shorter events, 17.0 us)
Async XLA Ops:
  7.2 3.6 %copy-start.12 = (bf16[3,1,64,256]{3,2,1,0:T(8,128)(2,1)S(1)}, bf16[3,1,64,256]{3,2,1,0:T(8,128)(2,1)}, u32[]{:S(2)}) copy-start(bf16[3,1,64,256]{3,2,1,0:T(8,128)(2,1)} %r0.1) | copy-start | bytes 294916
  7.2 6.6 %copy-start.18 = (bf16[2,1,1024,128]{3,2,1,0:T(8,128)(2,1)S(1)}, bf16[2,1,1024,128]{3,2,1,0:T(8,128)(2,1)}, u32[]{:S(2)}) copy-start(bf16[2,1,1024,128]{3,2,1,0:T(8,128)(2,1)} %param.8) | copy-start | bytes 1572868
  7.2 80.5 %all-gather.7.cloned.1.call-start = ((), (), s32[]{:S(2)}) async-start(), calls=%async_computation.10 | async-start | bytes 2621440 | tf_op jit(solution)/shard_map/all_gather | solution.py:211
  9.9 8.7 %copy-start.19 = (s32[2,64,512]{2,1,0:T(8,128)S(1)}, s32[2,64,512]{2,1,0:T(8,128)}, u32[]{:S(2)}) copy-start(s32[2,64,512]{2,1,0:T(8,128)} %param.9) | copy-start | bytes 786436
  9.9 8.8 %copy-start.20 = (s32[2,64]{1,0:T(2,128)S(1)}, s32[2,64]{1,0:T(2,128)}, u32[]{:S(2)}) copy-start(s32[2,64]{1,0:T(2,128)} %param.10) | copy-start | bytes 1540
  9.9 8.8 %copy-start.21 = (s32[2,64]{1,0:T(2,128)S(1)}, s32[2,64]{1,0:T(2,128)}, u32[]{:S(2)}) copy-start(s32[2,64]{1,0:T(2,128)} %param.11) | copy-start | bytes 1540
  10.0 100.2 %all-gather.9.cloned.1.call-start = ((), (), s32[]{:S(2)}) async-start(), calls=%async_computation.11 | async-start | bytes 2621440 | tf_op jit(solution)/shard_map/all_gather | solution.py:212
  10.7 160.2 %all-gather.11.cloned.1.call-start = ((), (), s32[]{:S(2)}) async-start(), calls=%async_computation.12 | async-start | bytes 2621440 | tf_op jit(solution)/shard_map/all_gather | solution.py:213
  10.8 7.7 %collective-permute-start = (bf16[64,256]{1,0:T(8,128)(2,1)S(1)}, bf16[64,256]{1,0:T(8,128)(2,1)S(1)}, u32[]{:S(2)}, u32[]{:S(2)}) collective-permute-start(bf16[64,256]{1,0:T(8,128)(2,1)S(1)} %slice_bitcast_fusion.2), channel_id=1, source_target_pairs={{0,1},{1,2},{2,3},{3,0},{4,5},{5,6},{6,7},{7,4},{8,9},{9,10},{10,1... | collective-permute-start | bytes 98312 | tf_op jit(solution)/shard_map/ppermute | solution.py:192
  12.8 11.9 %collective-permute-start.1 = (bf16[64,256]{1,0:T(8,128)(2,1)S(1)}, bf16[64,256]{1,0:T(8,128)(2,1)S(1)}, u32[]{:S(2)}, u32[]{:S(2)}) collective-permute-start(bf16[64,256]{1,0:T(8,128)(2,1)S(1)} %slice_bitcast_fusion.2), channel_id=1, source_target_pairs={{0,2},{1,3},{2,0},{3,1},{4,6},{5,7},{6,4},{7,5},{8,10},{9,11},{10,... | collective-permute-start | bytes 98312 | tf_op jit(solution)/shard_map/ppermute | solution.py:192
  13.7 14.3 %collective-permute-start.2 = (bf16[64,256]{1,0:T(8,128)(2,1)S(1)}, bf16[64,256]{1,0:T(8,128)(2,1)S(1)}, u32[]{:S(2)}, u32[]{:S(2)}) collective-permute-start(bf16[64,256]{1,0:T(8,128)(2,1)S(1)} %slice_bitcast_fusion.2), channel_id=1, source_target_pairs={{0,3},{1,0},{2,1},{3,2},{4,7},{5,4},{6,5},{7,6},{8,11},{9,8},{10,9... | collective-permute-start | bytes 98312 | tf_op jit(solution)/shard_map/ppermute | solution.py:192
  13.8 21.6 %collective-permute-start.3 = (bf16[1024,128]{1,0:T(8,128)(2,1)S(1)}, bf16[1024,128]{1,0:T(8,128)(2,1)S(1)}, u32[]{:S(2)}, u32[]{:S(2)}) collective-permute-start(bf16[1024,128]{1,0:T(8,128)(2,1)S(1)} %get-tuple-element.19.c0), channel_id=1, source_target_pairs={{0,1},{1,2},{2,3},{3,0},{4,5},{5,6},{6,7},{7,4},{8,9},{9,10},{10,1... | collective-permute-start | bytes 786440 | tf_op jit(solution)/shard_map/ppermute | solution.py:192
  17.0 35.0 %collective-permute-start.4 = (bf16[1024,128]{1,0:T(8,128)(2,1)S(1)}, bf16[1024,128]{1,0:T(8,128)(2,1)S(1)}, u32[]{:S(2)}, u32[]{:S(2)}) collective-permute-start(bf16[1024,128]{1,0:T(8,128)(2,1)S(1)} %get-tuple-element.19.c0), channel_id=1, source_target_pairs={{0,2},{1,3},{2,0},{3,1},{4,6},{5,7},{6,4},{7,5},{8,10},{9,11},{10,... | collective-permute-start | bytes 786440 | tf_op jit(solution)/shard_map/ppermute | solution.py:192
  18.5 33.5 %collective-permute-start.5 = (bf16[1024,128]{1,0:T(8,128)(2,1)S(1)}, bf16[1024,128]{1,0:T(8,128)(2,1)S(1)}, u32[]{:S(2)}, u32[]{:S(2)}) collective-permute-start(bf16[1024,128]{1,0:T(8,128)(2,1)S(1)} %get-tuple-element.19.c0), channel_id=1, source_target_pairs={{0,3},{1,0},{2,1},{3,2},{4,7},{5,4},{6,5},{7,6},{8,11},{9,8},{10,9... | collective-permute-start | bytes 786440 | tf_op jit(solution)/shard_map/ppermute | solution.py:192
  24.7 55.4 %collective-permute-start.6 = (bf16[1024,128]{1,0:T(8,128)(2,1)S(1)}, bf16[1024,128]{1,0:T(8,128)(2,1)S(1)}, u32[]{:S(2)}, u32[]{:S(2)}) collective-permute-start(bf16[1024,128]{1,0:T(8,128)(2,1)S(1)} %get-tuple-element.18.c0), channel_id=1, source_target_pairs={{0,1},{1,2},{2,3},{3,0},{4,5},{5,6},{6,7},{7,4},{8,9},{9,10},{10,1... | collective-permute-start | bytes 786440 | tf_op jit(solution)/shard_map/ppermute | solution.py:192
  28.0 52.2 %collective-permute-start.7 = (bf16[1024,128]{1,0:T(8,128)(2,1)S(1)}, bf16[1024,128]{1,0:T(8,128)(2,1)S(1)}, u32[]{:S(2)}, u32[]{:S(2)}) collective-permute-start(bf16[1024,128]{1,0:T(8,128)(2,1)S(1)} %get-tuple-element.18.c0), channel_id=1, source_target_pairs={{0,2},{1,3},{2,0},{3,1},{4,6},{5,7},{6,4},{7,5},{8,10},{9,11},{10,... | collective-permute-start | bytes 786440 | tf_op jit(solution)/shard_map/ppermute | solution.py:192
  30.9 21.1 %all-to-all-start = ((bf16[4,3,16,256]{3,2,1,0:T(8,128)(2,1)}), bf16[4,3,16,256]{3,2,1,0:T(8,128)(2,1)S(1)}, u32[]{:S(2)}, u32[]{:S(2)}) async-start(bf16[4,3,16,256]{3,2,1,0:T(8,128)(2,1)} %get-tuple-element.8), calls=%async_computation | async-start | bytes 196608 | tf_op jit(solution)/shard_map/all_to_all | solution.py:221
  35.4 44.7 %collective-permute-start.8 = (bf16[1024,128]{1,0:T(8,128)(2,1)S(1)}, bf16[1024,128]{1,0:T(8,128)(2,1)S(1)}, u32[]{:S(2)}, u32[]{:S(2)}) collective-permute-start(bf16[1024,128]{1,0:T(8,128)(2,1)S(1)} %get-tuple-element.18.c0), channel_id=1, source_target_pairs={{0,3},{1,0},{2,1},{3,2},{4,7},{5,4},{6,5},{7,6},{8,11},{9,8},{10,9... | collective-permute-start | bytes 786440 | tf_op jit(solution)/shard_map/ppermute | solution.py:192
  52.0 39.0 %copy-start.4 = (bf16[1024,128]{1,0:T(8,128)(2,1)}, bf16[1024,128]{1,0:T(8,128)(2,1)S(1)}, u32[]{:S(2)}) copy-start(bf16[1024,128]{1,0:T(8,128)(2,1)S(1)} %collective-permute-done.5.c3) | copy-start | bytes 786436
  53.9 20.4 %all-to-all-start.1 = ((bf16[8,16,1024]{2,1,0:T(8,128)(2,1)}), bf16[8,16,1024]{2,1,0:T(8,128)(2,1)S(1)}, u32[]{:S(2)}, u32[]{:S(2)}) async-start(bf16[8,16,1024]{2,1,0:T(8,128)(2,1)} %shard_map.78), calls=%async_computation.1 | async-start | bytes 524288 | tf_op jit(solution)/shard_map/all_to_all | solution.py:229
  75.7 11.9 %all-to-all-start.2 = ((bf16[8,16,1024]{2,1,0:T(8,128)(2,1)}), bf16[8,16,1024]{2,1,0:T(8,128)(2,1)S(1)}, u32[]{:S(2)}, u32[]{:S(2)}) async-start(bf16[8,16,1024]{2,1,0:T(8,128)(2,1)} %shard_map.79), calls=%async_computation.2 | async-start | bytes 524288 | tf_op jit(solution)/shard_map/all_to_all | solution.py:234
  80.1 26.5 %copy-start.6 = (bf16[1024,128]{1,0:T(8,128)(2,1)}, bf16[1024,128]{1,0:T(8,128)(2,1)S(1)}, u32[]{:S(2)}) copy-start(bf16[1024,128]{1,0:T(8,128)(2,1)S(1)} %collective-permute-done.6.c1) | copy-start | bytes 786436
  80.1 26.5 %copy-start.8 = (bf16[1024,128]{1,0:T(8,128)(2,1)}, bf16[1024,128]{1,0:T(8,128)(2,1)S(1)}, u32[]{:S(2)}) copy-start(bf16[1024,128]{1,0:T(8,128)(2,1)S(1)} %collective-permute-done.7.c2) | copy-start | bytes 786436
  80.2 26.5 %copy-start.10 = (bf16[1024,128]{1,0:T(8,128)(2,1)}, bf16[1024,128]{1,0:T(8,128)(2,1)S(1)}, u32[]{:S(2)}) copy-start(bf16[1024,128]{1,0:T(8,128)(2,1)S(1)} %collective-permute-done.8.c3) | copy-start | bytes 786436
  87.6 1.6 copy-start
  106.7 10.9 %all-to-all-start.4 = ((bf16[8,16,1024]{2,1,0:T(8,128)(2,1)}), bf16[8,16,1024]{2,1,0:T(8,128)(2,1)S(1)}, u32[]{:S(2)}, u32[]{:S(2)}) async-start(bf16[8,16,1024]{2,1,0:T(8,128)(2,1)} %shard_map.81), calls=%async_computation.4 | async-start | bytes 524288 | tf_op jit(solution)/shard_map/all_to_all | solution.py:234
  110.1 37.6 %copy-start.1 = (bf16[4,1,256,1024]{3,2,1,0:T(8,128)(2,1)S(1)}, bf16[4,1,256,1024]{3,2,1,0:T(8,128)(2,1)}, u32[]{:S(2)}) copy-start(bf16[4,1,256,1024]{3,2,1,0:T(8,128)(2,1)} %all-gather.7.cloned.1.call-done) | copy-start | bytes 6291460
  117.6 1.6 copy-start.2
  121.4 15.2 %all-to-all-start.5 = ((bf16[8,16,1024]{2,1,0:T(8,128)(2,1)}), bf16[8,16,1024]{2,1,0:T(8,128)(2,1)S(1)}, u32[]{:S(2)}, u32[]{:S(2)}) async-start(bf16[8,16,1024]{2,1,0:T(8,128)(2,1)} %get-tuple-element.10.s2), calls=%async_computation.5 | async-start | bytes 524288 | tf_op jit(solution)/shard_map/all_to_all | solution.py:237
  167.5 10.9 %all-to-all-start.8 = ((bf16[8,16,1024]{2,1,0:T(8,128)(2,1)}), bf16[8,16,1024]{2,1,0:T(8,128)(2,1)S(1)}, u32[]{:S(2)}, u32[]{:S(2)}) async-start(bf16[8,16,1024]{2,1,0:T(8,128)(2,1)} %shard_map.85), calls=%async_computation.8 | async-start | bytes 524288 | tf_op jit(solution)/shard_map/all_to_all | solution.py:239
  178.4 1.6 copy-start.3
  181.7 14.7 %copy-start.16 = (bf16[64,256]{1,0:T(8,128)(2,1)S(1)}, bf16[64,256]{1,0:T(8,128)(2,1)}, u32[]{:S(2)}) copy-start(bf16[64,256]{1,0:T(8,128)(2,1)} %copy-done.15) | copy-start | bytes 98308
  (8 other events, 6.4 us)
Sparse Core Ops, SparseCore 0:
  10.1 50.4 all-gather.6
  62.4 34.0 all-gather.8
  98.3 33.4 all-gather.10

commit v2 on v1

v2 whole, which is shorter than its diff:
```python
import functools

import jax
import jax.numpy as jnp
from jax import lax
from jax.experimental import pallas as pl
from jax.experimental.pallas import tpu as pltpu
from jax.sharding import Mesh, PartitionSpec as P

BF = jnp.bfloat16
F32 = jnp.float32
GROUP = 8
VMEM = pl.BlockSpec(memory_space=pltpu.VMEM)
SMEM = pl.BlockSpec(memory_space=pltpu.SMEM)
HBM = pl.BlockSpec(memory_space=pltpu.HBM)
PARAMS = pltpu.CompilerParams(vmem_limit_bytes=8 * 1024 * 1024)
NT = (((1,), (1,)), ((), ()))
NN = (((1,), (0,)), ((), ()))


def mul_t(a, b):
    return lax.dot_general(a, b, NT, preferred_element_type=F32)


def mul(a, b):
    return lax.dot_general(a, b, NN, preferred_element_type=F32)


def call(body, outs, *args, specs=None, outs_at=None, scratch=(), alias=None):
    specs = [VMEM] * len(args) if specs is None else specs
    outs = tuple(outs) if isinstance(outs, (list, tuple)) else outs
    outs_at = jax.tree.map(lambda _: VMEM, outs) if outs_at is None else tuple(outs_at)
    return pl.pallas_call(
        body,
        out_shape=outs,
        in_specs=specs,
        out_specs=outs_at,
        scratch_shapes=list(scratch),
        input_output_aliases=alias or {},
        compiler_params=PARAMS,
    )(*args)


def sds(*shape, dtype=BF):
    return jax.ShapeDtypeStruct(shape, dtype)


def leaf_place():
    z = lax.axis_index("z")
    lane = lax.axis_index("x") * lax.axis_size("core") + lax.axis_index("core")
    return z, lane, z * GROUP + lane


def order(k, panels):
    return lax.rem(lax.axis_index("panel") + panels - k, panels)


def pack_body(rhs, coupling, *outs):
    panels = len(outs) + 1
    quarter = rhs.shape[-1]
    for k, out in enumerate(outs, 1):
        target = lax.rem(lax.axis_index("panel") + k, panels)
        put_halves(out, rhs[0, 0])
        start = pl.multiple_of(target * quarter, quarter)
        out[2 * rhs.shape[2] :] = coupling[0, 0, pl.ds(start, quarter), :]


def put_halves(out, value):
    rows = value.shape[0]
    out[:rows] = value[:, :128]
    out[rows : 2 * rows] = value[:, 128:]


def first_body(rhs, coupling, m1, m2, m3, inv, send, mine, *cols):
    panels = send.shape[0]
    rows, quarter = rhs.shape[2:]
    total = None
    for k, ref in enumerate((rhs, m1, m2, m3)):
        q = order(k, panels)
        block = rhs[0, 0] if k == 0 else jnp.concatenate([ref[:rows], ref[rows : 2 * rows]], axis=1)
        part = mul_t(block, inv[:, pl.ds(pl.multiple_of(q * quarter, quarter), quarter)])
        total = part if total is None else total + part
    f = total.astype(BF)
    mine[...] = f
    few = rows // panels
    own = pl.multiple_of(lax.axis_index("panel") * quarter, quarter)
    for k, ref in enumerate((coupling, m1, m2, m3)):
        q = order(k, panels)
        part = mul(f, coupling[0, 0, pl.ds(own, quarter), :] if k == 0 else ref[2 * rows :])
        high = part.astype(BF)
        low = (part - high.astype(F32)).astype(BF)
        for d in range(panels):
            send[d, q] = high[d * few : (d + 1) * few]
            send[d, panels + q] = low[d * few : (d + 1) * few]
    for k, out in enumerate(cols):
        target = lax.rem(lax.axis_index("panel") + k, panels)
        out[...] = inv[:, pl.ds(pl.multiple_of(target * quarter, quarter), quarter)]
    for d in range(panels):
        span = slice(d * few, (d + 1) * few)
        for index, value in enumerate((f[span], rhs[1, 0, span], rhs[2, 0, span])):
            send[d, 2 * panels + 2 * index] = value[:, :128]
            send[d, 2 * panels + 2 * index + 1] = value[:, 128:]


def place_body(level, counts, lists, out):
    _, _, leaf = leaf_place()
    mine = lists[level, pl.ds(leaf, 1), :]
    row = lax.broadcasted_iota(jnp.int32, out.shape, 0)
    col = lax.broadcasted_iota(jnp.int32, out.shape, 1)
    out[...] = jnp.where((row == mine) & (col < counts[level, leaf]), 1.0, 0.0).astype(BF)


def laid_out(level, u, placed, counts):
    _, _, leaf = leaf_place()
    col = lax.broadcasted_iota(jnp.int32, u.shape, 1)
    u = jnp.where(col < counts[level, leaf], u, 0.0).astype(BF)
    return mul_t(u, placed[...]).astype(BF)


def whole(got, index):
    panels = got.shape[0]
    first = 2 * panels + 2 * index
    return jnp.concatenate(
        [got[q, first + half] for q in range(panels) for half in range(2)], axis=1
    )


def up0_body(counts, got, placed, out):
    panels = got.shape[0]
    pieces = []
    for q in range(panels):
        total = None
        for source in range(panels):
            part = got[source, q].astype(F32) + got[source, panels + q].astype(F32)
            total = part if total is None else total + part
        pieces.append(total)
    e = laid_out(0, jnp.concatenate(pieces, axis=1), placed, counts)
    for d in range(out.shape[0]):
        out[d] = e


def summed(recv):
    total = recv[0].astype(F32)
    for j in range(1, recv.shape[0]):
        total = total + recv[j].astype(F32)
    return total


def forward(resid, inv):
    return jnp.concatenate([mul_t(resid, inv[q]) for q in range(inv.shape[0])], axis=1).astype(BF)


def backward(reduced, inv):
    rows = inv.shape[1]
    total = None
    for q in range(inv.shape[0]):
        part = mul(reduced[:, q * rows : (q + 1) * rows], inv[q])
        total = part if total is None else total + part
    return total.astype(BF)


def to_all(out, value):
    for d in range(out.shape[0]):
        out[d] = value


def up1_body(counts, recv, got, inv, placed, c0, c1, c2, c3, fout, out, scratch):
    resid = (whole(got, 1).astype(F32) - summed(recv)).astype(BF)
    f = forward(resid, inv)
    fout[...] = f
    blocks = (c0, c1, c2, c3)
    width = c0.shape[-1]
    for k, ref in enumerate(blocks):
        q = order(k, len(blocks))
        scratch[:, pl.ds(pl.multiple_of(q * width, width), width)] = mul(f, ref[...])
    to_all(out, laid_out(1, scratch[...], placed, counts))


def top_body(recv, got, inv, fout, out):
    resid = (whole(got, 2).astype(F32) - summed(recv)).astype(BF)
    f = forward(resid, inv)
    fout[...] = f
    to_all(out, backward(f, inv))


def fold_body(level, parents, blocks, out, acc):
    z, lane, _ = leaf_place()
    acc[...] = jnp.zeros_like(acc)
    for j in range(blocks.shape[0]):
        parent = parents[level, j * GROUP + lane]
        d = jnp.where(lax.div(parent, GROUP) == z, lax.rem(parent, GROUP), GROUP)
        acc[d] = acc[d] + blocks[j].astype(F32)
    for d in range(out.shape[0]):
        out[d] = acc[d].astype(BF)


def route_body(level, parents, blocks, out):
    z, _, _ = leaf_place()
    for d in range(out.shape[0]):
        out[d] = blocks[lax.div(parents[level, z * GROUP + d], GROUP)]


def lessened(level, f, recv, parents, placed, blocks, scratch):
    _, _, leaf = leaf_place()
    above = recv[lax.rem(parents[level, leaf], GROUP)]
    scratch[...] = mul(above, placed[...]).astype(BF)
    width = blocks[0].shape[-1]
    back = None
    for k, ref in enumerate(blocks):
        q = order(k, len(blocks))
        term = mul_t(scratch[:, pl.ds(pl.multiple_of(q * width, width), width)], ref[...])
        back = term if back is None else back + term
    return (f.astype(F32) - back).astype(BF)


def down1_body(parents, recv, f, inv, placed, c0, c1, c2, c3, out, scratch):
    red = lessened(1, f[...], recv, parents, placed, (c0, c1, c2, c3), scratch)
    to_all(out, backward(red, inv))


def down0_body(parents, recv, got, placed, c0, c1, c2, c3, f1, f2, s2, s1, o0, o1, o2, o3, scratch):
    outs = (o0, o1, o2, o3)
    width = f1.shape[1]
    quarter = width // len(outs)
    red = lessened(0, whole(got, 0), recv, parents, placed, (c0, c1, c2, c3), scratch)
    for k, out in enumerate(outs):
        target = lax.rem(lax.axis_index("panel") + k, len(outs))
        cols = pl.ds(pl.multiple_of(target * quarter, quarter), quarter)
        out[:, :width] = red
        for index, value in enumerate((f1[:, cols], f2[:, cols], s2[0, :, cols], s1[0, :, cols])):
            out[:, width + index * quarter : width + (index + 1) * quarter] = value


def last_body(mine, *refs):
    panels = (len(refs) - 3) // 2
    ends, cols = refs[:panels], refs[panels : 2 * panels]
    fwd, sol, reds = refs[2 * panels :]
    width = reds.shape[1]
    quarter = width // panels
    rows = ends[0].shape[0]
    fwd[0, 0] = mine[...]
    for k in range(panels):
        q = order(k, panels)
        span = pl.ds(pl.multiple_of(q * rows, rows), rows)
        reds[span] = ends[k][:, :width]
        for index, (out, level) in enumerate(((fwd, 1), (fwd, 2), (sol, 2), (sol, 1))):
            out[level, 0, span] = ends[k][:, width + index * quarter : width + (index + 1) * quarter]
    total = None
    for k in range(panels):
        q = order(k, panels)
        part = mul(reds[:, pl.ds(pl.multiple_of(q * quarter, quarter), quarter)], cols[k][...])
        total = part if total is None else total + part
    sol[0, 0] = total.astype(BF)


def local(rhs, inv_diag, coupling, row_lists, parents, counts):
    panels = lax.axis_size("panel")
    rows = rhs.shape[2] // panels
    mid = (GROUP, rows, inv_diag.shape[3])
    after = lax.optimization_barrier

    def spread(x):
        return [x] + [
            lax.ppermute(x, "panel", [(i, (i + k) % panels) for i in range(panels)])
            for k in range(1, panels)
        ]

    def gathered(level):
        return lax.all_gather(inv_late[level, 0], "panel", axis=0)

    def shifted(x, k):
        return lax.ppermute(x, "panel", [(i, (i + k) % panels) for i in range(panels)])

    def placement(level, counts):
        return call(
            functools.partial(place_body, level),
            sds(inv_diag.shape[3], row_lists.shape[2]),
            counts, row_lists,
            specs=[SMEM, VMEM],
        )

    half = coupling.shape[3]
    tall = rhs.shape[3]
    packs = call(
        pack_body, [sds(2 * rhs.shape[2] + tall, half)] * (panels - 1), rhs, coupling,
    )
    packs = [shifted(x, k) for k, x in enumerate(packs, 1)]
    placed0 = placement(0, counts)
    inv1 = lax.all_gather(inv_diag[1, 0], "panel", axis=0)
    base = inv_diag[0, 0]
    in2, in3, in4 = inv_diag[2, 0], coupling[0, 0], coupling[1, 0]
    base, in2, in3, in4 = after((base, in2, in3, in4))
    send, mine, *cols = call(
        first_body,
        [sds(panels, 14, rows, half), sds(rhs.shape[2], tall)] + [sds(tall, tall)] * panels,
        rhs, coupling, *packs, base,
    )
    got = lax.all_to_all(send, "panel", 0, 0)
    touched = pltpu.VMEM((rows, panels * half), BF)
    wide = pltpu.VMEM((rows, panels * half), F32)
    e = call(up0_body, sds(*mid), counts, got, placed0, specs=[SMEM] + [VMEM] * 2)
    e, early, in2, in4 = after((e, counts, in2, in4))
    c1 = spread(in4)
    inv2 = lax.all_gather(in2, "panel", axis=0)

    def beside(x, axes, small):
        x, small = after((x, small))
        x = lax.all_to_all(x, axes, 0, 0)
        return after((x, jnp.maximum(small, 0)))

    def fold(e, level, table):
        return call(
            functools.partial(fold_body, level), sds(*mid), table, e,
            specs=[SMEM, VMEM], scratch=[pltpu.VMEM((GROUP + 1, *mid[1:]), F32)],
        )

    def route(s, level, table):
        return call(functools.partial(route_body, level), sds(*mid), table, s, specs=[SMEM, VMEM])

    e = lax.all_to_all(e, "z", 0, 0)
    e, placed1 = after((e, placement(1, early)))
    e = fold(e, 0, parents)
    e = lax.all_to_all(e, ("x", "core"), 0, 0)
    f1, e = call(
        up1_body, (sds(*mid[1:]), sds(*mid)),
        counts, e, got, inv1, placed1, *c1,
        specs=[SMEM] + [VMEM] * 8, scratch=[wide],
    )
    e, table = beside(e, "z", parents)
    e = fold(e, 1, table)
    e = lax.all_to_all(e, ("x", "core"), 0, 0)
    f2, s2 = call(top_body, (sds(*mid[1:]), sds(*mid)), e, got, inv2)
    s = lax.all_to_all(s2, "z", 0, 0)
    s = route(s, 1, table)
    s = lax.all_to_all(s, ("x", "core"), 0, 0)
    s1 = call(
        down1_body, sds(*mid),
        table, s, f1, inv1, placed1, *c1,
        specs=[SMEM] + [VMEM] * 8, scratch=[touched],
    )
    s, in3, *cols = after((s1, in3, *cols))
    c0 = spread(in3)
    cols = cols[:1] + [shifted(x, k) for k, x in enumerate(cols[1:], 1)]
    s = lax.all_to_all(s, "z", 0, 0)
    s = route(s, 0, table)
    s = lax.all_to_all(s, ("x", "core"), 0, 0)
    ends = call(
        down0_body, [sds(rows, 2 * mid[2])] * panels,
        table, s, got, placed0, *c0, f1, f2, s2, s1,
        specs=[SMEM] + [VMEM] * 11, scratch=[touched],
    )
    ends = [ends[0]] + [shifted(x, k) for k, x in enumerate(ends[1:], 1)]
    return call(
        last_body, (sds(*rhs.shape), sds(*rhs.shape)), mine, *ends, *cols,
        scratch=[pltpu.VMEM((rhs.shape[2], mid[2]), BF)],
    )


def solution(mesh):
    leaves, panels = mesh.shape["leaf"], mesh.shape["panel"]
    inner = Mesh(
        mesh.devices.reshape(leaves // GROUP, GROUP // 2, 2, panels), ("z", "x", "core", "panel")
    )
    leaf = ("z", "x", "core")
    placed = (
        P(None, leaf, None, "panel"),
        P(None, leaf, "panel", None),
        P(None, leaf, None, "panel"),
        P(),
        P(),
        P(),
    )
    return jax.shard_map(
        local,
        mesh=inner,
        in_specs=placed,
        out_specs=(P(None, leaf, None, "panel"), P(None, leaf, None, "panel")),
        check_vma=False,
    )
```

time: 206 us -> 178 us (0.86)
  blocking collectives: 51.2 us -> 24.1 us
  starting transfers between devices: 42 us -> 50.9 us
  local copies, waits for them, and re-layouts: 17.6 us -> 10.5 us
  between operations: 17.9 us -> 14.3 us
  Pallas kernels: 15.4 us -> 18.5 us
    all_to_all x4 -> x2, blocking collectives: 51.2 us -> 24.1 us  [the longest x1 14.2 us: local(): s = lax.all_to_all(s2, 'z', 0, 0)]
    ppermute x0 -> x9, waiting for transfers between devices: none -> 11.1 us  [shifted(): lax.ppermute(x, 'panel', [(i, (i + k) % panels) for i in range(panels)])]
    ppermute x0 -> x9, starting transfers between devices: none -> 10.5 us  [shifted(): lax.ppermute(x, 'panel', [(i, (i + k) % panels) for i in range(panels)])]
    all_to_all x1, waiting for transfers between devices: 15.7 us -> 5.75 us  [local(): got = lax.all_to_all(send, 'panel', 0, 0)]
    unnamed x44 -> x36, local copies, waits for them, and re-layouts: 11.2 us -> 7.96 us
    ppermute x9 -> x6, starting transfers between devices: 12.8 us -> 9.63 us  [spread(): lax.ppermute(x, 'panel', [(i, (i + k) % panels) for i in range(panels)])]
    pallas_call x11 -> x14, Pallas kernels: 15.4 us -> 18.5 us  [call(): pl.pallas_call(body, out_shape=outs, in_specs=specs, out_specs=outs_at, s...]
    all_to_all x5 -> x6, starting transfers between devices: 24.6 us -> 26.2 us  [the longest x1 8.22 us: local(): e = lax.all_to_all(e, 'z', 0, 0)]
  transfers between devices with their start and end apart: 18 -> 24, of which waited for: 6 -> 13; matrix products, arithmetic and copies ran while one was open for 2% -> 0% of each run, Pallas kernels for 6% -> 7%
where the time goes in v2:
time: 178 us; the launch traced here: 176 us
  waiting for transfers between devices  58.2 us (33%)
  starting transfers between devices  50.9 us (29%)
  blocking collectives  24.1 us (14%)
  Pallas kernels  18.5 us (10%)
  between operations  14.3 us (8%)
  local copies, waits for them, and re-layouts  10.5 us (6%)
    pallas_call x14, Pallas kernels, call(): pl.pallas_call(body, out_shape=outs, in_specs=specs, out_specs=outs_at, s...  18.5 us
    all_to_all x2, waiting for transfers between devices, local(): e = lax.all_to_all(e, ('x', 'core'), 0, 0)  14.9 us
    all_to_all x1, blocking collectives, local(): s = lax.all_to_all(s2, 'z', 0, 0)  14.2 us
    all_to_all x1, waiting for transfers between devices, beside(): x = lax.all_to_all(x, axes, 0, 0)  11.6 us
    ppermute x9, waiting for transfers between devices, shifted(): lax.ppermute(x, 'panel', [(i, (i + k) % panels) for i in range(panels)])  11.1 us
    ppermute x9, starting transfers between devices, shifted(): lax.ppermute(x, 'panel', [(i, (i + k) % panels) for i in range(panels)])  10.5 us
    all_to_all x1, blocking collectives, local(): s = lax.all_to_all(s, ('x', 'core'), 0, 0)  9.95 us
    ppermute x6, starting transfers between devices, spread(): lax.ppermute(x, 'panel', [(i, (i + k) % panels) for i in range(panels)])  9.63 us
  transfers between devices with their start and end apart: 24, of which 13 were waited for; matrix products, arithmetic and copies ran while one was open for 0% of the time, Pallas kernels for 7%

profile of v2, /device:TPU:24, one launch (start us, length us, event | category | flops | bytes accessed | tf_op | source)
XLA Modules:
  0.0 176.4 jit_solution(12024108690993405655)
XLA Ops:
  7.2 2.5 %fusion = (bf16[1,1,256,1024]{3,2,1,0:T(8,128)(2,1)}, bf16[256,1024]{1,0:T(8,128)(2,1)S(1)}, bf16[256,1024]{1,0:T(8,128)(2,1)}) fusion(bf16[3,1,256,1024]{3,2,1,0:T(8,128)(2,1)} %param.7), kind=kLoop, calls=%fused_computation.5 | loop fusion | bytes 3145728 | tf_op jit(solution)/shard_map/slice | solution.py:289
  9.8 2.0 %collective-permute-start = (bf16[384,128]{1,0:T(8,128)(2,1)S(1)}, bf16[384,128]{1,0:T(8,128)(2,1)S(1)}, u32[]{:S(2)}, u32[]{:S(2)}) collective-permute-start(bf16[384,128]{1,0:T(8,128)(2,1)S(1)} %get-tuple-element.39), channel_id=1, source_target_pairs={{0,1},{1,2},{2,3},{3,0},{4,5},{5,6},{6,7},{7,4},{8,9},{9,10},{10,1... | collective-permute-start | bytes 294920 | tf_op jit(solution)/shard_map/ppermute | solution.py:272
  12.8 2.6 %collective-permute-done.m1 = bf16[384,128]{1,0:T(8,128)(2,1)S(1)} collective-permute-done((bf16[384,128]{1,0:T(8,128)(2,1)S(1)}, bf16[384,128]{1,0:T(8,128)(2,1)S(1)}, u32[]{:S(2)}, u32[]{:S(2)}) %collective-permute-start) | collective-permute-done | bytes 98336 | tf_op jit(solution)/shard_map/ppermute | solution.py:272
  15.5 2.6 %collective-permute-done.1.m2 = bf16[384,128]{1,0:T(8,128)(2,1)S(1)} collective-permute-done((bf16[384,128]{1,0:T(8,128)(2,1)S(1)}, bf16[384,128]{1,0:T(8,128)(2,1)S(1)}, u32[]{:S(2)}, u32[]{:S(2)}) %collective-permute-start.1) | collective-permute-done | bytes 98336 | tf_op jit(solution)/shard_map/ppermute | solution.py:272
  20.9 4.5 %all-to-all-start = ((bf16[4,14,16,128]{3,2,1,0:T(8,128)(2,1)}), bf16[4,14,16,128]{3,2,1,0:T(8,128)(2,1)S(1)}, u32[]{:S(2)}, u32[]{:S(2)}) async-start(bf16[4,14,16,128]{3,2,1,0:T(8,128)(2,1)} %get-tuple-element.44), calls=%async_computation | async-start | bytes 458752 | tf_op jit(solution)/shard_map/all_to_all | solution.py:298
  26.2 5.8 %all-to-all-done.got = bf16[4,14,16,128]{3,2,1,0:T(8,128)(2,1)S(1)} async-done(((bf16[4,14,16,128]{3,2,1,0:T(8,128)(2,1)}), bf16[4,14,16,128]{3,2,1,0:T(8,128)(2,1)S(1)}, u32[]{:S(2)}, u32[]{:S(2)}) %all-to-all-start) | async-done | bytes 229408 | tf_op jit(solution)/shard_map/all_to_all | solution.py:298
  31.9 1.6 shard_map.80
  33.6 8.2 %all-to-all-start.1 = ((bf16[8,16,1024]{2,1,0:T(8,128)(2,1)}), bf16[8,16,1024]{2,1,0:T(8,128)(2,1)S(1)}, u32[]{:S(2)}, u32[]{:S(2)}) async-start(bf16[8,16,1024]{2,1,0:T(8,128)(2,1)} %shard_map.80), calls=%async_computation.1 | async-start | bytes 524288 | tf_op jit(solution)/shard_map/all_to_all | solution.py:320
  41.8 3.7 %collective-permute-start.4 = (bf16[1024,128]{1,0:T(8,128)(2,1)S(1)}, bf16[1024,128]{1,0:T(8,128)(2,1)}, u32[]{:S(2)}, u32[]{:S(2)}) collective-permute-start(bf16[1024,128]{1,0:T(8,128)(2,1)S(1)} %get-tuple-element.51.c0), channel_id=1, source_target_pairs={{0,2},{1,3},{2,0},{3,1},{4,6},{5,7},{6,4},{7,5},{8,10},{9,11},{10,... | collective-permute-start | bytes 786440 | tf_op jit(solution)/shard_map/ppermute | solution.py:264
  47.4 4.9 %all-to-all-done.1.blocks = bf16[8,16,1024]{2,1,0:T(8,128)(2,1)S(1)} async-done(((bf16[8,16,1024]{2,1,0:T(8,128)(2,1)}), bf16[8,16,1024]{2,1,0:T(8,128)(2,1)S(1)}, u32[]{:S(2)}, u32[]{:S(2)}) %all-to-all-start.1) | async-done | bytes 262176 | tf_op jit(solution)/shard_map/all_to_all | solution.py:320
  53.7 4.3 %all-to-all-start.2 = ((bf16[8,16,1024]{2,1,0:T(8,128)(2,1)}), bf16[8,16,1024]{2,1,0:T(8,128)(2,1)S(1)}, u32[]{:S(2)}, u32[]{:S(2)}) async-start(bf16[8,16,1024]{2,1,0:T(8,128)(2,1)} %shard_map.82), calls=%async_computation.2 | async-start | bytes 524288 | tf_op jit(solution)/shard_map/all_to_all | solution.py:323
  58.1 7.5 %all-to-all-done.2.recv = bf16[8,16,1024]{2,1,0:T(8,128)(2,1)S(1)} async-done(((bf16[8,16,1024]{2,1,0:T(8,128)(2,1)}), bf16[8,16,1024]{2,1,0:T(8,128)(2,1)S(1)}, u32[]{:S(2)}, u32[]{:S(2)}) %all-to-all-start.2) | async-done | bytes 262176 | tf_op jit(solution)/shard_map/all_to_all | solution.py:323
  65.6 1.7 copy-done
  67.3 3.1 %shard_map.83 = (bf16[16,1024]{1,0:T(8,128)(2,1)S(1)}, bf16[8,16,1024]{2,1,0:T(8,128)(2,1)}) custom-call(s32[2,64]{1,0:T(2,128)S(1)} %copy-done.13, bf16[8,16,1024]{2,1,0:T(8,128)(2,1)S(1)} %all-to-all-done.2.recv, bf16[4,14,16,128]{3,2,1,0:T(8,128)(2,1)S(1)} %all-to-all-done.got, bf16[4,256,1024]{2,1,0:T(8,128)(2,1)S(1)} %bitcast.10, ...), custom_call_target="tpu_custom_call" | custom-call | tf_op jit(solution)/shard_map/pallas_call | solution.py:33
  70.4 3.4 %all-to-all-start.3 = ((bf16[8,16,1024]{2,1,0:T(8,128)(2,1)}), bf16[8,16,1024]{2,1,0:T(8,128)(2,1)S(1)}, u32[]{:S(2)}, u32[]{:S(2)}) async-start(bf16[8,16,1024]{2,1,0:T(8,128)(2,1)} %get-tuple-element.53), calls=%async_computation.3 | async-start | bytes 524288 | tf_op jit(solution)/shard_map/all_to_all | solution.py:308
  73.8 11.6 %all-to-all-done.3.blocks = bf16[8,16,1024]{2,1,0:T(8,128)(2,1)S(1)} async-done(((bf16[8,16,1024]{2,1,0:T(8,128)(2,1)}), bf16[8,16,1024]{2,1,0:T(8,128)(2,1)S(1)}, u32[]{:S(2)}, u32[]{:S(2)}) %all-to-all-start.3) | async-done | bytes 262176 | tf_op jit(solution)/shard_map/all_to_all | solution.py:308
  86.8 3.4 %all-to-all-start.4 = ((bf16[8,16,1024]{2,1,0:T(8,128)(2,1)}), bf16[8,16,1024]{2,1,0:T(8,128)(2,1)S(1)}, u32[]{:S(2)}, u32[]{:S(2)}) async-start(bf16[8,16,1024]{2,1,0:T(8,128)(2,1)} %copy-done.4), calls=%async_computation.4 | async-start | bytes 524288 | tf_op jit(solution)/shard_map/all_to_all | solution.py:331
  90.2 7.4 %all-to-all-done.4.recv = bf16[8,16,1024]{2,1,0:T(8,128)(2,1)S(1)} async-done(((bf16[8,16,1024]{2,1,0:T(8,128)(2,1)}), bf16[8,16,1024]{2,1,0:T(8,128)(2,1)S(1)}, u32[]{:S(2)}, u32[]{:S(2)}) %all-to-all-start.4) | async-done | bytes 262176 | tf_op jit(solution)/shard_map/all_to_all | solution.py:331
  97.7 1.7 copy-done.3
  100.4 14.2 %all_to_all.45.blocks = bf16[8,16,1024]{2,1,0:T(8,128)(2,1)S(1)} all-to-all(bf16[8,16,1024]{2,1,0:T(8,128)(2,1)S(1)} %get-tuple-element.58.s2), channel_id=1, replica_groups=mesh['z'=8,'x'=4,'core'=2,'panel'=4] {'z'}, dimensions={0} | all-to-all | bytes 524288 | tf_op jit(solution)/shard_map/all_to_all | solution.py:333
  115.2 9.9 %all_to_all.46.recv = bf16[8,16,1024]{2,1,0:T(8,128)(2,1)S(1)} all-to-all(bf16[8,16,1024]{2,1,0:T(8,128)(2,1)S(1)} %shard_map.86), channel_id=1, replica_groups=mesh['z'=8,'x'=4,'core'=2,'panel'=4] {'x','core'}, dimensions={0} | all-to-all | bytes 524288 | tf_op jit(solution)/shard_map/all_to_all | solution.py:335
  125.1 2.8 %shard_map.87.s1 = bf16[8,16,1024]{2,1,0:T(8,128)(2,1)} custom-call(s32[2,64]{1,0:T(2,128)S(1)} %broadcast_maximum_fusion.parents, bf16[8,16,1024]{2,1,0:T(8,128)(2,1)S(1)} %all_to_all.46.recv, bf16[16,1024]{1,0:T(8,128)(2,1)S(1)} %get-tuple-element.59.f.f1, bf16[4,256,1024]{2,1,0:T(8,128)(2,1)S(1)} %bitcast.11, bf16[1024,512]{1,0:T(8,128)(2,1)S(1)} %shard_map.81.placed, ...), custom_call_target="tpu_custom_call" | custom-call | tf_op jit(solution)/shard_map/pallas_call | solution.py:33
  127.9 3.4 %all-to-all-start.7 = ((bf16[8,16,1024]{2,1,0:T(8,128)(2,1)}), bf16[8,16,1024]{2,1,0:T(8,128)(2,1)S(1)}, u32[]{:S(2)}, u32[]{:S(2)}) async-start(bf16[8,16,1024]{2,1,0:T(8,128)(2,1)} %shard_map.87.s1), calls=%async_computation.7 | async-start | bytes 524288 | tf_op jit(solution)/shard_map/all_to_all | solution.py:344
  131.4 3.8 %collective-permute-start.7 = (bf16[1024,128]{1,0:T(8,128)(2,1)S(1)}, bf16[1024,128]{1,0:T(8,128)(2,1)S(1)}, u32[]{:S(2)}, u32[]{:S(2)}) collective-permute-start(bf16[1024,128]{1,0:T(8,128)(2,1)S(1)} %get-tuple-element.66.c0), channel_id=1, source_target_pairs={{0,2},{1,3},{2,0},{3,1},{4,6},{5,7},{6,4},{7,5},{8,10},{9,11},{10,... | collective-permute-start | bytes 786440 | tf_op jit(solution)/shard_map/ppermute | solution.py:264
  136.2 6.8 %all-to-all-done.7.blocks = bf16[8,16,1024]{2,1,0:T(8,128)(2,1)S(1)} async-done(((bf16[8,16,1024]{2,1,0:T(8,128)(2,1)}), bf16[8,16,1024]{2,1,0:T(8,128)(2,1)S(1)}, u32[]{:S(2)}, u32[]{:S(2)}) %all-to-all-start.7) | async-done | bytes 262176 | tf_op jit(solution)/shard_map/all_to_all | solution.py:344
  144.3 3.4 %all-to-all-start.8 = ((bf16[8,16,1024]{2,1,0:T(8,128)(2,1)}), bf16[8,16,1024]{2,1,0:T(8,128)(2,1)S(1)}, u32[]{:S(2)}, u32[]{:S(2)}) async-start(bf16[8,16,1024]{2,1,0:T(8,128)(2,1)} %shard_map.88), calls=%async_computation.8 | async-start | bytes 524288 | tf_op jit(solution)/shard_map/all_to_all | solution.py:346
  147.7 2.6 %collective-permute-start.12 = (bf16[256,256]{1,0:T(8,128)(2,1)}, bf16[256,256]{1,0:T(8,128)(2,1)S(1)}, u32[]{:S(2)}, u32[]{:S(2)}) collective-permute-start(bf16[256,256]{1,0:T(8,128)(2,1)} %copy-done.17), channel_id=1, source_target_pairs={{0,1},{1,2},{2,3},{3,0},{4,5},{5,6},{6,7},{7,4},{8,9},{9,10},{10,1... | collective-permute-start | bytes 393224 | tf_op jit(solution)/shard_map/ppermute | solution.py:272
  152.2 2.9 %all-to-all-done.8.recv = bf16[8,16,1024]{2,1,0:T(8,128)(2,1)S(1)} async-done(((bf16[8,16,1024]{2,1,0:T(8,128)(2,1)}), bf16[8,16,1024]{2,1,0:T(8,128)(2,1)S(1)}, u32[]{:S(2)}, u32[]{:S(2)}) %all-to-all-start.8) | async-done | bytes 262176 | tf_op jit(solution)/shard_map/all_to_all | solution.py:346
  156.9 1.6 shard_map.89
  158.4 2.4 %collective-permute-start.9 = (bf16[16,2048]{1,0:T(8,128)(2,1)S(1)}, bf16[16,2048]{1,0:T(8,128)(2,1)S(1)}, u32[]{:S(2)}, u32[]{:S(2)}) collective-permute-start(bf16[16,2048]{1,0:T(8,128)(2,1)S(1)} %get-tuple-element.69), channel_id=1, source_target_pairs={{0,1},{1,2},{2,3},{3,0},{4,5},{5,6},{6,7},{7,4},{8,9},{9,10},{10,1... | collective-permute-start | bytes 196616 | tf_op jit(solution)/shard_map/ppermute | solution.py:272
  163.2 3.4 %collective-permute-done.10.refs_2_ = bf16[16,2048]{1,0:T(8,128)(2,1)S(1)} collective-permute-done((bf16[16,2048]{1,0:T(8,128)(2,1)S(1)}, bf16[16,2048]{1,0:T(8,128)(2,1)S(1)}, u32[]{:S(2)}, u32[]{:S(2)}) %collective-permute-start.10) | collective-permute-done | bytes 65568 | tf_op jit(solution)/shard_map/ppermute | solution.py:272
  167.8 1.8 shard_map.90
  (73 shorter events, 20.4 us)
Async XLA Ops:
  7.2 58.4 %all-gather.5.cloned.1.call-start = ((), (), s32[]{:S(2)}) async-start(), calls=%async_computation.9 | async-start | bytes 2621440 | tf_op jit(solution)/shard_map/all_gather | solution.py:289
  9.7 15.7 %copy-start.5 = (s32[2,64,512]{2,1,0:T(8,128)S(1)}, s32[2,64,512]{2,1,0:T(8,128)}, u32[]{:S(2)}) copy-start(s32[2,64,512]{2,1,0:T(8,128)} %lists.3) | copy-start | bytes 786436
  9.7 15.7 %copy-start.13 = (s32[2,64]{1,0:T(2,128)S(1)}, s32[2,64]{1,0:T(2,128)}, u32[]{:S(2)}) copy-start(s32[2,64]{1,0:T(2,128)} %counts.6) | copy-start | bytes 1540
  9.8 5.7 %collective-permute-start = (bf16[384,128]{1,0:T(8,128)(2,1)S(1)}, bf16[384,128]{1,0:T(8,128)(2,1)S(1)}, u32[]{:S(2)}, u32[]{:S(2)}) collective-permute-start(bf16[384,128]{1,0:T(8,128)(2,1)S(1)} %get-tuple-element.39), channel_id=1, source_target_pairs={{0,1},{1,2},{2,3},{3,0},{4,5},{5,6},{6,7},{7,4},{8,9},{9,10},{10,1... | collective-permute-start | bytes 294920 | tf_op jit(solution)/shard_map/ppermute | solution.py:272
  11.8 6.2 %collective-permute-start.1 = (bf16[384,128]{1,0:T(8,128)(2,1)S(1)}, bf16[384,128]{1,0:T(8,128)(2,1)S(1)}, u32[]{:S(2)}, u32[]{:S(2)}) collective-permute-start(bf16[384,128]{1,0:T(8,128)(2,1)S(1)} %get-tuple-element.40), channel_id=1, source_target_pairs={{0,2},{1,3},{2,0},{3,1},{4,6},{5,7},{6,4},{7,5},{8,10},{9,11},{10,... | collective-permute-start | bytes 294920 | tf_op jit(solution)/shard_map/ppermute | solution.py:272
  12.7 6.4 %collective-permute-start.2 = (bf16[384,128]{1,0:T(8,128)(2,1)S(1)}, bf16[384,128]{1,0:T(8,128)(2,1)S(1)}, u32[]{:S(2)}, u32[]{:S(2)}) collective-permute-start(bf16[384,128]{1,0:T(8,128)(2,1)S(1)} %get-tuple-element.41), channel_id=1, source_target_pairs={{0,3},{1,0},{2,1},{3,2},{4,7},{5,4},{6,5},{7,6},{8,11},{9,8},{10,9... | collective-permute-start | bytes 294920 | tf_op jit(solution)/shard_map/ppermute | solution.py:272
  20.9 24.6 %copy-start.15 = (bf16[256,256]{1,0:T(8,128)(2,1)}, bf16[256,256]{1,0:T(8,128)(2,1)S(1)}, u32[]{:S(2)}) copy-start(bf16[256,256]{1,0:T(8,128)(2,1)S(1)} %get-tuple-element.75) | copy-start | bytes 393220
  20.9 24.6 %copy-start.16 = (bf16[256,256]{1,0:T(8,128)(2,1)}, bf16[256,256]{1,0:T(8,128)(2,1)S(1)}, u32[]{:S(2)}) copy-start(bf16[256,256]{1,0:T(8,128)(2,1)S(1)} %get-tuple-element.74) | copy-start | bytes 393220
  20.9 24.6 %copy-start.17 = (bf16[256,256]{1,0:T(8,128)(2,1)}, bf16[256,256]{1,0:T(8,128)(2,1)S(1)}, u32[]{:S(2)}) copy-start(bf16[256,256]{1,0:T(8,128)(2,1)S(1)} %get-tuple-element.73) | copy-start | bytes 393220
  20.9 11.0 %all-to-all-start = ((bf16[4,14,16,128]{3,2,1,0:T(8,128)(2,1)}), bf16[4,14,16,128]{3,2,1,0:T(8,128)(2,1)S(1)}, u32[]{:S(2)}, u32[]{:S(2)}) async-start(bf16[4,14,16,128]{3,2,1,0:T(8,128)(2,1)} %get-tuple-element.44), calls=%async_computation | async-start | bytes 458752 | tf_op jit(solution)/shard_map/all_to_all | solution.py:298
  25.4 64.8 %all-gather.7.cloned.1.call-start = ((), (), s32[]{:S(2)}) async-start(), calls=%async_computation.10 | async-start | bytes 2621440 | tf_op jit(solution)/shard_map/all_gather | solution.py:304
  26.2 26.1 %copy-start.14 = (s32[2,64]{1,0:T(2,128)S(1)}, s32[2,64]{1,0:T(2,128)}, u32[]{:S(2)}) copy-start(s32[2,64]{1,0:T(2,128)} %parents.1) | copy-start | bytes 1540
  33.6 18.7 %all-to-all-start.1 = ((bf16[8,16,1024]{2,1,0:T(8,128)(2,1)}), bf16[8,16,1024]{2,1,0:T(8,128)(2,1)S(1)}, u32[]{:S(2)}, u32[]{:S(2)}) async-start(bf16[8,16,1024]{2,1,0:T(8,128)(2,1)} %shard_map.80), calls=%async_computation.1 | async-start | bytes 524288 | tf_op jit(solution)/shard_map/all_to_all | solution.py:320
  41.8 16.2 %collective-permute-start.5 = (bf16[1024,128]{1,0:T(8,128)(2,1)S(1)}, bf16[1024,128]{1,0:T(8,128)(2,1)}, u32[]{:S(2)}, u32[]{:S(2)}) collective-permute-start(bf16[1024,128]{1,0:T(8,128)(2,1)S(1)} %get-tuple-element.51.c0), channel_id=1, source_target_pairs={{0,3},{1,0},{2,1},{3,2},{4,7},{5,4},{6,5},{7,6},{8,11},{9,8},{10,9... | collective-permute-start | bytes 786440 | tf_op jit(solution)/shard_map/ppermute | solution.py:264
  41.8 16.2 %collective-permute-start.4 = (bf16[1024,128]{1,0:T(8,128)(2,1)S(1)}, bf16[1024,128]{1,0:T(8,128)(2,1)}, u32[]{:S(2)}, u32[]{:S(2)}) collective-permute-start(bf16[1024,128]{1,0:T(8,128)(2,1)S(1)} %get-tuple-element.51.c0), channel_id=1, source_target_pairs={{0,2},{1,3},{2,0},{3,1},{4,6},{5,7},{6,4},{7,5},{8,10},{9,11},{10,... | collective-permute-start | bytes 786440 | tf_op jit(solution)/shard_map/ppermute | solution.py:264
  45.5 12.5 %collective-permute-start.3 = (bf16[1024,128]{1,0:T(8,128)(2,1)S(1)}, bf16[1024,128]{1,0:T(8,128)(2,1)}, u32[]{:S(2)}, u32[]{:S(2)}) collective-permute-start(bf16[1024,128]{1,0:T(8,128)(2,1)S(1)} %get-tuple-element.51.c0), channel_id=1, source_target_pairs={{0,1},{1,2},{2,3},{3,0},{4,5},{5,6},{6,7},{7,4},{8,9},{9,10},{10,1... | collective-permute-start | bytes 786440 | tf_op jit(solution)/shard_map/ppermute | solution.py:264
  53.7 11.9 %all-to-all-start.2 = ((bf16[8,16,1024]{2,1,0:T(8,128)(2,1)}), bf16[8,16,1024]{2,1,0:T(8,128)(2,1)S(1)}, u32[]{:S(2)}, u32[]{:S(2)}) async-start(bf16[8,16,1024]{2,1,0:T(8,128)(2,1)} %shard_map.82), calls=%async_computation.2 | async-start | bytes 524288 | tf_op jit(solution)/shard_map/all_to_all | solution.py:323
  70.4 15.0 %all-to-all-start.3 = ((bf16[8,16,1024]{2,1,0:T(8,128)(2,1)}), bf16[8,16,1024]{2,1,0:T(8,128)(2,1)S(1)}, u32[]{:S(2)}, u32[]{:S(2)}) async-start(bf16[8,16,1024]{2,1,0:T(8,128)(2,1)} %get-tuple-element.53), calls=%async_computation.3 | async-start | bytes 524288 | tf_op jit(solution)/shard_map/all_to_all | solution.py:308
  86.8 10.9 %all-to-all-start.4 = ((bf16[8,16,1024]{2,1,0:T(8,128)(2,1)}), bf16[8,16,1024]{2,1,0:T(8,128)(2,1)S(1)}, u32[]{:S(2)}, u32[]{:S(2)}) async-start(bf16[8,16,1024]{2,1,0:T(8,128)(2,1)} %copy-done.4), calls=%async_computation.4 | async-start | bytes 524288 | tf_op jit(solution)/shard_map/all_to_all | solution.py:331
  97.7 27.4 %copy-start.1 = (bf16[4,1,256,1024]{3,2,1,0:T(8,128)(2,1)S(1)}, bf16[4,1,256,1024]{3,2,1,0:T(8,128)(2,1)}, u32[]{:S(2)}) copy-start(bf16[4,1,256,1024]{3,2,1,0:T(8,128)(2,1)} %all-gather.5.cloned.1.call-done) | copy-start | bytes 6291460
  100.3 27.5 %copy-start.9 = (bf16[16,1024]{1,0:T(8,128)(2,1)}, bf16[16,1024]{1,0:T(8,128)(2,1)S(1)}, u32[]{:S(2)}) copy-start(bf16[16,1024]{1,0:T(8,128)(2,1)S(1)} %get-tuple-element.67.f2) | copy-start | bytes 98308
  127.9 15.1 %all-to-all-start.7 = ((bf16[8,16,1024]{2,1,0:T(8,128)(2,1)}), bf16[8,16,1024]{2,1,0:T(8,128)(2,1)S(1)}, u32[]{:S(2)}, u32[]{:S(2)}) async-start(bf16[8,16,1024]{2,1,0:T(8,128)(2,1)} %shard_map.87.s1), calls=%async_computation.7 | async-start | bytes 524288 | tf_op jit(solution)/shard_map/all_to_all | solution.py:344
  131.3 19.0 %collective-permute-start.8 = (bf16[1024,128]{1,0:T(8,128)(2,1)S(1)}, bf16[1024,128]{1,0:T(8,128)(2,1)S(1)}, u32[]{:S(2)}, u32[]{:S(2)}) collective-permute-start(bf16[1024,128]{1,0:T(8,128)(2,1)S(1)} %get-tuple-element.66.c0), channel_id=1, source_target_pairs={{0,3},{1,0},{2,1},{3,2},{4,7},{5,4},{6,5},{7,6},{8,11},{9,8},{10,9... | collective-permute-start | bytes 786440 | tf_op jit(solution)/shard_map/ppermute | solution.py:264
  131.4 20.2 %collective-permute-start.7 = (bf16[1024,128]{1,0:T(8,128)(2,1)S(1)}, bf16[1024,128]{1,0:T(8,128)(2,1)S(1)}, u32[]{:S(2)}, u32[]{:S(2)}) collective-permute-start(bf16[1024,128]{1,0:T(8,128)(2,1)S(1)} %get-tuple-element.66.c0), channel_id=1, source_target_pairs={{0,2},{1,3},{2,0},{3,1},{4,6},{5,7},{6,4},{7,5},{8,10},{9,11},{10,... | collective-permute-start | bytes 786440 | tf_op jit(solution)/shard_map/ppermute | solution.py:264
  135.2 16.4 %collective-permute-start.6 = (bf16[1024,128]{1,0:T(8,128)(2,1)S(1)}, bf16[1024,128]{1,0:T(8,128)(2,1)S(1)}, u32[]{:S(2)}, u32[]{:S(2)}) collective-permute-start(bf16[1024,128]{1,0:T(8,128)(2,1)S(1)} %get-tuple-element.66.c0), channel_id=1, source_target_pairs={{0,1},{1,2},{2,3},{3,0},{4,5},{5,6},{6,7},{7,4},{8,9},{9,10},{10,1... | collective-permute-start | bytes 786440 | tf_op jit(solution)/shard_map/ppermute | solution.py:264
  144.3 10.9 %all-to-all-start.8 = ((bf16[8,16,1024]{2,1,0:T(8,128)(2,1)}), bf16[8,16,1024]{2,1,0:T(8,128)(2,1)S(1)}, u32[]{:S(2)}, u32[]{:S(2)}) async-start(bf16[8,16,1024]{2,1,0:T(8,128)(2,1)} %shard_map.88), calls=%async_computation.8 | async-start | bytes 524288 | tf_op jit(solution)/shard_map/all_to_all | solution.py:346
  147.7 13.2 %collective-permute-start.12 = (bf16[256,256]{1,0:T(8,128)(2,1)}, bf16[256,256]{1,0:T(8,128)(2,1)S(1)}, u32[]{:S(2)}, u32[]{:S(2)}) collective-permute-start(bf16[256,256]{1,0:T(8,128)(2,1)} %copy-done.17), channel_id=1, source_target_pairs={{0,1},{1,2},{2,3},{3,0},{4,5},{5,6},{6,7},{7,4},{8,9},{9,10},{10,1... | collective-permute-start | bytes 393224 | tf_op jit(solution)/shard_map/ppermute | solution.py:272
  150.3 11.8 %collective-permute-start.13 = (bf16[256,256]{1,0:T(8,128)(2,1)}, bf16[256,256]{1,0:T(8,128)(2,1)S(1)}, u32[]{:S(2)}, u32[]{:S(2)}) collective-permute-start(bf16[256,256]{1,0:T(8,128)(2,1)} %copy-done.16), channel_id=1, source_target_pairs={{0,2},{1,3},{2,0},{3,1},{4,6},{5,7},{6,4},{7,5},{8,10},{9,11},{10,... | collective-permute-start | bytes 393224 | tf_op jit(solution)/shard_map/ppermute | solution.py:272
  150.3 11.8 %collective-permute-start.14 = (bf16[256,256]{1,0:T(8,128)(2,1)}, bf16[256,256]{1,0:T(8,128)(2,1)}, u32[]{:S(2)}, u32[]{:S(2)}) collective-permute-start(bf16[256,256]{1,0:T(8,128)(2,1)} %copy-done.15), channel_id=1, source_target_pairs={{0,3},{1,0},{2,1},{3,2},{4,7},{5,4},{6,5},{7,6},{8,11},{9,8},{10,9... | collective-permute-start | bytes 393224 | tf_op jit(solution)/shard_map/ppermute | solution.py:272
  158.4 4.8 %collective-permute-start.9 = (bf16[16,2048]{1,0:T(8,128)(2,1)S(1)}, bf16[16,2048]{1,0:T(8,128)(2,1)S(1)}, u32[]{:S(2)}, u32[]{:S(2)}) collective-permute-start(bf16[16,2048]{1,0:T(8,128)(2,1)S(1)} %get-tuple-element.69), channel_id=1, source_target_pairs={{0,1},{1,2},{2,3},{3,0},{4,5},{5,6},{6,7},{7,4},{8,9},{9,10},{10,1... | collective-permute-start | bytes 196616 | tf_op jit(solution)/shard_map/ppermute | solution.py:272
  160.8 5.8 %collective-permute-start.10 = (bf16[16,2048]{1,0:T(8,128)(2,1)S(1)}, bf16[16,2048]{1,0:T(8,128)(2,1)S(1)}, u32[]{:S(2)}, u32[]{:S(2)}) collective-permute-start(bf16[16,2048]{1,0:T(8,128)(2,1)S(1)} %get-tuple-element.70), channel_id=1, source_target_pairs={{0,2},{1,3},{2,0},{3,1},{4,6},{5,7},{6,4},{7,5},{8,10},{9,11},{10,... | collective-permute-start | bytes 196616 | tf_op jit(solution)/shard_map/ppermute | solution.py:272
  160.8 6.2 %collective-permute-start.11 = (bf16[16,2048]{1,0:T(8,128)(2,1)S(1)}, bf16[16,2048]{1,0:T(8,128)(2,1)S(1)}, u32[]{:S(2)}, u32[]{:S(2)}) collective-permute-start(bf16[16,2048]{1,0:T(8,128)(2,1)S(1)} %get-tuple-element.71), channel_id=1, source_target_pairs={{0,3},{1,0},{2,1},{3,2},{4,7},{5,4},{6,5},{7,6},{8,11},{9,8},{10,9... | collective-permute-start | bytes 196616 | tf_op jit(solution)/shard_map/ppermute | solution.py:272
  (10 other events, 13.1 us)
Sparse Core Ops, SparseCore 0:
  9.9 38.2 all-gather.4
  50.0 36.6 all-gather.6

commit v3 on v2

v3 whole, which is shorter than its diff:
```python
import functools

import jax
import jax.numpy as jnp
from jax import lax
from jax.experimental import pallas as pl
from jax.experimental.pallas import tpu as pltpu
from jax.sharding import Mesh, PartitionSpec as P

BF = jnp.bfloat16
F32 = jnp.float32
GROUP = 8
VMEM = pl.BlockSpec(memory_space=pltpu.VMEM)
SMEM = pl.BlockSpec(memory_space=pltpu.SMEM)
HBM = pl.BlockSpec(memory_space=pltpu.HBM)
PARAMS = pltpu.CompilerParams(vmem_limit_bytes=8 * 1024 * 1024)
NT = (((1,), (1,)), ((), ()))
NN = (((1,), (0,)), ((), ()))


def mul_t(a, b):
    return lax.dot_general(a, b, NT, preferred_element_type=F32)


def mul(a, b):
    return lax.dot_general(a, b, NN, preferred_element_type=F32)


def call(body, outs, *args, specs=None, outs_at=VMEM, scratch=()):
    specs = [VMEM] * len(args) if specs is None else specs
    args = [far(x) if spec is HBM else x for x, spec in zip(args, specs)]
    return pl.pallas_call(
        body,
        out_shape=tuple(outs) if isinstance(outs, list) else outs,
        in_specs=specs,
        out_specs=outs_at if isinstance(outs_at, list) else jax.tree.map(lambda _: outs_at, outs),
        scratch_shapes=list(scratch),
        compiler_params=PARAMS,
    )(*args)


def far(x):
    return pltpu.with_memory_space_constraint(x, pltpu.HBM)


def sds(*shape, dtype=BF):
    return jax.ShapeDtypeStruct(shape, dtype)


def leaf_place():
    z = lax.axis_index("z")
    lane = lax.axis_index("x") * lax.axis_size("core") + lax.axis_index("core")
    return z, lane, z * GROUP + lane


def order(k, panels):
    return lax.rem(lax.axis_index("panel") + panels - k, panels)


def pack_body(rhs, coupling, *outs):
    panels = len(outs) + 1
    quarter = rhs.shape[-1]
    for k, out in enumerate(outs, 1):
        target = lax.rem(lax.axis_index("panel") + k, panels)
        put_halves(out, rhs[0, 0])
        start = pl.multiple_of(target * quarter, quarter)
        out[2 * rhs.shape[2] :] = coupling[0, 0, pl.ds(start, quarter), :]


def fold_coupling_body(coupling, out):
    width = coupling.shape[-1]
    rows = out.shape[0]
    for part in range(out.shape[1] // width):
        out[:, part * width : (part + 1) * width] = coupling[
            1, 0, part * rows : (part + 1) * rows, :
        ]


def last_weights_body(coupling, inv, *refs):
    *outs, sems = refs
    rows = inv.shape[2]
    width = coupling.shape[-1]
    parts = len(outs)
    copies = []
    for k, out in enumerate(outs):
        target = lax.rem(lax.axis_index("panel") + k, parts)
        for part in range(parts):
            source = coupling.at[0, 0, pl.ds(part * rows, rows)]
            copies.append((source, out.at[:, pl.ds(part * width, width)]))
        cols = pl.ds(pl.multiple_of(target * rows, rows), rows)
        copies.append((inv.at[0, 0, :, cols], out.at[:, pl.ds(parts * width, rows)]))
    copies = [pltpu.make_async_copy(a, b, sems.at[i]) for i, (a, b) in enumerate(copies)]
    for copy in copies:
        copy.start()
    for copy in copies:
        copy.wait()


def put_halves(out, value):
    rows = value.shape[0]
    out[:rows] = value[:, :128]
    out[rows : 2 * rows] = value[:, 128:]


def first_body(rhs, coupling, m1, m2, m3, inv, send):
    panels = send.shape[0]
    rows, quarter = rhs.shape[2:]
    total = None
    for k, ref in enumerate((rhs, m1, m2, m3)):
        q = order(k, panels)
        block = rhs[0, 0] if k == 0 else jnp.concatenate([ref[:rows], ref[rows : 2 * rows]], axis=1)
        part = mul_t(block, inv[:, pl.ds(pl.multiple_of(q * quarter, quarter), quarter)])
        total = part if total is None else total + part
    f = total.astype(BF)
    few = rows // panels
    own = pl.multiple_of(lax.axis_index("panel") * quarter, quarter)
    for k, ref in enumerate((coupling, m1, m2, m3)):
        q = order(k, panels)
        part = mul(f, coupling[0, 0, pl.ds(own, quarter), :] if k == 0 else ref[2 * rows :])
        high = part.astype(BF)
        low = (part - high.astype(F32)).astype(BF)
        for d in range(panels):
            send[d, q] = high[d * few : (d + 1) * few]
            send[d, panels + q] = low[d * few : (d + 1) * few]
    for d in range(panels):
        span = slice(d * few, (d + 1) * few)
        for index, value in enumerate((f[span], rhs[1, 0, span], rhs[2, 0, span])):
            send[d, 2 * panels + 2 * index] = value[:, :128]
            send[d, 2 * panels + 2 * index + 1] = value[:, 128:]


def place(level, counts, lists, rows):
    _, _, leaf = leaf_place()
    mine = lists[level, pl.ds(leaf, 1), :]
    shape = (rows, lists.shape[-1])
    row = lax.broadcasted_iota(jnp.int32, shape, 0)
    col = lax.broadcasted_iota(jnp.int32, shape, 1)
    return jnp.where((row == mine) & (col < counts[level, leaf]), 1.0, 0.0).astype(BF)


def place_body(level, counts, lists, out):
    out[...] = place(level, counts, lists, out.shape[0])


def laid_out(level, u, placed, counts):
    _, _, leaf = leaf_place()
    col = lax.broadcasted_iota(jnp.int32, u.shape, 1)
    u = jnp.where(col < counts[level, leaf], u, 0.0).astype(BF)
    return mul_t(u, placed).astype(BF)


def whole(got, index):
    panels = got.shape[0]
    first = 2 * panels + 2 * index
    return jnp.concatenate(
        [got[q, first + half] for q in range(panels) for half in range(2)], axis=1
    )


def up0_body(counts, got, placed, out):
    panels = got.shape[0]
    pieces = []
    for q in range(panels):
        total = None
        for source in range(panels):
            part = got[source, q].astype(F32) + got[source, panels + q].astype(F32)
            total = part if total is None else total + part
        pieces.append(total)
    e = laid_out(0, jnp.concatenate(pieces, axis=1), placed[...], counts)
    for d in range(out.shape[0]):
        out[d] = e


def summed(recv):
    total = recv[0].astype(F32)
    for j in range(1, recv.shape[0]):
        total = total + recv[j].astype(F32)
    return total


def forward(resid, blocks, out):
    rows, cols = blocks[0].shape[0], out.shape[1]
    for k, ref in enumerate(blocks):
        start = pl.multiple_of(order(k, len(blocks)) * rows, rows)
        out[:, pl.ds(start, rows)] = mul_t(resid, ref[:, :cols]).astype(BF)
    return out[...]


def backward(reduced, blocks):
    rows, cols = blocks[0].shape[0], reduced.shape[1]
    total = None
    for k, ref in enumerate(blocks):
        start = pl.multiple_of(order(k, len(blocks)) * rows, rows)
        part = mul(reduced[:, pl.ds(start, rows)], ref[:, :cols])
        total = part if total is None else total + part
    return total.astype(BF)


def coupled(f, blocks, first, out):
    rows = blocks[0].shape[0]
    parts = f.shape[1] // rows
    width = out.shape[1] // len(blocks)
    for k, ref in enumerate(blocks):
        total = None
        for part in range(parts):
            lanes = slice(first + part * width, first + (part + 1) * width)
            term = mul(f[:, part * rows : (part + 1) * rows], ref[:, lanes])
            total = term if total is None else total + term
        out[:, pl.ds(pl.multiple_of(order(k, len(blocks)) * width, width), width)] = total


def lessened(level, f, recv, parents, placed, blocks, first, picked):
    _, _, leaf = leaf_place()
    above = recv[lax.rem(parents[level, leaf], GROUP)]
    picked[...] = mul(above, placed).astype(BF)
    rows = blocks[0].shape[0]
    width = picked.shape[1] // len(blocks)
    pieces = []
    for part in range(f.shape[1] // rows):
        lanes = slice(first + part * width, first + (part + 1) * width)
        total = None
        for k, ref in enumerate(blocks):
            start = pl.multiple_of(order(k, len(blocks)) * width, width)
            term = mul_t(picked[:, pl.ds(start, width)], ref[:, lanes])
            total = term if total is None else total + term
        pieces.append(total)
    return (f.astype(F32) - jnp.concatenate(pieces, axis=1)).astype(BF)


def to_all(out, value):
    for d in range(out.shape[0]):
        out[d] = value


def up1_body(counts, recv, got, lists, i0, i1, i2, i3, c0, c1, c2, c3, fout, out, keep, scratch, sems):
    inverse, blocks = (i0, i1, i2, i3), (c0, c1, c2, c3)
    cols = i0.shape[1]
    copies = []
    for k in range(len(blocks)):
        for part, (source, span) in enumerate(
            ((inverse[k], pl.ds(0, cols)), (blocks[k], pl.ds(cols, c0.shape[1])))
        ):
            copies.append(pltpu.make_async_copy(source, keep.at[k, :, span], sems.at[k, part]))
    for copy in copies:
        copy.start()
    resid = (whole(got, 1).astype(F32) - summed(recv)).astype(BF)
    placed = place(1, counts, lists, fout.shape[1])
    f = forward(resid, inverse, fout)
    coupled(f, blocks, 0, scratch)
    to_all(out, laid_out(1, scratch[...], placed, counts))
    for copy in copies:
        copy.wait()


def top_body(recv, got, i0, i1, i2, i3, fout, out):
    resid = (whole(got, 2).astype(F32) - summed(recv)).astype(BF)
    blocks = (i0, i1, i2, i3)
    forward(resid, blocks, fout)
    to_all(out, backward(fout, blocks))


def fold_body(level, parents, blocks, out, acc):
    z, lane, _ = leaf_place()
    acc[...] = jnp.zeros_like(acc)
    for j in range(blocks.shape[0]):
        parent = parents[level, j * GROUP + lane]
        d = jnp.where(lax.div(parent, GROUP) == z, lax.rem(parent, GROUP), GROUP)
        acc[d] = acc[d] + blocks[j].astype(F32)
    for d in range(out.shape[0]):
        out[d] = acc[d].astype(BF)


def route_body(level, parents, blocks, out):
    z, _, _ = leaf_place()
    for d in range(out.shape[0]):
        out[d] = blocks[lax.div(parents[level, z * GROUP + d], GROUP)]


def down1_body(parents, counts, recv, f, lists, keep, out, picked, red):
    blocks = [keep.at[k] for k in range(keep.shape[0])]
    placed = place(1, counts, lists, red.shape[1])
    red[...] = lessened(1, f[...], recv, parents, placed, blocks, red.shape[1], picked)
    to_all(out, backward(red, blocks))


def down0_body(
    parents, counts, recv, got, lists, b0, b1, b2, b3, f1, f2, s2, s1,
    o0, o1, o2, o3, scratch, f0,
):
    outs = (o0, o1, o2, o3)
    width = f1.shape[1]
    quarter = width // len(outs)
    f0[...] = whole(got, 0)
    placed = place(0, counts, lists, width)
    red = lessened(0, f0[...], recv, parents, placed, (b0, b1, b2, b3), 0, scratch)
    for k, out in enumerate(outs):
        target = lax.rem(lax.axis_index("panel") + k, len(outs))
        cols = pl.ds(pl.multiple_of(target * quarter, quarter), quarter)
        out[:, :width] = red
        for index, value in enumerate(
            (f0[:, cols], f1[:, cols], f2[:, cols], s2[0, :, cols], s1[0, :, cols])
        ):
            out[:, width + index * quarter : width + (index + 1) * quarter] = value


def last_body(*refs):
    panels = (len(refs) - 3) // 2
    ends, cols = refs[:panels], refs[panels : 2 * panels]
    fwd, sol, reds = refs[2 * panels :]
    width = reds.shape[1]
    quarter = width // panels
    rows = ends[0].shape[0]
    for k in range(panels):
        q = order(k, panels)
        span = pl.ds(pl.multiple_of(q * rows, rows), rows)
        reds[span] = ends[k][:, :width]
        for index, (out, level) in enumerate(
            ((fwd, 0), (fwd, 1), (fwd, 2), (sol, 2), (sol, 1))
        ):
            out[level, 0, span] = ends[k][:, width + index * quarter : width + (index + 1) * quarter]
    total = None
    for k in range(panels):
        q = order(k, panels)
        part = mul(
            reds[:, pl.ds(pl.multiple_of(q * quarter, quarter), quarter)], cols[k][:, -quarter:]
        )
        total = part if total is None else total + part
    sol[0, 0] = total.astype(BF)


def local(rhs, inv_diag, coupling, row_lists, parents, counts):
    panels = lax.axis_size("panel")
    rows = rhs.shape[2] // panels
    mid = (GROUP, rows, inv_diag.shape[3])
    after = lax.optimization_barrier

    def shifted(x, k):
        return lax.ppermute(x, "panel", [(i, (i + k) % panels) for i in range(panels)])

    def placement(level, counts):
        return call(
            functools.partial(place_body, level),
            sds(inv_diag.shape[3], row_lists.shape[2]),
            counts, row_lists,
            specs=[SMEM, VMEM],
        )

    half = coupling.shape[3]
    tall = rhs.shape[3]
    half = coupling.shape[3]
    tall = rhs.shape[3]
    width = inv_diag.shape[3]

    def exchange(x, axes, weights=(), shifts=()):
        x, *weights = after((x, *weights))
        moved = [shifted(w, k) for w, k in zip(weights, shifts)]
        x = lax.all_to_all(x, axes, 0, 0)
        return after((x, *moved))

    packs = call(
        pack_body, [sds(2 * rhs.shape[2] + tall, half)] * (panels - 1), rhs, coupling,
    )
    packs = [shifted(x, k) for k, x in enumerate(packs, 1)]
    base = inv_diag[0, 0]
    placed0 = placement(0, counts)
    c1 = call(fold_coupling_body, sds(tall, panels * half), coupling)
    in1, in2 = inv_diag[1, 0], inv_diag[2, 0]
    base, placed0, c1, in1, in2 = after((base, placed0, c1, in1, in2))
    send = call(
        first_body, sds(panels, 14, rows, half), rhs, coupling, *packs, base,
    )
    got, c11, c13 = exchange(send, "panel", [c1, c1], [1, 3])
    touched = pltpu.VMEM((rows, panels * half), BF)
    wide = pltpu.VMEM((rows, panels * half), F32)
    e = call(up0_body, sds(*mid), counts, got, placed0, specs=[SMEM] + [VMEM] * 2)

    def fold(e, level, table):
        return call(
            functools.partial(fold_body, level), sds(*mid), table, e,
            specs=[SMEM, VMEM], scratch=[pltpu.VMEM((GROUP + 1, *mid[1:]), F32)],
        )

    def route(s, level, table):
        return call(functools.partial(route_body, level), sds(*mid), table, s, specs=[SMEM, VMEM])

    e, in11, in13, c12 = exchange(e, "z", [in1, in1, c1], [1, 3, 2])
    e = fold(e, 0, parents)
    e, in12 = exchange(e, ("x", "core"), [in1], [2])
    level1 = (in1, in11, in12, in13, c1, c11, c12, c13)
    f1, e, keep = call(
        up1_body, [sds(*mid[1:]), sds(*mid), sds(panels, tall, width + panels * half)],
        counts, e, got, row_lists, *level1,
        specs=[SMEM] + [VMEM] * 11, outs_at=[VMEM, VMEM, HBM],
        scratch=[wide, pltpu.SemaphoreType.DMA((panels, 2))],
    )
    e, in21, in23 = exchange(e, "z", [in2, in2], [1, 3])
    e = fold(e, 1, parents)
    e, in22 = exchange(e, ("x", "core"), [in2], [2])
    f2, s2 = call(
        top_body, (sds(*mid[1:]), sds(*mid)), e, got, in2, in21, in22, in23
    )
    s, inv_late, near_coupling = after((s2, inv_diag, coupling))
    w0 = call(
        last_weights_body, [sds(tall, panels * half + tall)] * panels, near_coupling, inv_late,
        specs=[HBM] * 2, outs_at=HBM,
        scratch=[pltpu.SemaphoreType.DMA((panels * (panels + 1),))],
    )
    s = lax.all_to_all(s, "z", 0, 0)
    s, *w0 = after((s, *w0))
    s = route(s, 1, parents)
    s, w01, w03 = exchange(s, ("x", "core"), [w0[1], w0[3]], [1, 3])
    s1 = call(
        down1_body, sds(*mid), parents, counts, s, f1, row_lists, keep,
        specs=[SMEM] * 2 + [VMEM] * 4, scratch=[touched, pltpu.VMEM(mid[1:], BF)],
    )
    s, far2 = after((s1, w0[2]))
    w02 = shifted(far2, 2)
    s = lax.all_to_all(s, "z", 0, 0)
    w0 = (w0[0], w01, w02, w03)
    s = route(s, 0, parents)
    s = lax.all_to_all(s, ("x", "core"), 0, 0)
    ends = call(
        down0_body, [sds(rows, mid[2] + 5 * tall)] * panels,
        parents, counts, s, got, row_lists, *w0, f1, f2, s2, s1,
        specs=[SMEM] * 2 + [VMEM] * 11, scratch=[touched, pltpu.VMEM(mid[1:], BF)],
    )
    ends = [ends[0]] + [shifted(x, k) for k, x in enumerate(ends[1:], 1)]
    return call(
        last_body, (sds(*rhs.shape), sds(*rhs.shape)), *ends, *w0,
        scratch=[pltpu.VMEM((rhs.shape[2], mid[2]), BF)],
    )


def solution(mesh):
    leaves, panels = mesh.shape["leaf"], mesh.shape["panel"]
    inner = Mesh(
        mesh.devices.reshape(leaves // GROUP, GROUP // 2, 2, panels), ("z", "x", "core", "panel")
    )
    leaf = ("z", "x", "core")
    placed = (
        P(None, leaf, None, "panel"),
        P(None, leaf, "panel", None),
        P(None, leaf, None, "panel"),
        P(),
        P(),
        P(),
    )
    return jax.shard_map(
        local,
        mesh=inner,
        in_specs=placed,
        out_specs=(P(None, leaf, None, "panel"), P(None, leaf, None, "panel")),
        check_vma=False,
    )
```

time: 178 us -> 171 us (0.961)
  blocking collectives: 24.1 us -> 57.9 us
  between operations: 14.3 us -> 0.83 us
  waiting for transfers between devices: 58.2 us -> 45.3 us
  starting transfers between devices: 50.9 us -> 40.9 us
  local copies, waits for them, and re-layouts: 10.5 us -> 7.99 us
    all_to_all x5 -> x1, waiting for transfers between devices: 37.2 us -> 0.96 us  [exchange(): x = lax.all_to_all(x, axes, 0, 0)]
    all_to_all x2 -> x5, blocking collectives: 24.1 us -> 57.9 us  [exchange(): x = lax.all_to_all(x, axes, 0, 0)]
    all_to_all x5 -> x1, starting transfers between devices: 23.9 us -> 8.08 us  [exchange(): x = lax.all_to_all(x, axes, 0, 0)]
    all_to_all x1 -> x2, waiting for transfers between devices: 6.82 us -> 20.4 us  [local(): s = lax.all_to_all(s, 'z', 0, 0)]
    ppermute x9 -> x18, starting transfers between devices: 10.5 us -> 22.1 us  [shifted(): lax.ppermute(x, 'panel', [(i, (i + k) % panels) for i in range(panels)])]
    ppermute x6 -> x0, starting transfers between devices: 9.63 us -> none  [spread(): lax.ppermute(x, 'panel', [(i, (i + k) % panels) for i in range(panels)])]
    ppermute x9 -> x18, waiting for transfers between devices: 11.1 us -> 16.5 us  [shifted(): lax.ppermute(x, 'panel', [(i, (i + k) % panels) for i in range(panels)])]
    all_to_all x1, waiting for transfers between devices: 2.9 us -> 7.45 us  [local(): s = lax.all_to_all(s, ('x', 'core'), 0, 0)]
  transfers between devices with their start and end apart: 24 -> 22, of which waited for: 13 -> 11; matrix products, arithmetic and copies ran while one was open for 0% -> 1% of each run, Pallas kernels for 7% -> 2%
where the time goes in v3:
time: 171 us; the launch traced here: 170 us
  blocking collectives  57.9 us (34%)
  waiting for transfers between devices  45.3 us (26%)
  starting transfers between devices  40.9 us (24%)
  Pallas kernels  16.9 us (10%)
  local copies, waits for them, and re-layouts  7.99 us (5%)
    all_to_all x5, blocking collectives, exchange(): x = lax.all_to_all(x, axes, 0, 0)  57.9 us
    ppermute x18, starting transfers between devices, shifted(): lax.ppermute(x, 'panel', [(i, (i + k) % panels) for i in range(panels)])  22.1 us
    all_to_all x2, waiting for transfers between devices, local(): s = lax.all_to_all(s, 'z', 0, 0)  20.4 us
    pallas_call x15, Pallas kernels, call(): pl.pallas_call(body, out_shape=tuple(outs) if isinstance(outs, list) else...  16.9 us
    ppermute x18, waiting for transfers between devices, shifted(): lax.ppermute(x, 'panel', [(i, (i + k) % panels) for i in range(panels)])  16.5 us
    all_to_all x1, starting transfers between devices, exchange(): x = lax.all_to_all(x, axes, 0, 0)  8.08 us
    all_to_all x1, waiting for transfers between devices, local(): s = lax.all_to_all(s, ('x', 'core'), 0, 0)  7.45 us
    all_to_all x2, starting transfers between devices, local(): s = lax.all_to_all(s, 'z', 0, 0)  7.26 us
  transfers between devices with their start and end apart: 22, of which 11 were waited for; matrix products, arithmetic and copies ran while one was open for 1% of the time, Pallas kernels for 2%

profile of v3, /device:TPU:24, one launch (start us, length us, event | category | flops | bytes accessed | tf_op | source)
XLA Modules:
  0.0 169.8 jit_solution(7875013761558369817)
XLA Ops:
  2.6 2.0 %collective-permute-start = (bf16[384,128]{1,0:T(8,128)(2,1)S(1)}, bf16[384,128]{1,0:T(8,128)(2,1)S(1)}, u32[]{:S(2)}, u32[]{:S(2)}) collective-permute-start(bf16[384,128]{1,0:T(8,128)(2,1)S(1)} %get-tuple-element.67), channel_id=1, source_target_pairs={{0,1},{1,2},{2,3},{3,0},{4,5},{5,6},{6,7},{7,4},{8,9},{9,10},{10,1... | collective-permute-start | bytes 294920 | tf_op jit(solution)/shard_map/ppermute | solution.py:338
  5.6 1.5 slice_bitcast_fusion
  8.3 2.6 %collective-permute-done.1.m2 = bf16[384,128]{1,0:T(8,128)(2,1)S(1)} collective-permute-done((bf16[384,128]{1,0:T(8,128)(2,1)S(1)}, bf16[384,128]{1,0:T(8,128)(2,1)S(1)}, u32[]{:S(2)}, u32[]{:S(2)}) %collective-permute-start.1) | collective-permute-done | bytes 98336 | tf_op jit(solution)/shard_map/ppermute | solution.py:338
  13.0 1.5 collective-permute-start.4
  14.5 8.7 %all_to_all.45.got = bf16[4,14,16,128]{3,2,1,0:T(8,128)(2,1)S(1)} all-to-all(bf16[4,14,16,128]{3,2,1,0:T(8,128)(2,1)S(1)} %shard_map.80), channel_id=1, replica_groups=mesh['z'=8,'x'=4,'core'=2,'panel'=4] {'panel'}, dimensions={0} | all-to-all | bytes 458752 | tf_op jit(solution)/shard_map/all_to_all | solution.py:357
  23.2 1.7 shard_map.81
  24.9 2.1 %collective-permute-start.5 = (bf16[256,1024]{1,0:T(8,128)(2,1)S(1)}, bf16[256,1024]{1,0:T(8,128)(2,1)S(1)}, u32[]{:S(2)}, u32[]{:S(2)}) collective-permute-start(bf16[256,1024]{1,0:T(8,128)(2,1)S(1)} %get-tuple-element.84.i0), channel_id=1, source_target_pairs={{0,1},{1,2},{2,3},{3,0},{4,5},{5,6},{6,7},{7,4},{8,9},{9,10},{10,1... | collective-permute-start | bytes 1572872 | tf_op jit(solution)/shard_map/ppermute | solution.py:338
  27.0 8.1 %all-to-all-start.1 = ((bf16[8,16,1024]{2,1,0:T(8,128)(2,1)}), bf16[8,16,1024]{2,1,0:T(8,128)(2,1)S(1)}, u32[]{:S(2)}, u32[]{:S(2)}) async-start(bf16[8,16,1024]{2,1,0:T(8,128)(2,1)} %shard_map.81), calls=%async_computation.1 | async-start | bytes 524288 | tf_op jit(solution)/shard_map/all_to_all | solution.py:357
  35.1 1.9 %collective-permute-start.7 = (bf16[256,512]{1,0:T(8,128)(2,1)S(1)}, bf16[256,512]{1,0:T(8,128)(2,1)S(1)}, u32[]{:S(2)}, u32[]{:S(2)}) collective-permute-start(bf16[256,512]{1,0:T(8,128)(2,1)S(1)} %shard_map.79.c0), channel_id=1, source_target_pairs={{0,2},{1,3},{2,0},{3,1},{4,6},{5,7},{6,4},{7,5},{8,10},{9,11},{10,... | collective-permute-start | bytes 786440 | tf_op jit(solution)/shard_map/ppermute | solution.py:338
  36.9 6.9 %collective-permute-done.7.c2 = bf16[256,512]{1,0:T(8,128)(2,1)S(1)} collective-permute-done((bf16[256,512]{1,0:T(8,128)(2,1)S(1)}, bf16[256,512]{1,0:T(8,128)(2,1)S(1)}, u32[]{:S(2)}, u32[]{:S(2)}) %collective-permute-start.7) | collective-permute-done | bytes 262176 | tf_op jit(solution)/shard_map/ppermute | solution.py:338
  46.2 2.0 %collective-permute-start.8 = (bf16[256,1024]{1,0:T(8,128)(2,1)S(1)}, bf16[256,1024]{1,0:T(8,128)(2,1)S(1)}, u32[]{:S(2)}, u32[]{:S(2)}) collective-permute-start(bf16[256,1024]{1,0:T(8,128)(2,1)S(1)} %get-tuple-element.84.i0), channel_id=1, source_target_pairs={{0,2},{1,3},{2,0},{3,1},{4,6},{5,7},{6,4},{7,5},{8,10},{9,11},{10,... | collective-permute-start | bytes 1572872 | tf_op jit(solution)/shard_map/ppermute | solution.py:338
  48.2 11.6 %all_to_all.46.recv = bf16[8,16,1024]{2,1,0:T(8,128)(2,1)S(1)} all-to-all(bf16[8,16,1024]{2,1,0:T(8,128)(2,1)S(1)} %shard_map.82), channel_id=1, replica_groups=mesh['z'=8,'x'=4,'core'=2,'panel'=4] {'x','core'}, dimensions={0} | all-to-all | bytes 524288 | tf_op jit(solution)/shard_map/all_to_all | solution.py:357
  61.8 2.1 %shard_map.83 = (bf16[16,1024]{1,0:T(8,128)(2,1)S(1)}, bf16[8,16,1024]{2,1,0:T(8,128)(2,1)S(1)}, bf16[4,256,1536]{2,1,0:T(8,128)(2,1)S(1)}) custom-call(s32[2,64]{1,0:T(2,128)S(1)} %copy-done.12, bf16[8,16,1024]{2,1,0:T(8,128)(2,1)S(1)} %all_to_all.46.recv, bf16[4,14,16,128]{3,2,1,0:T(8,128)(2,1)S(1)} %all_to_all.45.got, s32[2,64,512]{2,1,0:T(8,128)S(1)} %copy-done.2, ...), custom_call_target="tpu_custom_call" | custom-call | tf_op jit(solution)/shard_map/pallas_call | solution.py:32
  63.9 1.3 collective-permute-start.9
  66.1 17.6 %all_to_all.47.blocks = bf16[8,16,1024]{2,1,0:T(8,128)(2,1)S(1)} all-to-all(bf16[8,16,1024]{2,1,0:T(8,128)(2,1)S(1)} %get-tuple-element.94), channel_id=1, replica_groups=mesh['z'=8,'x'=4,'core'=2,'panel'=4] {'z'}, dimensions={0} | all-to-all | bytes 524288 | tf_op jit(solution)/shard_map/all_to_all | solution.py:357
  84.4 2.3 %collective-permute-start.11 = (bf16[256,1024]{1,0:T(8,128)(2,1)S(1)}, bf16[256,1024]{1,0:T(8,128)(2,1)S(1)}, u32[]{:S(2)}, u32[]{:S(2)}) collective-permute-start(bf16[256,1024]{1,0:T(8,128)(2,1)S(1)} %get-tuple-element.99.i0), channel_id=1, source_target_pairs={{0,2},{1,3},{2,0},{3,1},{4,6},{5,7},{6,4},{7,5},{8,10},{9,11},{10,... | collective-permute-start | bytes 1572872 | tf_op jit(solution)/shard_map/ppermute | solution.py:338
  86.7 10.1 %all_to_all.48.recv = bf16[8,16,1024]{2,1,0:T(8,128)(2,1)S(1)} all-to-all(bf16[8,16,1024]{2,1,0:T(8,128)(2,1)S(1)} %shard_map.84), channel_id=1, replica_groups=mesh['z'=8,'x'=4,'core'=2,'panel'=4] {'x','core'}, dimensions={0} | all-to-all | bytes 524288 | tf_op jit(solution)/shard_map/all_to_all | solution.py:357
  96.8 1.7 %shard_map.85 = (bf16[16,1024]{1,0:T(8,128)(2,1)S(1)}, bf16[8,16,1024]{2,1,0:T(8,128)(2,1)}) custom-call(bf16[8,16,1024]{2,1,0:T(8,128)(2,1)S(1)} %all_to_all.48.recv, bf16[4,14,16,128]{3,2,1,0:T(8,128)(2,1)S(1)} %all_to_all.45.got, bf16[256,1024]{1,0:T(8,128)(2,1)S(1)} %get-tuple-element.99.i0, bf16[256,1024]{1,0:T(8,128)(2,1)S(1)} %collective-permute-done.9.i1, ...), custom_call_target="tpu_custom_call" | custom-call | tf_op jit(solution)/shard_map/pallas_call | solution.py:32
  98.5 3.8 %all-to-all-start.5 = ((bf16[8,16,1024]{2,1,0:T(8,128)(2,1)}), bf16[8,16,1024]{2,1,0:T(8,128)(2,1)S(1)}, u32[]{:S(2)}, u32[]{:S(2)}) async-start(bf16[8,16,1024]{2,1,0:T(8,128)(2,1)} %get-tuple-element.105.s2), calls=%async_computation.5 | async-start | bytes 524288 | tf_op jit(solution)/shard_map/all_to_all | solution.py:408
  102.4 1.9 %shard_map.86 = (bf16[256,768]{1,0:T(8,128)(2,1)S(1)}, bf16[256,768]{1,0:T(8,128)(2,1)S(1)}, bf16[256,768]{1,0:T(8,128)(2,1)S(1)}, bf16[256,768]{1,0:T(8,128)(2,1)S(1)}) custom-call(bf16[2,1,1024,128]{3,2,1,0:T(8,128)(2,1)} %coupling.6, bf16[3,1,256,1024]{3,2,1,0:T(8,128)(2,1)} %inv), custom_call_target="tpu_custom_call" | custom-call | tf_op jit(solution)/shard_map/pallas_call | solution.py:32
  104.3 9.9 %all-to-all-done.5.blocks = bf16[8,16,1024]{2,1,0:T(8,128)(2,1)S(1)} async-done(((bf16[8,16,1024]{2,1,0:T(8,128)(2,1)}), bf16[8,16,1024]{2,1,0:T(8,128)(2,1)S(1)}, u32[]{:S(2)}, u32[]{:S(2)}) %all-to-all-start.5) | async-done | bytes 262176 | tf_op jit(solution)/shard_map/all_to_all | solution.py:408
  116.8 9.9 %all_to_all.49.recv = bf16[8,16,1024]{2,1,0:T(8,128)(2,1)S(1)} all-to-all(bf16[8,16,1024]{2,1,0:T(8,128)(2,1)S(1)} %shard_map.87), channel_id=1, replica_groups=mesh['z'=8,'x'=4,'core'=2,'panel'=4] {'x','core'}, dimensions={0} | all-to-all | bytes 524288 | tf_op jit(solution)/shard_map/all_to_all | solution.py:357
  126.8 1.9 %copy-done.4 = bf16[4,256,1536]{2,1,0:T(8,128)(2,1)S(1)} copy-done((bf16[4,256,1536]{2,1,0:T(8,128)(2,1)S(1)}, bf16[4,256,1536]{2,1,0:T(8,128)(2,1)}, u32[]{:S(2)}) %copy-start.4) | copy-done | bytes 3145752
  128.7 2.4 %shard_map.88.s1 = bf16[8,16,1024]{2,1,0:T(8,128)(2,1)} custom-call(s32[2,64]{1,0:T(2,128)S(1)} %copy-done.11, s32[2,64]{1,0:T(2,128)S(1)} %copy-done.12, bf16[8,16,1024]{2,1,0:T(8,128)(2,1)S(1)} %all_to_all.49.recv, bf16[16,1024]{1,0:T(8,128)(2,1)S(1)} %get-tuple-element.119.f.f1, s32[2,64,512]{2,1,0:T(8,128)S(1)} %copy-done.2, ...), custom_call_target="tpu_custom_call" | custom-call | tf_op jit(solution)/shard_map/pallas_call | solution.py:32
  131.0 3.4 %all-to-all-start.7 = ((bf16[8,16,1024]{2,1,0:T(8,128)(2,1)}), bf16[8,16,1024]{2,1,0:T(8,128)(2,1)S(1)}, u32[]{:S(2)}, u32[]{:S(2)}) async-start(bf16[8,16,1024]{2,1,0:T(8,128)(2,1)} %shard_map.88.s1), calls=%async_computation.7 | async-start | bytes 524288 | tf_op jit(solution)/shard_map/all_to_all | solution.py:418
  135.6 10.5 %all-to-all-done.7.blocks = bf16[8,16,1024]{2,1,0:T(8,128)(2,1)S(1)} async-done(((bf16[8,16,1024]{2,1,0:T(8,128)(2,1)}), bf16[8,16,1024]{2,1,0:T(8,128)(2,1)S(1)}, u32[]{:S(2)}, u32[]{:S(2)}) %all-to-all-start.7) | async-done | bytes 262176 | tf_op jit(solution)/shard_map/all_to_all | solution.py:418
  147.5 3.4 %all-to-all-start.8 = ((bf16[8,16,1024]{2,1,0:T(8,128)(2,1)}), bf16[8,16,1024]{2,1,0:T(8,128)(2,1)S(1)}, u32[]{:S(2)}, u32[]{:S(2)}) async-start(bf16[8,16,1024]{2,1,0:T(8,128)(2,1)} %shard_map.89), calls=%async_computation.8 | async-start | bytes 524288 | tf_op jit(solution)/shard_map/all_to_all | solution.py:421
  150.9 7.4 %all-to-all-done.8.recv = bf16[8,16,1024]{2,1,0:T(8,128)(2,1)S(1)} async-done(((bf16[8,16,1024]{2,1,0:T(8,128)(2,1)}), bf16[8,16,1024]{2,1,0:T(8,128)(2,1)S(1)}, u32[]{:S(2)}, u32[]{:S(2)}) %all-to-all-start.8) | async-done | bytes 262176 | tf_op jit(solution)/shard_map/all_to_all | solution.py:421
  158.3 1.7 shard_map.90
  160.0 2.2 %collective-permute-start.15 = (bf16[16,2304]{1,0:T(8,128)(2,1)S(1)}, bf16[16,2304]{1,0:T(8,128)(2,1)S(1)}, u32[]{:S(2)}, u32[]{:S(2)}) collective-permute-start(bf16[16,2304]{1,0:T(8,128)(2,1)S(1)} %get-tuple-element.129), channel_id=1, source_target_pairs={{0,1},{1,2},{2,3},{3,0},{4,5},{5,6},{6,7},{7,4},{8,9},{9,10},{10,1... | collective-permute-start | bytes 221192 | tf_op jit(solution)/shard_map/ppermute | solution.py:338
  163.2 1.8 %collective-permute-done.15.refs_1_ = bf16[16,2304]{1,0:T(8,128)(2,1)S(1)} collective-permute-done((bf16[16,2304]{1,0:T(8,128)(2,1)S(1)}, bf16[16,2304]{1,0:T(8,128)(2,1)S(1)}, u32[]{:S(2)}, u32[]{:S(2)}) %collective-permute-start.15) | collective-permute-done | bytes 73760 | tf_op jit(solution)/shard_map/ppermute | solution.py:338
  165.0 3.1 %collective-permute-done.16.refs_2_ = bf16[16,2304]{1,0:T(8,128)(2,1)S(1)} collective-permute-done((bf16[16,2304]{1,0:T(8,128)(2,1)S(1)}, bf16[16,2304]{1,0:T(8,128)(2,1)S(1)}, u32[]{:S(2)}, u32[]{:S(2)}) %collective-permute-start.16) | collective-permute-done | bytes 73760 | tf_op jit(solution)/shard_map/ppermute | solution.py:338
  (59 shorter events, 19.8 us)
Async XLA Ops:
  0.6 1.0 copy-start
  2.6 5.7 %collective-permute-start = (bf16[384,128]{1,0:T(8,128)(2,1)S(1)}, bf16[384,128]{1,0:T(8,128)(2,1)S(1)}, u32[]{:S(2)}, u32[]{:S(2)}) collective-permute-start(bf16[384,128]{1,0:T(8,128)(2,1)S(1)} %get-tuple-element.67), channel_id=1, source_target_pairs={{0,1},{1,2},{2,3},{3,0},{4,5},{5,6},{6,7},{7,4},{8,9},{9,10},{10,1... | collective-permute-start | bytes 294920 | tf_op jit(solution)/shard_map/ppermute | solution.py:338
  4.6 6.2 %collective-permute-start.1 = (bf16[384,128]{1,0:T(8,128)(2,1)S(1)}, bf16[384,128]{1,0:T(8,128)(2,1)S(1)}, u32[]{:S(2)}, u32[]{:S(2)}) collective-permute-start(bf16[384,128]{1,0:T(8,128)(2,1)S(1)} %get-tuple-element.68), channel_id=1, source_target_pairs={{0,2},{1,3},{2,0},{3,1},{4,6},{5,7},{6,4},{7,5},{8,10},{9,11},{10,... | collective-permute-start | bytes 294920 | tf_op jit(solution)/shard_map/ppermute | solution.py:338
  5.5 1.6 copy-start.1
  5.5 1.7 %copy-start.2 = (s32[2,64,512]{2,1,0:T(8,128)S(1)}, s32[2,64,512]{2,1,0:T(8,128)}, u32[]{:S(2)}) copy-start(s32[2,64,512]{2,1,0:T(8,128)} %lists.7) | copy-start | bytes 786436
  5.5 1.7 %copy-start.12 = (s32[2,64]{1,0:T(2,128)S(1)}, s32[2,64]{1,0:T(2,128)}, u32[]{:S(2)}) copy-start(s32[2,64]{1,0:T(2,128)} %counts.9) | copy-start | bytes 1540
  5.5 6.4 %collective-permute-start.2 = (bf16[384,128]{1,0:T(8,128)(2,1)S(1)}, bf16[384,128]{1,0:T(8,128)(2,1)S(1)}, u32[]{:S(2)}, u32[]{:S(2)}) collective-permute-start(bf16[384,128]{1,0:T(8,128)(2,1)S(1)} %get-tuple-element.69), channel_id=1, source_target_pairs={{0,3},{1,0},{2,1},{3,2},{4,7},{5,4},{6,5},{7,6},{8,11},{9,8},{10,9... | collective-permute-start | bytes 294920 | tf_op jit(solution)/shard_map/ppermute | solution.py:338
  7.1 4.7 %copy-start.6 = (bf16[3,1,64,256]{3,2,1,0:T(8,128)(2,1)S(1)}, bf16[3,1,64,256]{3,2,1,0:T(8,128)(2,1)}, u32[]{:S(2)}) copy-start(bf16[3,1,64,256]{3,2,1,0:T(8,128)(2,1)} %rhs.3) | copy-start | bytes 294916
  12.4 33.2 %copy-start.11 = (s32[2,64]{1,0:T(2,128)S(1)}, s32[2,64]{1,0:T(2,128)}, u32[]{:S(2)}) copy-start(s32[2,64]{1,0:T(2,128)} %parents.11) | copy-start | bytes 1540
  12.4 10.8 %collective-permute-start.3 = (bf16[256,512]{1,0:T(8,128)(2,1)S(1)}, bf16[256,512]{1,0:T(8,128)(2,1)S(1)}, u32[]{:S(2)}, u32[]{:S(2)}) collective-permute-start(bf16[256,512]{1,0:T(8,128)(2,1)S(1)} %shard_map.79.c0), channel_id=1, source_target_pairs={{0,1},{1,2},{2,3},{3,0},{4,5},{5,6},{6,7},{7,4},{8,9},{9,10},{10,1... | collective-permute-start | bytes 786440 | tf_op jit(solution)/shard_map/ppermute | solution.py:338
  13.0 10.2 %collective-permute-start.4 = (bf16[256,512]{1,0:T(8,128)(2,1)S(1)}, bf16[256,512]{1,0:T(8,128)(2,1)S(1)}, u32[]{:S(2)}, u32[]{:S(2)}) collective-permute-start(bf16[256,512]{1,0:T(8,128)(2,1)S(1)} %shard_map.79.c0), channel_id=1, source_target_pairs={{0,3},{1,0},{2,1},{3,2},{4,7},{5,4},{6,5},{7,6},{8,11},{9,8},{10,9... | collective-permute-start | bytes 786440 | tf_op jit(solution)/shard_map/ppermute | solution.py:338
  23.2 3.7 %copy-start.7 = (bf16[256,512]{1,0:T(8,128)(2,1)}, bf16[256,512]{1,0:T(8,128)(2,1)S(1)}, u32[]{:S(2)}) copy-start(bf16[256,512]{1,0:T(8,128)(2,1)S(1)} %collective-permute-done.4.c3) | copy-start | bytes 786436
  24.9 20.6 %collective-permute-start.5 = (bf16[256,1024]{1,0:T(8,128)(2,1)S(1)}, bf16[256,1024]{1,0:T(8,128)(2,1)S(1)}, u32[]{:S(2)}, u32[]{:S(2)}) collective-permute-start(bf16[256,1024]{1,0:T(8,128)(2,1)S(1)} %get-tuple-element.84.i0), channel_id=1, source_target_pairs={{0,1},{1,2},{2,3},{3,0},{4,5},{5,6},{6,7},{7,4},{8,9},{9,10},{10,1... | collective-permute-start | bytes 1572872 | tf_op jit(solution)/shard_map/ppermute | solution.py:338
  27.0 18.6 %collective-permute-start.6 = (bf16[256,1024]{1,0:T(8,128)(2,1)S(1)}, bf16[256,1024]{1,0:T(8,128)(2,1)S(1)}, u32[]{:S(2)}, u32[]{:S(2)}) collective-permute-start(bf16[256,1024]{1,0:T(8,128)(2,1)S(1)} %get-tuple-element.84.i0), channel_id=1, source_target_pairs={{0,3},{1,0},{2,1},{3,2},{4,7},{5,4},{6,5},{7,6},{8,11},{9,8},{10,9... | collective-permute-start | bytes 1572872 | tf_op jit(solution)/shard_map/ppermute | solution.py:338
  27.0 18.6 %all-to-all-start.1 = ((bf16[8,16,1024]{2,1,0:T(8,128)(2,1)}), bf16[8,16,1024]{2,1,0:T(8,128)(2,1)S(1)}, u32[]{:S(2)}, u32[]{:S(2)}) async-start(bf16[8,16,1024]{2,1,0:T(8,128)(2,1)} %shard_map.81), calls=%async_computation.1 | async-start | bytes 524288 | tf_op jit(solution)/shard_map/all_to_all | solution.py:357
  35.1 8.8 %collective-permute-start.7 = (bf16[256,512]{1,0:T(8,128)(2,1)S(1)}, bf16[256,512]{1,0:T(8,128)(2,1)S(1)}, u32[]{:S(2)}, u32[]{:S(2)}) collective-permute-start(bf16[256,512]{1,0:T(8,128)(2,1)S(1)} %shard_map.79.c0), channel_id=1, source_target_pairs={{0,2},{1,3},{2,0},{3,1},{4,6},{5,7},{6,4},{7,5},{8,10},{9,11},{10,... | collective-permute-start | bytes 786440 | tf_op jit(solution)/shard_map/ppermute | solution.py:338
  46.2 13.6 %collective-permute-start.8 = (bf16[256,1024]{1,0:T(8,128)(2,1)S(1)}, bf16[256,1024]{1,0:T(8,128)(2,1)S(1)}, u32[]{:S(2)}, u32[]{:S(2)}) collective-permute-start(bf16[256,1024]{1,0:T(8,128)(2,1)S(1)} %get-tuple-element.84.i0), channel_id=1, source_target_pairs={{0,2},{1,3},{2,0},{3,1},{4,6},{5,7},{6,4},{7,5},{8,10},{9,11},{10,... | collective-permute-start | bytes 1572872 | tf_op jit(solution)/shard_map/ppermute | solution.py:338
  59.8 1.0 copy-start.8
  63.9 34.7 %copy-start.3 = (bf16[4,256,1536]{2,1,0:T(8,128)(2,1)}, bf16[4,256,1536]{2,1,0:T(8,128)(2,1)S(1)}, u32[]{:S(2)}) copy-start(bf16[4,256,1536]{2,1,0:T(8,128)(2,1)S(1)} %get-tuple-element.120.keep) | copy-start | bytes 9437188
  63.9 19.8 %collective-permute-start.9 = (bf16[256,1024]{1,0:T(8,128)(2,1)S(1)}, bf16[256,1024]{1,0:T(8,128)(2,1)S(1)}, u32[]{:S(2)}, u32[]{:S(2)}) collective-permute-start(bf16[256,1024]{1,0:T(8,128)(2,1)S(1)} %get-tuple-element.99.i0), channel_id=1, source_target_pairs={{0,1},{1,2},{2,3},{3,0},{4,5},{5,6},{6,7},{7,4},{8,9},{9,10},{10,1... | collective-permute-start | bytes 1572872 | tf_op jit(solution)/shard_map/ppermute | solution.py:338
  65.2 18.5 %collective-permute-start.10 = (bf16[256,1024]{1,0:T(8,128)(2,1)S(1)}, bf16[256,1024]{1,0:T(8,128)(2,1)S(1)}, u32[]{:S(2)}, u32[]{:S(2)}) collective-permute-start(bf16[256,1024]{1,0:T(8,128)(2,1)S(1)} %get-tuple-element.99.i0), channel_id=1, source_target_pairs={{0,3},{1,0},{2,1},{3,2},{4,7},{5,4},{6,5},{7,6},{8,11},{9,8},{10,9... | collective-permute-start | bytes 1572872 | tf_op jit(solution)/shard_map/ppermute | solution.py:338
  84.4 12.4 %collective-permute-start.11 = (bf16[256,1024]{1,0:T(8,128)(2,1)S(1)}, bf16[256,1024]{1,0:T(8,128)(2,1)S(1)}, u32[]{:S(2)}, u32[]{:S(2)}) collective-permute-start(bf16[256,1024]{1,0:T(8,128)(2,1)S(1)} %get-tuple-element.99.i0), channel_id=1, source_target_pairs={{0,2},{1,3},{2,0},{3,1},{4,6},{5,7},{6,4},{7,5},{8,10},{9,11},{10,... | collective-permute-start | bytes 1572872 | tf_op jit(solution)/shard_map/ppermute | solution.py:338
  98.5 15.6 %all-to-all-start.5 = ((bf16[8,16,1024]{2,1,0:T(8,128)(2,1)}), bf16[8,16,1024]{2,1,0:T(8,128)(2,1)S(1)}, u32[]{:S(2)}, u32[]{:S(2)}) async-start(bf16[8,16,1024]{2,1,0:T(8,128)(2,1)} %get-tuple-element.105.s2), calls=%async_computation.5 | async-start | bytes 524288 | tf_op jit(solution)/shard_map/all_to_all | solution.py:408
  114.7 12.0 %collective-permute-start.12 = (bf16[256,768]{1,0:T(8,128)(2,1)S(1)}, bf16[256,768]{1,0:T(8,128)(2,1)S(1)}, u32[]{:S(2)}, u32[]{:S(2)}) collective-permute-start(bf16[256,768]{1,0:T(8,128)(2,1)S(1)} %get-tuple-element.116), channel_id=1, source_target_pairs={{0,1},{1,2},{2,3},{3,0},{4,5},{5,6},{6,7},{7,4},{8,9},{9,10},{10,1... | collective-permute-start | bytes 1179656 | tf_op jit(solution)/shard_map/ppermute | solution.py:338
  115.8 11.0 %collective-permute-start.13 = (bf16[256,768]{1,0:T(8,128)(2,1)S(1)}, bf16[256,768]{1,0:T(8,128)(2,1)S(1)}, u32[]{:S(2)}, u32[]{:S(2)}) collective-permute-start(bf16[256,768]{1,0:T(8,128)(2,1)S(1)} %get-tuple-element.117), channel_id=1, source_target_pairs={{0,3},{1,0},{2,1},{3,2},{4,7},{5,4},{6,5},{7,6},{8,11},{9,8},{10,9... | collective-permute-start | bytes 1179656 | tf_op jit(solution)/shard_map/ppermute | solution.py:338
  126.8 1.9 %copy-start.4 = (bf16[4,256,1536]{2,1,0:T(8,128)(2,1)S(1)}, bf16[4,256,1536]{2,1,0:T(8,128)(2,1)}, u32[]{:S(2)}) copy-start(bf16[4,256,1536]{2,1,0:T(8,128)(2,1)} %copy-done.3) | copy-start | bytes 9437188
  131.0 15.1 %all-to-all-start.7 = ((bf16[8,16,1024]{2,1,0:T(8,128)(2,1)}), bf16[8,16,1024]{2,1,0:T(8,128)(2,1)S(1)}, u32[]{:S(2)}, u32[]{:S(2)}) async-start(bf16[8,16,1024]{2,1,0:T(8,128)(2,1)} %shard_map.88.s1), calls=%async_computation.7 | async-start | bytes 524288 | tf_op jit(solution)/shard_map/all_to_all | solution.py:418
  134.5 16.4 %collective-permute-start.14 = (bf16[256,768]{1,0:T(8,128)(2,1)S(1)}, bf16[256,768]{1,0:T(8,128)(2,1)S(1)}, u32[]{:S(2)}, u32[]{:S(2)}) collective-permute-start(bf16[256,768]{1,0:T(8,128)(2,1)S(1)} %get-tuple-element.125), channel_id=1, source_target_pairs={{0,2},{1,3},{2,0},{3,1},{4,6},{5,7},{6,4},{7,5},{8,10},{9,11},{10,... | collective-permute-start | bytes 1179656 | tf_op jit(solution)/shard_map/ppermute | solution.py:338
  147.5 10.9 %all-to-all-start.8 = ((bf16[8,16,1024]{2,1,0:T(8,128)(2,1)}), bf16[8,16,1024]{2,1,0:T(8,128)(2,1)S(1)}, u32[]{:S(2)}, u32[]{:S(2)}) async-start(bf16[8,16,1024]{2,1,0:T(8,128)(2,1)} %shard_map.89), calls=%async_computation.8 | async-start | bytes 524288 | tf_op jit(solution)/shard_map/all_to_all | solution.py:421
  160.0 5.0 %collective-permute-start.15 = (bf16[16,2304]{1,0:T(8,128)(2,1)S(1)}, bf16[16,2304]{1,0:T(8,128)(2,1)S(1)}, u32[]{:S(2)}, u32[]{:S(2)}) collective-permute-start(bf16[16,2304]{1,0:T(8,128)(2,1)S(1)} %get-tuple-element.129), channel_id=1, source_target_pairs={{0,1},{1,2},{2,3},{3,0},{4,5},{5,6},{6,7},{7,4},{8,9},{9,10},{10,1... | collective-permute-start | bytes 221192 | tf_op jit(solution)/shard_map/ppermute | solution.py:338
  162.3 5.9 %collective-permute-start.16 = (bf16[16,2304]{1,0:T(8,128)(2,1)S(1)}, bf16[16,2304]{1,0:T(8,128)(2,1)S(1)}, u32[]{:S(2)}, u32[]{:S(2)}) collective-permute-start(bf16[16,2304]{1,0:T(8,128)(2,1)S(1)} %get-tuple-element.130), channel_id=1, source_target_pairs={{0,2},{1,3},{2,0},{3,1},{4,6},{5,7},{6,4},{7,5},{8,10},{9,11},{10,... | collective-permute-start | bytes 221192 | tf_op jit(solution)/shard_map/ppermute | solution.py:338
  163.0 5.9 %collective-permute-start.17 = (bf16[16,2304]{1,0:T(8,128)(2,1)S(1)}, bf16[16,2304]{1,0:T(8,128)(2,1)S(1)}, u32[]{:S(2)}, u32[]{:S(2)}) collective-permute-start(bf16[16,2304]{1,0:T(8,128)(2,1)S(1)} %get-tuple-element.131), channel_id=1, source_target_pairs={{0,3},{1,0},{2,1},{3,2},{4,7},{5,4},{6,5},{7,6},{8,11},{9,8},{10,9... | collective-permute-start | bytes 221192 | tf_op jit(solution)/shard_map/ppermute | solution.py:338
  (3 other events, 2.6 us)

commit v4 on v3

--- a/solution.py
+++ b/solution.py
@@ -57,23 +57,31 @@
     return lax.rem(lax.axis_index("panel") + panels - k, panels)
 
 
-def pack_body(rhs, coupling, *outs):
+def pack_body(rhs, coupling, own, beside, *refs):
+    *outs, sems = refs
     panels = len(outs) + 1
-    quarter = rhs.shape[-1]
-    for k, out in enumerate(outs, 1):
+    rows, quarter = rhs.shape[2:]
+    width = coupling.shape[-1]
+    pairs = []
+    for k, out in enumerate((own, *outs)):
         target = lax.rem(lax.axis_index("panel") + k, panels)
-        put_halves(out, rhs[0, 0])
         start = pl.multiple_of(target * quarter, quarter)
-        out[2 * rhs.shape[2] :] = coupling[0, 0, pl.ds(start, quarter), :]
-
-
-def fold_coupling_body(coupling, out):
-    width = coupling.shape[-1]
-    rows = out.shape[0]
-    for part in range(out.shape[1] // width):
-        out[:, part * width : (part + 1) * width] = coupling[
-            1, 0, part * rows : (part + 1) * rows, :
-        ]
+        source = coupling.at[0, 0, pl.ds(start, quarter)]
+        if k == 0:
+            pairs.append((source, out))
+            continue
+        pairs.append((source, out.at[pl.ds(2 * rows, quarter)]))
+        for half in range(2):
+            lanes = pl.ds(half * width, width)
+            pairs.append((rhs.at[0, 0, :, lanes], out.at[pl.ds(half * rows, rows)]))
+    for part in range(panels):
+        source = coupling.at[1, 0, pl.ds(part * quarter, quarter)]
+        pairs.append((source, beside.at[:, pl.ds(part * width, width)]))
+    copies = [pltpu.make_async_copy(a, b, sems.at[i]) for i, (a, b) in enumerate(pairs)]
+    for copy in copies:
+        copy.start()
+    for copy in copies:
+        copy.wait()
 
 
 def last_weights_body(coupling, inv, *refs):
@@ -96,13 +104,7 @@
         copy.wait()
 
 
-def put_halves(out, value):
-    rows = value.shape[0]
-    out[:rows] = value[:, :128]
-    out[rows : 2 * rows] = value[:, 128:]
-
-
-def first_body(rhs, coupling, m1, m2, m3, inv, send):
+def first_body(rhs, own, m1, m2, m3, inv, send):
     panels = send.shape[0]
     rows, quarter = rhs.shape[2:]
     total = None
@@ -113,10 +115,9 @@
         total = part if total is None else total + part
     f = total.astype(BF)
     few = rows // panels
-    own = pl.multiple_of(lax.axis_index("panel") * quarter, quarter)
-    for k, ref in enumerate((coupling, m1, m2, m3)):
+    for k, ref in enumerate((own, m1, m2, m3)):
         q = order(k, panels)
-        part = mul(f, coupling[0, 0, pl.ds(own, quarter), :] if k == 0 else ref[2 * rows :])
+        part = mul(f, own[...] if k == 0 else ref[2 * rows :])
         high = part.astype(BF)
         low = (part - high.astype(F32)).astype(BF)
         for d in range(panels):
@@ -276,10 +277,25 @@
         out[d] = blocks[lax.div(parents[level, z * GROUP + d], GROUP)]
 
 
-def down1_body(parents, counts, recv, f, lists, keep, out, picked, red):
-    blocks = [keep.at[k] for k in range(keep.shape[0])]
-    placed = place(1, counts, lists, red.shape[1])
-    red[...] = lessened(1, f[...], recv, parents, placed, blocks, red.shape[1], picked)
+def down1_body(parents, counts, recv, f, lists, keep, out, picked, red, held, sems):
+    cols = red.shape[1]
+    parts = (pl.ds(cols, held.shape[2] - cols), pl.ds(0, cols))
+    copies = [
+        [
+            pltpu.make_async_copy(keep.at[k, :, span], held.at[k, :, span], sems.at[k, part])
+            for k in range(keep.shape[0])
+        ]
+        for part, span in enumerate(parts)
+    ]
+    for copy in copies[0] + copies[1]:
+        copy.start()
+    blocks = [held.at[k] for k in range(keep.shape[0])]
+    placed = place(1, counts, lists, cols)
+    for copy in copies[0]:
+        copy.wait()
+    red[...] = lessened(1, f[...], recv, parents, placed, blocks, cols, picked)
+    for copy in copies[1]:
+        copy.wait()
     to_all(out, backward(red, blocks))
 
 
@@ -357,19 +373,24 @@
         x = lax.all_to_all(x, axes, 0, 0)
         return after((x, *moved))
 
-    packs = call(
-        pack_body, [sds(2 * rhs.shape[2] + tall, half)] * (panels - 1), rhs, coupling,
+    own, c1, *packs = call(
+        pack_body,
+        [sds(tall, half), sds(tall, panels * half)]
+        + [sds(2 * rhs.shape[2] + tall, half)] * (panels - 1),
+        rhs, coupling, specs=[HBM] * 2,
+        scratch=[pltpu.SemaphoreType.DMA((4 * panels - 2,))],
     )
     packs = [shifted(x, k) for k, x in enumerate(packs, 1)]
-    base = inv_diag[0, 0]
+    base, in1, in2 = (inv_diag[level, 0] for level in range(3))
+    packs[0], c1 = after((packs[0], c1))
+    c11, c12, c13 = (shifted(c1, k) for k in range(1, panels))
     placed0 = placement(0, counts)
-    c1 = call(fold_coupling_body, sds(tall, panels * half), coupling)
-    in1, in2 = inv_diag[1, 0], inv_diag[2, 0]
-    base, placed0, c1, in1, in2 = after((base, placed0, c1, in1, in2))
+    base, placed0, in1, in2 = after((base, placed0, in1, in2))
     send = call(
-        first_body, sds(panels, 14, rows, half), rhs, coupling, *packs, base,
-    )
-    got, c11, c13 = exchange(send, "panel", [c1, c1], [1, 3])
+        first_body, sds(panels, 14, rows, half), rhs, own, *packs, base,
+    )
+    got = lax.all_to_all(send, "panel", 0, 0)
+    got, c11, c12, c13 = after((got, c11, c12, c13))
     touched = pltpu.VMEM((rows, panels * half), BF)
     wide = pltpu.VMEM((rows, panels * half), F32)
     e = call(up0_body, sds(*mid), counts, got, placed0, specs=[SMEM] + [VMEM] * 2)
@@ -383,7 +404,7 @@
     def route(s, level, table):
         return call(functools.partial(route_body, level), sds(*mid), table, s, specs=[SMEM, VMEM])
 
-    e, in11, in13, c12 = exchange(e, "z", [in1, in1, c1], [1, 3, 2])
+    e, in11, in13 = exchange(e, "z", [in1, in1], [1, 3])
     e = fold(e, 0, parents)
     e, in12 = exchange(e, ("x", "core"), [in1], [2])
     level1 = (in1, in11, in12, in13, c1, c11, c12, c13)
@@ -411,7 +432,11 @@
     s, w01, w03 = exchange(s, ("x", "core"), [w0[1], w0[3]], [1, 3])
     s1 = call(
         down1_body, sds(*mid), parents, counts, s, f1, row_lists, keep,
-        specs=[SMEM] * 2 + [VMEM] * 4, scratch=[touched, pltpu.VMEM(mid[1:], BF)],
+        specs=[SMEM] * 2 + [VMEM] * 3 + [HBM],
+        scratch=[
+            touched, pltpu.VMEM(mid[1:], BF), pltpu.VMEM(keep.shape, BF),
+            pltpu.SemaphoreType.DMA((panels, 2)),
+        ],
     )
     s, far2 = after((s1, w0[2]))
     w02 = shifted(far2, 2)

time: 171 us -> 166 us (0.971)
  blocking collectives: 57.9 us -> 72.5 us
  waiting for transfers between devices: 45.3 us -> 35.8 us
  local copies, waits for them, and re-layouts: 7.99 us -> 1.5 us
  starting transfers between devices: 40.9 us -> 35.7 us
    all_to_all x0 -> x1, blocking collectives: none -> 10.2 us  [local(): got = lax.all_to_all(send, 'panel', 0, 0)]
    all_to_all x1 -> x0, starting transfers between devices: 8.08 us -> none  [exchange(): x = lax.all_to_all(x, axes, 0, 0)]
    unnamed x26 -> x10, local copies, waits for them, and re-layouts: 6.46 us -> 0.02 us
    ppermute x18, waiting for transfers between devices: 16.5 us -> 10.4 us  [shifted(): lax.ppermute(x, 'panel', [(i, (i + k) % panels) for i in range(panels)])]
    all_to_all x5, blocking collectives: 57.9 us -> 62.3 us  [exchange(): x = lax.all_to_all(x, axes, 0, 0)]
    ppermute x18, starting transfers between devices: 22.1 us -> 25.3 us  [shifted(): lax.ppermute(x, 'panel', [(i, (i + k) % panels) for i in range(panels)])]
    all_to_all x2, waiting for transfers between devices: 20.4 us -> 18 us  [local(): s = lax.all_to_all(s, 'z', 0, 0)]
    pallas_call x15 -> x14, Pallas kernels: 16.9 us -> 18.6 us  [call(): pl.pallas_call(body, out_shape=tuple(outs) if isinstance(outs, list) else...]
  transfers between devices with their start and end apart: 22 -> 21, of which waited for: 11 -> 8; matrix products, arithmetic and copies ran while one was open for 1% -> 1% of each run, Pallas kernels for 2% -> 3%
where the time goes in v4:
time: 166 us; the launch traced here: 165 us
  blocking collectives  72.5 us (44%)
  waiting for transfers between devices  35.8 us (22%)
  starting transfers between devices  35.7 us (22%)
  Pallas kernels  18.6 us (11%)
    all_to_all x5, blocking collectives, exchange(): x = lax.all_to_all(x, axes, 0, 0)  62.3 us
    ppermute x18, starting transfers between devices, shifted(): lax.ppermute(x, 'panel', [(i, (i + k) % panels) for i in range(panels)])  25.3 us
    pallas_call x14, Pallas kernels, call(): pl.pallas_call(body, out_shape=tuple(outs) if isinstance(outs, list) else...  18.6 us
    all_to_all x2, waiting for transfers between devices, local(): s = lax.all_to_all(s, 'z', 0, 0)  18 us
    ppermute x18, waiting for transfers between devices, shifted(): lax.ppermute(x, 'panel', [(i, (i + k) % panels) for i in range(panels)])  10.4 us
    all_to_all x1, blocking collectives, local(): got = lax.all_to_all(send, 'panel', 0, 0)  10.2 us
    all_to_all x1, waiting for transfers between devices, local(): s = lax.all_to_all(s, ('x', 'core'), 0, 0)  7.45 us
    all_to_all x2, starting transfers between devices, local(): s = lax.all_to_all(s, 'z', 0, 0)  7.01 us
  transfers between devices with their start and end apart: 21, of which 8 were waited for; matrix products, arithmetic and copies ran while one was open for 1% of the time, Pallas kernels for 3%

profile of v4, /device:TPU:24, one launch (start us, length us, event | category | flops | bytes accessed | tf_op | source)
XLA Modules:
  0.0 164.9 jit_solution(16108705906113282415)
XLA Ops:
  0.6 1.3 shard_map.77
  1.9 2.0 %collective-permute-start = (bf16[384,128]{1,0:T(8,128)(2,1)S(1)}, bf16[384,128]{1,0:T(8,128)(2,1)S(1)}, u32[]{:S(2)}, u32[]{:S(2)}) collective-permute-start(bf16[384,128]{1,0:T(8,128)(2,1)S(1)} %get-tuple-element.67), channel_id=1, source_target_pairs={{0,1},{1,2},{2,3},{3,0},{4,5},{5,6},{6,7},{7,4},{8,9},{9,10},{10,1... | collective-permute-start | bytes 294920 | tf_op jit(solution)/shard_map/ppermute | solution.py:354
  4.9 2.7 %collective-permute-done.m1 = bf16[384,128]{1,0:T(8,128)(2,1)S(1)} collective-permute-done((bf16[384,128]{1,0:T(8,128)(2,1)S(1)}, bf16[384,128]{1,0:T(8,128)(2,1)S(1)}, u32[]{:S(2)}, u32[]{:S(2)}) %collective-permute-start) | collective-permute-done | bytes 98336 | tf_op jit(solution)/shard_map/ppermute | solution.py:354
  7.6 5.4 %collective-permute-start.4 = (bf16[256,512]{1,0:T(8,128)(2,1)S(1)}, bf16[256,512]{1,0:T(8,128)(2,1)S(1)}, u32[]{:S(2)}, u32[]{:S(2)}) collective-permute-start(bf16[256,512]{1,0:T(8,128)(2,1)S(1)} %get-tuple-element.73.c0), channel_id=1, source_target_pairs={{0,2},{1,3},{2,0},{3,1},{4,6},{5,7},{6,4},{7,5},{8,10},{9,11},{10,... | collective-permute-start | bytes 786440 | tf_op jit(solution)/shard_map/ppermute | solution.py:354
  13.0 1.5 slice_bitcast_fusion
  15.9 10.2 %all_to_all.45.got = bf16[4,14,16,128]{3,2,1,0:T(8,128)(2,1)S(1)} all-to-all(bf16[4,14,16,128]{3,2,1,0:T(8,128)(2,1)S(1)} %shard_map.79), channel_id=1, replica_groups=mesh['z'=8,'x'=4,'core'=2,'panel'=4] {'panel'}, dimensions={0} | all-to-all | bytes 458752 | tf_op jit(solution)/shard_map/all_to_all | solution.py:392
  27.0 2.5 %collective-permute-start.6 = (bf16[256,1024]{1,0:T(8,128)(2,1)S(1)}, bf16[256,1024]{1,0:T(8,128)(2,1)S(1)}, u32[]{:S(2)}, u32[]{:S(2)}) collective-permute-start(bf16[256,1024]{1,0:T(8,128)(2,1)S(1)} %get-tuple-element.82.i0), channel_id=1, source_target_pairs={{0,1},{1,2},{2,3},{3,0},{4,5},{5,6},{6,7},{7,4},{8,9},{9,10},{10,1... | collective-permute-start | bytes 1572872 | tf_op jit(solution)/shard_map/ppermute | solution.py:354
  29.5 17.2 %all_to_all.46.blocks = bf16[8,16,1024]{2,1,0:T(8,128)(2,1)S(1)} all-to-all(bf16[8,16,1024]{2,1,0:T(8,128)(2,1)S(1)} %shard_map.80), channel_id=1, replica_groups=mesh['z'=8,'x'=4,'core'=2,'panel'=4] {'z'}, dimensions={0} | all-to-all | bytes 524288 | tf_op jit(solution)/shard_map/all_to_all | solution.py:373
  47.4 1.9 %collective-permute-start.8 = (bf16[256,1024]{1,0:T(8,128)(2,1)S(1)}, bf16[256,1024]{1,0:T(8,128)(2,1)S(1)}, u32[]{:S(2)}, u32[]{:S(2)}) collective-permute-start(bf16[256,1024]{1,0:T(8,128)(2,1)S(1)} %get-tuple-element.82.i0), channel_id=1, source_target_pairs={{0,2},{1,3},{2,0},{3,1},{4,6},{5,7},{6,4},{7,5},{8,10},{9,11},{10,... | collective-permute-start | bytes 1572872 | tf_op jit(solution)/shard_map/ppermute | solution.py:354
  49.3 11.6 %all_to_all.47.recv = bf16[8,16,1024]{2,1,0:T(8,128)(2,1)S(1)} all-to-all(bf16[8,16,1024]{2,1,0:T(8,128)(2,1)S(1)} %shard_map.81), channel_id=1, replica_groups=mesh['z'=8,'x'=4,'core'=2,'panel'=4] {'x','core'}, dimensions={0} | all-to-all | bytes 524288 | tf_op jit(solution)/shard_map/all_to_all | solution.py:373
  60.9 2.1 %shard_map.82 = (bf16[16,1024]{1,0:T(8,128)(2,1)S(1)}, bf16[8,16,1024]{2,1,0:T(8,128)(2,1)S(1)}, bf16[4,256,1536]{2,1,0:T(8,128)(2,1)S(1)}) custom-call(s32[2,64]{1,0:T(2,128)S(1)} %copy-done.4, bf16[8,16,1024]{2,1,0:T(8,128)(2,1)S(1)} %all_to_all.47.recv, bf16[4,14,16,128]{3,2,1,0:T(8,128)(2,1)S(1)} %all_to_all.45.got, s32[2,64,512]{2,1,0:T(8,128)S(1)} %copy-done, ...), custom_call_target="tpu_custom_call" | custom-call | tf_op jit(solution)/shard_map/pallas_call | solution.py:32
  63.0 1.4 collective-permute-start.9
  65.1 13.6 %all_to_all.48.blocks = bf16[8,16,1024]{2,1,0:T(8,128)(2,1)S(1)} all-to-all(bf16[8,16,1024]{2,1,0:T(8,128)(2,1)S(1)} %get-tuple-element.92), channel_id=1, replica_groups=mesh['z'=8,'x'=4,'core'=2,'panel'=4] {'z'}, dimensions={0} | all-to-all | bytes 524288 | tf_op jit(solution)/shard_map/all_to_all | solution.py:373
  79.5 1.9 %collective-permute-start.11 = (bf16[256,1024]{1,0:T(8,128)(2,1)S(1)}, bf16[256,1024]{1,0:T(8,128)(2,1)S(1)}, u32[]{:S(2)}, u32[]{:S(2)}) collective-permute-start(bf16[256,1024]{1,0:T(8,128)(2,1)S(1)} %get-tuple-element.97.i0), channel_id=1, source_target_pairs={{0,2},{1,3},{2,0},{3,1},{4,6},{5,7},{6,4},{7,5},{8,10},{9,11},{10,... | collective-permute-start | bytes 1572872 | tf_op jit(solution)/shard_map/ppermute | solution.py:354
  81.3 9.9 %all_to_all.49.recv = bf16[8,16,1024]{2,1,0:T(8,128)(2,1)S(1)} all-to-all(bf16[8,16,1024]{2,1,0:T(8,128)(2,1)S(1)} %shard_map.83), channel_id=1, replica_groups=mesh['z'=8,'x'=4,'core'=2,'panel'=4] {'x','core'}, dimensions={0} | all-to-all | bytes 524288 | tf_op jit(solution)/shard_map/all_to_all | solution.py:373
  91.3 2.0 %collective-permute-done.11.i2 = bf16[256,1024]{1,0:T(8,128)(2,1)S(1)} collective-permute-done((bf16[256,1024]{1,0:T(8,128)(2,1)S(1)}, bf16[256,1024]{1,0:T(8,128)(2,1)S(1)}, u32[]{:S(2)}, u32[]{:S(2)}) %collective-permute-start.11) | collective-permute-done | bytes 524320 | tf_op jit(solution)/shard_map/ppermute | solution.py:354
  93.2 1.7 %shard_map.84 = (bf16[16,1024]{1,0:T(8,128)(2,1)S(1)}, bf16[8,16,1024]{2,1,0:T(8,128)(2,1)}) custom-call(bf16[8,16,1024]{2,1,0:T(8,128)(2,1)S(1)} %all_to_all.49.recv, bf16[4,14,16,128]{3,2,1,0:T(8,128)(2,1)S(1)} %all_to_all.45.got, bf16[256,1024]{1,0:T(8,128)(2,1)S(1)} %get-tuple-element.97.i0, bf16[256,1024]{1,0:T(8,128)(2,1)S(1)} %collective-permute-done.9.i1, ...), custom_call_target="tpu_custom_call" | custom-call | tf_op jit(solution)/shard_map/pallas_call | solution.py:32
  95.0 3.6 %all-to-all-start.5 = ((bf16[8,16,1024]{2,1,0:T(8,128)(2,1)}), bf16[8,16,1024]{2,1,0:T(8,128)(2,1)S(1)}, u32[]{:S(2)}, u32[]{:S(2)}) async-start(bf16[8,16,1024]{2,1,0:T(8,128)(2,1)} %get-tuple-element.103.s2), calls=%async_computation.5 | async-start | bytes 524288 | tf_op jit(solution)/shard_map/all_to_all | solution.py:429
  98.6 1.9 %shard_map.85 = (bf16[256,768]{1,0:T(8,128)(2,1)S(1)}, bf16[256,768]{1,0:T(8,128)(2,1)S(1)}, bf16[256,768]{1,0:T(8,128)(2,1)S(1)}, bf16[256,768]{1,0:T(8,128)(2,1)S(1)}) custom-call(bf16[2,1,1024,128]{3,2,1,0:T(8,128)(2,1)} %coupling.2, bf16[3,1,256,1024]{3,2,1,0:T(8,128)(2,1)} %inv), custom_call_target="tpu_custom_call" | custom-call | tf_op jit(solution)/shard_map/pallas_call | solution.py:32
  100.5 8.3 %all-to-all-done.5.blocks = bf16[8,16,1024]{2,1,0:T(8,128)(2,1)S(1)} async-done(((bf16[8,16,1024]{2,1,0:T(8,128)(2,1)}), bf16[8,16,1024]{2,1,0:T(8,128)(2,1)S(1)}, u32[]{:S(2)}, u32[]{:S(2)}) %all-to-all-start.5) | async-done | bytes 262176 | tf_op jit(solution)/shard_map/all_to_all | solution.py:429
  109.4 2.2 %collective-permute-start.12 = (bf16[256,768]{1,0:T(8,128)(2,1)S(1)}, bf16[256,768]{1,0:T(8,128)(2,1)S(1)}, u32[]{:S(2)}, u32[]{:S(2)}) collective-permute-start(bf16[256,768]{1,0:T(8,128)(2,1)S(1)} %get-tuple-element.114), channel_id=1, source_target_pairs={{0,1},{1,2},{2,3},{3,0},{4,5},{5,6},{6,7},{7,4},{8,9},{9,10},{10,1... | collective-permute-start | bytes 1179656 | tf_op jit(solution)/shard_map/ppermute | solution.py:354
  111.6 9.9 %all_to_all.50.recv = bf16[8,16,1024]{2,1,0:T(8,128)(2,1)S(1)} all-to-all(bf16[8,16,1024]{2,1,0:T(8,128)(2,1)S(1)} %shard_map.86), channel_id=1, replica_groups=mesh['z'=8,'x'=4,'core'=2,'panel'=4] {'x','core'}, dimensions={0} | all-to-all | bytes 524288 | tf_op jit(solution)/shard_map/all_to_all | solution.py:373
  121.5 3.6 %shard_map.87.s1 = bf16[8,16,1024]{2,1,0:T(8,128)(2,1)} custom-call(s32[2,64]{1,0:T(2,128)S(1)} %copy-done.3, s32[2,64]{1,0:T(2,128)S(1)} %copy-done.4, bf16[8,16,1024]{2,1,0:T(8,128)(2,1)S(1)} %all_to_all.50.recv, bf16[16,1024]{1,0:T(8,128)(2,1)S(1)} %get-tuple-element.117.f.f1, s32[2,64,512]{2,1,0:T(8,128)S(1)} %copy-done, bf16[4,256,1536]{2,1,0:T(8,128)(2,1)} %copy-done.1), custom_call_target="tpu_custom_call" | custom-call | tf_op jit(solution)/shard_map/pallas_call | solution.py:32
  125.1 3.4 %all-to-all-start.7 = ((bf16[8,16,1024]{2,1,0:T(8,128)(2,1)}), bf16[8,16,1024]{2,1,0:T(8,128)(2,1)S(1)}, u32[]{:S(2)}, u32[]{:S(2)}) async-start(bf16[8,16,1024]{2,1,0:T(8,128)(2,1)} %shard_map.87.s1), calls=%async_computation.7 | async-start | bytes 524288 | tf_op jit(solution)/shard_map/all_to_all | solution.py:443
  128.6 2.0 %collective-permute-start.14 = (bf16[256,768]{1,0:T(8,128)(2,1)S(1)}, bf16[256,768]{1,0:T(8,128)(2,1)S(1)}, u32[]{:S(2)}, u32[]{:S(2)}) collective-permute-start(bf16[256,768]{1,0:T(8,128)(2,1)S(1)} %get-tuple-element.123), channel_id=1, source_target_pairs={{0,2},{1,3},{2,0},{3,1},{4,6},{5,7},{6,4},{7,5},{8,10},{9,11},{10,... | collective-permute-start | bytes 1179656 | tf_op jit(solution)/shard_map/ppermute | solution.py:354
  130.6 9.7 %all-to-all-done.7.blocks = bf16[8,16,1024]{2,1,0:T(8,128)(2,1)S(1)} async-done(((bf16[8,16,1024]{2,1,0:T(8,128)(2,1)}), bf16[8,16,1024]{2,1,0:T(8,128)(2,1)S(1)}, u32[]{:S(2)}, u32[]{:S(2)}) %all-to-all-start.7) | async-done | bytes 262176 | tf_op jit(solution)/shard_map/all_to_all | solution.py:443
  141.5 3.4 %all-to-all-start.8 = ((bf16[8,16,1024]{2,1,0:T(8,128)(2,1)}), bf16[8,16,1024]{2,1,0:T(8,128)(2,1)S(1)}, u32[]{:S(2)}, u32[]{:S(2)}) async-start(bf16[8,16,1024]{2,1,0:T(8,128)(2,1)} %shard_map.88), calls=%async_computation.8 | async-start | bytes 524288 | tf_op jit(solution)/shard_map/all_to_all | solution.py:446
  145.0 7.4 %all-to-all-done.8.recv = bf16[8,16,1024]{2,1,0:T(8,128)(2,1)S(1)} async-done(((bf16[8,16,1024]{2,1,0:T(8,128)(2,1)}), bf16[8,16,1024]{2,1,0:T(8,128)(2,1)S(1)}, u32[]{:S(2)}, u32[]{:S(2)}) %all-to-all-start.8) | async-done | bytes 262176 | tf_op jit(solution)/shard_map/all_to_all | solution.py:446
  152.4 1.7 %shard_map.89 = (bf16[16,2304]{1,0:T(8,128)(2,1)S(1)}, bf16[16,2304]{1,0:T(8,128)(2,1)S(1)}, bf16[16,2304]{1,0:T(8,128)(2,1)S(1)}, bf16[16,2304]{1,0:T(8,128)(2,1)S(1)}) custom-call(s32[2,64]{1,0:T(2,128)S(1)} %copy-done.3, s32[2,64]{1,0:T(2,128)S(1)} %copy-done.4, bf16[8,16,1024]{2,1,0:T(8,128)(2,1)S(1)} %all-to-all-done.8.recv, ...), custom_call_target="tpu_custom_call" | custom-call | tf_op jit(solution)/shard_map/pallas_call | solution.py:32
  154.1 3.3 %collective-permute-start.15 = (bf16[16,2304]{1,0:T(8,128)(2,1)S(1)}, bf16[16,2304]{1,0:T(8,128)(2,1)S(1)}, u32[]{:S(2)}, u32[]{:S(2)}) collective-permute-start(bf16[16,2304]{1,0:T(8,128)(2,1)S(1)} %get-tuple-element.127), channel_id=1, source_target_pairs={{0,1},{1,2},{2,3},{3,0},{4,5},{5,6},{6,7},{7,4},{8,9},{9,10},{10,1... | collective-permute-start | bytes 221192 | tf_op jit(solution)/shard_map/ppermute | solution.py:354
  158.3 1.8 %collective-permute-done.15.refs_1_ = bf16[16,2304]{1,0:T(8,128)(2,1)S(1)} collective-permute-done((bf16[16,2304]{1,0:T(8,128)(2,1)S(1)}, bf16[16,2304]{1,0:T(8,128)(2,1)S(1)}, u32[]{:S(2)}, u32[]{:S(2)}) %collective-permute-start.15) | collective-permute-done | bytes 73760 | tf_op jit(solution)/shard_map/ppermute | solution.py:354
  160.2 3.1 %collective-permute-done.16.refs_2_ = bf16[16,2304]{1,0:T(8,128)(2,1)S(1)} collective-permute-done((bf16[16,2304]{1,0:T(8,128)(2,1)S(1)}, bf16[16,2304]{1,0:T(8,128)(2,1)S(1)}, u32[]{:S(2)}, u32[]{:S(2)}) %collective-permute-start.16) | collective-permute-done | bytes 73760 | tf_op jit(solution)/shard_map/ppermute | solution.py:354
  (41 shorter events, 9.7 us)
Async XLA Ops:
  1.9 5.7 %collective-permute-start = (bf16[384,128]{1,0:T(8,128)(2,1)S(1)}, bf16[384,128]{1,0:T(8,128)(2,1)S(1)}, u32[]{:S(2)}, u32[]{:S(2)}) collective-permute-start(bf16[384,128]{1,0:T(8,128)(2,1)S(1)} %get-tuple-element.67), channel_id=1, source_target_pairs={{0,1},{1,2},{2,3},{3,0},{4,5},{5,6},{6,7},{7,4},{8,9},{9,10},{10,1... | collective-permute-start | bytes 294920 | tf_op jit(solution)/shard_map/ppermute | solution.py:354
  4.0 11.3 %collective-permute-start.1 = (bf16[384,128]{1,0:T(8,128)(2,1)S(1)}, bf16[384,128]{1,0:T(8,128)(2,1)S(1)}, u32[]{:S(2)}, u32[]{:S(2)}) collective-permute-start(bf16[384,128]{1,0:T(8,128)(2,1)S(1)} %get-tuple-element.70), channel_id=1, source_target_pairs={{0,2},{1,3},{2,0},{3,1},{4,6},{5,7},{6,4},{7,5},{8,10},{9,11},{10,... | collective-permute-start | bytes 294920 | tf_op jit(solution)/shard_map/ppermute | solution.py:354
  4.8 10.5 %collective-permute-start.2 = (bf16[384,128]{1,0:T(8,128)(2,1)S(1)}, bf16[384,128]{1,0:T(8,128)(2,1)S(1)}, u32[]{:S(2)}, u32[]{:S(2)}) collective-permute-start(bf16[384,128]{1,0:T(8,128)(2,1)S(1)} %get-tuple-element.71), channel_id=1, source_target_pairs={{0,3},{1,0},{2,1},{3,2},{4,7},{5,4},{6,5},{7,6},{8,11},{9,8},{10,9... | collective-permute-start | bytes 294920 | tf_op jit(solution)/shard_map/ppermute | solution.py:354
  7.6 6.9 %copy-start = (s32[2,64,512]{2,1,0:T(8,128)S(1)}, s32[2,64,512]{2,1,0:T(8,128)}, u32[]{:S(2)}) copy-start(s32[2,64,512]{2,1,0:T(8,128)} %lists.7) | copy-start | bytes 786436
  7.6 6.9 %copy-start.4 = (s32[2,64]{1,0:T(2,128)S(1)}, s32[2,64]{1,0:T(2,128)}, u32[]{:S(2)}) copy-start(s32[2,64]{1,0:T(2,128)} %counts.9) | copy-start | bytes 1540
  7.6 7.7 %copy-start.2 = (bf16[3,1,64,256]{3,2,1,0:T(8,128)(2,1)S(1)}, bf16[3,1,64,256]{3,2,1,0:T(8,128)(2,1)}, u32[]{:S(2)}) copy-start(bf16[3,1,64,256]{3,2,1,0:T(8,128)(2,1)} %rhs.3) | copy-start | bytes 294916
  7.6 18.5 %collective-permute-start.5 = (bf16[256,512]{1,0:T(8,128)(2,1)S(1)}, bf16[256,512]{1,0:T(8,128)(2,1)S(1)}, u32[]{:S(2)}, u32[]{:S(2)}) collective-permute-start(bf16[256,512]{1,0:T(8,128)(2,1)S(1)} %get-tuple-element.73.c0), channel_id=1, source_target_pairs={{0,3},{1,0},{2,1},{3,2},{4,7},{5,4},{6,5},{7,6},{8,11},{9,8},{10,9... | collective-permute-start | bytes 786440 | tf_op jit(solution)/shard_map/ppermute | solution.py:354
  7.6 18.5 %collective-permute-start.4 = (bf16[256,512]{1,0:T(8,128)(2,1)S(1)}, bf16[256,512]{1,0:T(8,128)(2,1)S(1)}, u32[]{:S(2)}, u32[]{:S(2)}) collective-permute-start(bf16[256,512]{1,0:T(8,128)(2,1)S(1)} %get-tuple-element.73.c0), channel_id=1, source_target_pairs={{0,2},{1,3},{2,0},{3,1},{4,6},{5,7},{6,4},{7,5},{8,10},{9,11},{10,... | collective-permute-start | bytes 786440 | tf_op jit(solution)/shard_map/ppermute | solution.py:354
  13.0 13.1 %collective-permute-start.3 = (bf16[256,512]{1,0:T(8,128)(2,1)S(1)}, bf16[256,512]{1,0:T(8,128)(2,1)S(1)}, u32[]{:S(2)}, u32[]{:S(2)}) collective-permute-start(bf16[256,512]{1,0:T(8,128)(2,1)S(1)} %get-tuple-element.73.c0), channel_id=1, source_target_pairs={{0,1},{1,2},{2,3},{3,0},{4,5},{5,6},{6,7},{7,4},{8,9},{9,10},{10,1... | collective-permute-start | bytes 786440 | tf_op jit(solution)/shard_map/ppermute | solution.py:354
  15.3 31.4 %copy-start.3 = (s32[2,64]{1,0:T(2,128)S(1)}, s32[2,64]{1,0:T(2,128)}, u32[]{:S(2)}) copy-start(s32[2,64]{1,0:T(2,128)} %parents.11) | copy-start | bytes 1540
  27.0 19.7 %collective-permute-start.6 = (bf16[256,1024]{1,0:T(8,128)(2,1)S(1)}, bf16[256,1024]{1,0:T(8,128)(2,1)S(1)}, u32[]{:S(2)}, u32[]{:S(2)}) collective-permute-start(bf16[256,1024]{1,0:T(8,128)(2,1)S(1)} %get-tuple-element.82.i0), channel_id=1, source_target_pairs={{0,1},{1,2},{2,3},{3,0},{4,5},{5,6},{6,7},{7,4},{8,9},{9,10},{10,1... | collective-permute-start | bytes 1572872 | tf_op jit(solution)/shard_map/ppermute | solution.py:354
  29.5 17.2 %collective-permute-start.7 = (bf16[256,1024]{1,0:T(8,128)(2,1)S(1)}, bf16[256,1024]{1,0:T(8,128)(2,1)S(1)}, u32[]{:S(2)}, u32[]{:S(2)}) collective-permute-start(bf16[256,1024]{1,0:T(8,128)(2,1)S(1)} %get-tuple-element.82.i0), channel_id=1, source_target_pairs={{0,3},{1,0},{2,1},{3,2},{4,7},{5,4},{6,5},{7,6},{8,11},{9,8},{10,9... | collective-permute-start | bytes 1572872 | tf_op jit(solution)/shard_map/ppermute | solution.py:354
  47.4 13.5 %collective-permute-start.8 = (bf16[256,1024]{1,0:T(8,128)(2,1)S(1)}, bf16[256,1024]{1,0:T(8,128)(2,1)S(1)}, u32[]{:S(2)}, u32[]{:S(2)}) collective-permute-start(bf16[256,1024]{1,0:T(8,128)(2,1)S(1)} %get-tuple-element.82.i0), channel_id=1, source_target_pairs={{0,2},{1,3},{2,0},{3,1},{4,6},{5,7},{6,4},{7,5},{8,10},{9,11},{10,... | collective-permute-start | bytes 1572872 | tf_op jit(solution)/shard_map/ppermute | solution.py:354
  63.0 32.0 %copy-start.1 = (bf16[4,256,1536]{2,1,0:T(8,128)(2,1)}, bf16[4,256,1536]{2,1,0:T(8,128)(2,1)S(1)}, u32[]{:S(2)}) copy-start(bf16[4,256,1536]{2,1,0:T(8,128)(2,1)S(1)} %get-tuple-element.118.keep) | copy-start | bytes 9437188
  63.0 15.7 %collective-permute-start.9 = (bf16[256,1024]{1,0:T(8,128)(2,1)S(1)}, bf16[256,1024]{1,0:T(8,128)(2,1)S(1)}, u32[]{:S(2)}, u32[]{:S(2)}) collective-permute-start(bf16[256,1024]{1,0:T(8,128)(2,1)S(1)} %get-tuple-element.97.i0), channel_id=1, source_target_pairs={{0,1},{1,2},{2,3},{3,0},{4,5},{5,6},{6,7},{7,4},{8,9},{9,10},{10,1... | collective-permute-start | bytes 1572872 | tf_op jit(solution)/shard_map/ppermute | solution.py:354
  64.4 14.3 %collective-permute-start.10 = (bf16[256,1024]{1,0:T(8,128)(2,1)S(1)}, bf16[256,1024]{1,0:T(8,128)(2,1)S(1)}, u32[]{:S(2)}, u32[]{:S(2)}) collective-permute-start(bf16[256,1024]{1,0:T(8,128)(2,1)S(1)} %get-tuple-element.97.i0), channel_id=1, source_target_pairs={{0,3},{1,0},{2,1},{3,2},{4,7},{5,4},{6,5},{7,6},{8,11},{9,8},{10,9... | collective-permute-start | bytes 1572872 | tf_op jit(solution)/shard_map/ppermute | solution.py:354
  79.5 13.8 %collective-permute-start.11 = (bf16[256,1024]{1,0:T(8,128)(2,1)S(1)}, bf16[256,1024]{1,0:T(8,128)(2,1)S(1)}, u32[]{:S(2)}, u32[]{:S(2)}) collective-permute-start(bf16[256,1024]{1,0:T(8,128)(2,1)S(1)} %get-tuple-element.97.i0), channel_id=1, source_target_pairs={{0,2},{1,3},{2,0},{3,1},{4,6},{5,7},{6,4},{7,5},{8,10},{9,11},{10,... | collective-permute-start | bytes 1572872 | tf_op jit(solution)/shard_map/ppermute | solution.py:354
  95.0 13.8 %all-to-all-start.5 = ((bf16[8,16,1024]{2,1,0:T(8,128)(2,1)}), bf16[8,16,1024]{2,1,0:T(8,128)(2,1)S(1)}, u32[]{:S(2)}, u32[]{:S(2)}) async-start(bf16[8,16,1024]{2,1,0:T(8,128)(2,1)} %get-tuple-element.103.s2), calls=%async_computation.5 | async-start | bytes 524288 | tf_op jit(solution)/shard_map/all_to_all | solution.py:429
  109.4 12.1 %collective-permute-start.12 = (bf16[256,768]{1,0:T(8,128)(2,1)S(1)}, bf16[256,768]{1,0:T(8,128)(2,1)S(1)}, u32[]{:S(2)}, u32[]{:S(2)}) collective-permute-start(bf16[256,768]{1,0:T(8,128)(2,1)S(1)} %get-tuple-element.114), channel_id=1, source_target_pairs={{0,1},{1,2},{2,3},{3,0},{4,5},{5,6},{6,7},{7,4},{8,9},{9,10},{10,1... | collective-permute-start | bytes 1179656 | tf_op jit(solution)/shard_map/ppermute | solution.py:354
  111.6 9.9 %collective-permute-start.13 = (bf16[256,768]{1,0:T(8,128)(2,1)S(1)}, bf16[256,768]{1,0:T(8,128)(2,1)S(1)}, u32[]{:S(2)}, u32[]{:S(2)}) collective-permute-start(bf16[256,768]{1,0:T(8,128)(2,1)S(1)} %get-tuple-element.115), channel_id=1, source_target_pairs={{0,3},{1,0},{2,1},{3,2},{4,7},{5,4},{6,5},{7,6},{8,11},{9,8},{10,9... | collective-permute-start | bytes 1179656 | tf_op jit(solution)/shard_map/ppermute | solution.py:354
  125.1 15.1 %all-to-all-start.7 = ((bf16[8,16,1024]{2,1,0:T(8,128)(2,1)}), bf16[8,16,1024]{2,1,0:T(8,128)(2,1)S(1)}, u32[]{:S(2)}, u32[]{:S(2)}) async-start(bf16[8,16,1024]{2,1,0:T(8,128)(2,1)} %shard_map.87.s1), calls=%async_computation.7 | async-start | bytes 524288 | tf_op jit(solution)/shard_map/all_to_all | solution.py:443
  128.6 16.4 %collective-permute-start.14 = (bf16[256,768]{1,0:T(8,128)(2,1)S(1)}, bf16[256,768]{1,0:T(8,128)(2,1)S(1)}, u32[]{:S(2)}, u32[]{:S(2)}) collective-permute-start(bf16[256,768]{1,0:T(8,128)(2,1)S(1)} %get-tuple-element.123), channel_id=1, source_target_pairs={{0,2},{1,3},{2,0},{3,1},{4,6},{5,7},{6,4},{7,5},{8,10},{9,11},{10,... | collective-permute-start | bytes 1179656 | tf_op jit(solution)/shard_map/ppermute | solution.py:354
  141.5 10.9 %all-to-all-start.8 = ((bf16[8,16,1024]{2,1,0:T(8,128)(2,1)}), bf16[8,16,1024]{2,1,0:T(8,128)(2,1)S(1)}, u32[]{:S(2)}, u32[]{:S(2)}) async-start(bf16[8,16,1024]{2,1,0:T(8,128)(2,1)} %shard_map.88), calls=%async_computation.8 | async-start | bytes 524288 | tf_op jit(solution)/shard_map/all_to_all | solution.py:446
  154.1 6.1 %collective-permute-start.15 = (bf16[16,2304]{1,0:T(8,128)(2,1)S(1)}, bf16[16,2304]{1,0:T(8,128)(2,1)S(1)}, u32[]{:S(2)}, u32[]{:S(2)}) collective-permute-start(bf16[16,2304]{1,0:T(8,128)(2,1)S(1)} %get-tuple-element.127), channel_id=1, source_target_pairs={{0,1},{1,2},{2,3},{3,0},{4,5},{5,6},{6,7},{7,4},{8,9},{9,10},{10,1... | collective-permute-start | bytes 221192 | tf_op jit(solution)/shard_map/ppermute | solution.py:354
  157.4 5.9 %collective-permute-start.16 = (bf16[16,2304]{1,0:T(8,128)(2,1)S(1)}, bf16[16,2304]{1,0:T(8,128)(2,1)S(1)}, u32[]{:S(2)}, u32[]{:S(2)}) collective-permute-start(bf16[16,2304]{1,0:T(8,128)(2,1)S(1)} %get-tuple-element.128), channel_id=1, source_target_pairs={{0,2},{1,3},{2,0},{3,1},{4,6},{5,7},{6,4},{7,5},{8,10},{9,11},{10,... | collective-permute-start | bytes 221192 | tf_op jit(solution)/shard_map/ppermute | solution.py:354
  158.0 6.0 %collective-permute-start.17 = (bf16[16,2304]{1,0:T(8,128)(2,1)S(1)}, bf16[16,2304]{1,0:T(8,128)(2,1)S(1)}, u32[]{:S(2)}, u32[]{:S(2)}) collective-permute-start(bf16[16,2304]{1,0:T(8,128)(2,1)S(1)} %get-tuple-element.129), channel_id=1, source_target_pairs={{0,3},{1,0},{2,1},{3,2},{4,7},{5,4},{6,5},{7,6},{8,11},{9,8},{10,9... | collective-permute-start | bytes 221192 | tf_op jit(solution)/shard_map/ppermute | solution.py:354

commit v5 on v4

--- a/solution.py
+++ b/solution.py
@@ -139,10 +139,6 @@
     return jnp.where((row == mine) & (col < counts[level, leaf]), 1.0, 0.0).astype(BF)
 
 
-def place_body(level, counts, lists, out):
-    out[...] = place(level, counts, lists, out.shape[0])
-
-
 def laid_out(level, u, placed, counts):
     _, _, leaf = leaf_place()
     col = lax.broadcasted_iota(jnp.int32, u.shape, 1)
@@ -158,7 +154,8 @@
     )
 
 
-def up0_body(counts, got, placed, out):
+def up0_body(counts, got, lists, out):
+    placed = place(0, counts, lists, out.shape[2])
     panels = got.shape[0]
     pieces = []
     for q in range(panels):
@@ -167,7 +164,7 @@
             part = got[source, q].astype(F32) + got[source, panels + q].astype(F32)
             total = part if total is None else total + part
         pieces.append(total)
-    e = laid_out(0, jnp.concatenate(pieces, axis=1), placed[...], counts)
+    e = laid_out(0, jnp.concatenate(pieces, axis=1), placed, counts)
     for d in range(out.shape[0]):
         out[d] = e
 
@@ -353,14 +350,6 @@
     def shifted(x, k):
         return lax.ppermute(x, "panel", [(i, (i + k) % panels) for i in range(panels)])
 
-    def placement(level, counts):
-        return call(
-            functools.partial(place_body, level),
-            sds(inv_diag.shape[3], row_lists.shape[2]),
-            counts, row_lists,
-            specs=[SMEM, VMEM],
-        )
-
     half = coupling.shape[3]
     tall = rhs.shape[3]
     half = coupling.shape[3]
@@ -384,8 +373,7 @@
     base, in1, in2 = (inv_diag[level, 0] for level in range(3))
     packs[0], c1 = after((packs[0], c1))
     c11, c12, c13 = (shifted(c1, k) for k in range(1, panels))
-    placed0 = placement(0, counts)
-    base, placed0, in1, in2 = after((base, placed0, in1, in2))
+    base, in1, in2 = after((base, in1, in2))
     send = call(
         first_body, sds(panels, 14, rows, half), rhs, own, *packs, base,
     )
@@ -393,7 +381,7 @@
     got, c11, c12, c13 = after((got, c11, c12, c13))
     touched = pltpu.VMEM((rows, panels * half), BF)
     wide = pltpu.VMEM((rows, panels * half), F32)
-    e = call(up0_body, sds(*mid), counts, got, placed0, specs=[SMEM] + [VMEM] * 2)
+    e = call(up0_body, sds(*mid), counts, got, row_lists, specs=[SMEM] + [VMEM] * 2)
 
     def fold(e, level, table):
         return call(
@@ -426,10 +414,13 @@
         specs=[HBM] * 2, outs_at=HBM,
         scratch=[pltpu.SemaphoreType.DMA((panels * (panels + 1),))],
     )
+    w0 = [*w0]
     s = lax.all_to_all(s, "z", 0, 0)
-    s, *w0 = after((s, *w0))
+    w01, w03 = shifted(w0[1], 1), shifted(w0[3], 3)
+    s, w0[0], w0[2] = after((s, w0[0], w0[2]))
     s = route(s, 1, parents)
-    s, w01, w03 = exchange(s, ("x", "core"), [w0[1], w0[3]], [1, 3])
+    s = lax.all_to_all(s, ("x", "core"), 0, 0)
+    s, w01, w03 = after((s, w01, w03))
     s1 = call(
         down1_body, sds(*mid), parents, counts, s, f1, row_lists, keep,
         specs=[SMEM] * 2 + [VMEM] * 3 + [HBM],

time: 166 us -> 165 us (level)
  blocking collectives: 72.5 us -> 63.2 us
  waiting for transfers between devices: 35.8 us -> 40.6 us
  starting transfers between devices: 35.7 us -> 39.4 us
    all_to_all x5 -> x4, blocking collectives: 62.3 us -> 53 us  [exchange(): x = lax.all_to_all(x, axes, 0, 0)]
    all_to_all x1 -> x2, waiting for transfers between devices: 7.45 us -> 14.9 us  [local(): s = lax.all_to_all(s, ('x', 'core'), 0, 0)]
    all_to_all x1 -> x2, starting transfers between devices: 3.41 us -> 6.82 us  [local(): s = lax.all_to_all(s, ('x', 'core'), 0, 0)]
    pallas_call x14 -> x13, Pallas kernels: 18.6 us -> 18.5 us  [call(): pl.pallas_call(body, out_shape=tuple(outs) if isinstance(outs, list) else...]
  transfers between devices with their start and end apart: 21 -> 22, of which waited for: 8 -> 9; matrix products, arithmetic and copies ran while one was open for 1% -> 1% of each run, Pallas kernels for 3% -> 3%
where the time goes in v5:
time: 165 us; the launch traced here: 164 us
  blocking collectives  63.2 us (38%)
  waiting for transfers between devices  40.6 us (25%)
  starting transfers between devices  39.4 us (24%)
  Pallas kernels  18.5 us (11%)
    all_to_all x4, blocking collectives, exchange(): x = lax.all_to_all(x, axes, 0, 0)  53 us
    ppermute x18, starting transfers between devices, shifted(): lax.ppermute(x, 'panel', [(i, (i + k) % panels) for i in range(panels)])  25.7 us
    pallas_call x13, Pallas kernels, call(): pl.pallas_call(body, out_shape=tuple(outs) if isinstance(outs, list) else...  18.5 us
    all_to_all x2, waiting for transfers between devices, local(): s = lax.all_to_all(s, 'z', 0, 0)  16.5 us
    all_to_all x2, waiting for transfers between devices, local(): s = lax.all_to_all(s, ('x', 'core'), 0, 0)  14.9 us
    all_to_all x1, blocking collectives, local(): got = lax.all_to_all(send, 'panel', 0, 0)  10.2 us
    ppermute x18, waiting for transfers between devices, shifted(): lax.ppermute(x, 'panel', [(i, (i + k) % panels) for i in range(panels)])  9.19 us
    all_to_all x2, starting transfers between devices, local(): s = lax.all_to_all(s, 'z', 0, 0)  6.83 us
  transfers between devices with their start and end apart: 22, of which 9 were waited for; matrix products, arithmetic and copies ran while one was open for 1% of the time, Pallas kernels for 3%

profile of v5, /device:TPU:24, one launch (start us, length us, event | category | flops | bytes accessed | tf_op | source)
XLA Modules:
  0.0 164.1 jit_solution(3308313753886609042)
XLA Ops:
  1.9 2.0 %collective-permute-start = (bf16[384,128]{1,0:T(8,128)(2,1)S(1)}, bf16[384,128]{1,0:T(8,128)(2,1)S(1)}, u32[]{:S(2)}, u32[]{:S(2)}) collective-permute-start(bf16[384,128]{1,0:T(8,128)(2,1)S(1)} %get-tuple-element.61), channel_id=1, source_target_pairs={{0,1},{1,2},{2,3},{3,0},{4,5},{5,6},{6,7},{7,4},{8,9},{9,10},{10,1... | collective-permute-start | bytes 294920 | tf_op jit(solution)/shard_map/ppermute | solution.py:351
  4.9 2.7 %collective-permute-done.m1 = bf16[384,128]{1,0:T(8,128)(2,1)S(1)} collective-permute-done((bf16[384,128]{1,0:T(8,128)(2,1)S(1)}, bf16[384,128]{1,0:T(8,128)(2,1)S(1)}, u32[]{:S(2)}, u32[]{:S(2)}) %collective-permute-start) | collective-permute-done | bytes 98336 | tf_op jit(solution)/shard_map/ppermute | solution.py:351
  7.6 5.4 %collective-permute-start.4 = (bf16[256,512]{1,0:T(8,128)(2,1)S(1)}, bf16[256,512]{1,0:T(8,128)(2,1)S(1)}, u32[]{:S(2)}, u32[]{:S(2)}) collective-permute-start(bf16[256,512]{1,0:T(8,128)(2,1)S(1)} %get-tuple-element.67.c0), channel_id=1, source_target_pairs={{0,2},{1,3},{2,0},{3,1},{4,6},{5,7},{6,4},{7,5},{8,10},{9,11},{10,... | collective-permute-start | bytes 786440 | tf_op jit(solution)/shard_map/ppermute | solution.py:351
  13.0 1.5 slice_bitcast_fusion
  15.1 10.2 %all_to_all.45.got = bf16[4,14,16,128]{3,2,1,0:T(8,128)(2,1)S(1)} all-to-all(bf16[4,14,16,128]{3,2,1,0:T(8,128)(2,1)S(1)} %shard_map.78), channel_id=1, replica_groups=mesh['z'=8,'x'=4,'core'=2,'panel'=4] {'panel'}, dimensions={0} | all-to-all | bytes 458752 | tf_op jit(solution)/shard_map/all_to_all | solution.py:380
  26.3 2.1 %collective-permute-start.6 = (bf16[256,1024]{1,0:T(8,128)(2,1)S(1)}, bf16[256,1024]{1,0:T(8,128)(2,1)S(1)}, u32[]{:S(2)}, u32[]{:S(2)}) collective-permute-start(bf16[256,1024]{1,0:T(8,128)(2,1)S(1)} %get-tuple-element.75.i0), channel_id=1, source_target_pairs={{0,1},{1,2},{2,3},{3,0},{4,5},{5,6},{6,7},{7,4},{8,9},{9,10},{10,1... | collective-permute-start | bytes 1572872 | tf_op jit(solution)/shard_map/ppermute | solution.py:351
  28.5 17.7 %all_to_all.46.blocks = bf16[8,16,1024]{2,1,0:T(8,128)(2,1)S(1)} all-to-all(bf16[8,16,1024]{2,1,0:T(8,128)(2,1)S(1)} %shard_map.79), channel_id=1, replica_groups=mesh['z'=8,'x'=4,'core'=2,'panel'=4] {'z'}, dimensions={0} | all-to-all | bytes 524288 | tf_op jit(solution)/shard_map/all_to_all | solution.py:362
  46.9 2.2 %collective-permute-start.8 = (bf16[256,1024]{1,0:T(8,128)(2,1)S(1)}, bf16[256,1024]{1,0:T(8,128)(2,1)S(1)}, u32[]{:S(2)}, u32[]{:S(2)}) collective-permute-start(bf16[256,1024]{1,0:T(8,128)(2,1)S(1)} %get-tuple-element.75.i0), channel_id=1, source_target_pairs={{0,2},{1,3},{2,0},{3,1},{4,6},{5,7},{6,4},{7,5},{8,10},{9,11},{10,... | collective-permute-start | bytes 1572872 | tf_op jit(solution)/shard_map/ppermute | solution.py:351
  49.1 11.6 %all_to_all.47.recv = bf16[8,16,1024]{2,1,0:T(8,128)(2,1)S(1)} all-to-all(bf16[8,16,1024]{2,1,0:T(8,128)(2,1)S(1)} %shard_map.80), channel_id=1, replica_groups=mesh['z'=8,'x'=4,'core'=2,'panel'=4] {'x','core'}, dimensions={0} | all-to-all | bytes 524288 | tf_op jit(solution)/shard_map/all_to_all | solution.py:362
  60.7 2.1 %shard_map.81 = (bf16[16,1024]{1,0:T(8,128)(2,1)S(1)}, bf16[8,16,1024]{2,1,0:T(8,128)(2,1)S(1)}, bf16[4,256,1536]{2,1,0:T(8,128)(2,1)S(1)}) custom-call(s32[2,64]{1,0:T(2,128)S(1)} %copy-done.4, bf16[8,16,1024]{2,1,0:T(8,128)(2,1)S(1)} %all_to_all.47.recv, bf16[4,14,16,128]{3,2,1,0:T(8,128)(2,1)S(1)} %all_to_all.45.got, s32[2,64,512]{2,1,0:T(8,128)S(1)} %copy-done, ...), custom_call_target="tpu_custom_call" | custom-call | tf_op jit(solution)/shard_map/pallas_call | solution.py:32
  62.9 1.7 %collective-permute-start.9 = (bf16[256,1024]{1,0:T(8,128)(2,1)S(1)}, bf16[256,1024]{1,0:T(8,128)(2,1)S(1)}, u32[]{:S(2)}, u32[]{:S(2)}) collective-permute-start(bf16[256,1024]{1,0:T(8,128)(2,1)S(1)} %get-tuple-element.90.i0), channel_id=1, source_target_pairs={{0,1},{1,2},{2,3},{3,0},{4,5},{5,6},{6,7},{7,4},{8,9},{9,10},{10,1... | collective-permute-start | bytes 1572872 | tf_op jit(solution)/shard_map/ppermute | solution.py:351
  65.0 13.7 %all_to_all.48.blocks = bf16[8,16,1024]{2,1,0:T(8,128)(2,1)S(1)} all-to-all(bf16[8,16,1024]{2,1,0:T(8,128)(2,1)S(1)} %get-tuple-element.85), channel_id=1, replica_groups=mesh['z'=8,'x'=4,'core'=2,'panel'=4] {'z'}, dimensions={0} | all-to-all | bytes 524288 | tf_op jit(solution)/shard_map/all_to_all | solution.py:362
  79.3 2.1 %collective-permute-start.11 = (bf16[256,1024]{1,0:T(8,128)(2,1)S(1)}, bf16[256,1024]{1,0:T(8,128)(2,1)S(1)}, u32[]{:S(2)}, u32[]{:S(2)}) collective-permute-start(bf16[256,1024]{1,0:T(8,128)(2,1)S(1)} %get-tuple-element.90.i0), channel_id=1, source_target_pairs={{0,2},{1,3},{2,0},{3,1},{4,6},{5,7},{6,4},{7,5},{8,10},{9,11},{10,... | collective-permute-start | bytes 1572872 | tf_op jit(solution)/shard_map/ppermute | solution.py:351
  81.4 10.0 %all_to_all.49.recv = bf16[8,16,1024]{2,1,0:T(8,128)(2,1)S(1)} all-to-all(bf16[8,16,1024]{2,1,0:T(8,128)(2,1)S(1)} %shard_map.82), channel_id=1, replica_groups=mesh['z'=8,'x'=4,'core'=2,'panel'=4] {'x','core'}, dimensions={0} | all-to-all | bytes 524288 | tf_op jit(solution)/shard_map/all_to_all | solution.py:362
  92.3 1.7 %shard_map.83 = (bf16[16,1024]{1,0:T(8,128)(2,1)S(1)}, bf16[8,16,1024]{2,1,0:T(8,128)(2,1)}) custom-call(bf16[8,16,1024]{2,1,0:T(8,128)(2,1)S(1)} %all_to_all.49.recv, bf16[4,14,16,128]{3,2,1,0:T(8,128)(2,1)S(1)} %all_to_all.45.got, bf16[256,1024]{1,0:T(8,128)(2,1)S(1)} %get-tuple-element.90.i0, bf16[256,1024]{1,0:T(8,128)(2,1)S(1)} %collective-permute-done.9.i1, ...), custom_call_target="tpu_custom_call" | custom-call | tf_op jit(solution)/shard_map/pallas_call | solution.py:32
  94.1 3.4 %all-to-all-start.5 = ((bf16[8,16,1024]{2,1,0:T(8,128)(2,1)}), bf16[8,16,1024]{2,1,0:T(8,128)(2,1)S(1)}, u32[]{:S(2)}, u32[]{:S(2)}) async-start(bf16[8,16,1024]{2,1,0:T(8,128)(2,1)} %get-tuple-element.96.s2), calls=%async_computation.5 | async-start | bytes 524288 | tf_op jit(solution)/shard_map/all_to_all | solution.py:418
  97.5 1.9 %shard_map.84 = (bf16[256,768]{1,0:T(8,128)(2,1)S(1)}, bf16[256,768]{1,0:T(8,128)(2,1)S(1)}, bf16[256,768]{1,0:T(8,128)(2,1)S(1)}, bf16[256,768]{1,0:T(8,128)(2,1)S(1)}) custom-call(bf16[2,1,1024,128]{3,2,1,0:T(8,128)(2,1)} %coupling.2, bf16[3,1,256,1024]{3,2,1,0:T(8,128)(2,1)} %inv), custom_call_target="tpu_custom_call" | custom-call | tf_op jit(solution)/shard_map/pallas_call | solution.py:32
  99.4 1.9 %collective-permute-start.12 = (bf16[256,768]{1,0:T(8,128)(2,1)S(1)}, bf16[256,768]{1,0:T(8,128)(2,1)S(1)}, u32[]{:S(2)}, u32[]{:S(2)}) collective-permute-start(bf16[256,768]{1,0:T(8,128)(2,1)S(1)} %get-tuple-element.102), channel_id=1, source_target_pairs={{0,1},{1,2},{2,3},{3,0},{4,5},{5,6},{6,7},{7,4},{8,9},{9,10},{10,1... | collective-permute-start | bytes 1179656 | tf_op jit(solution)/shard_map/ppermute | solution.py:351
  101.7 6.9 %all-to-all-done.5.blocks = bf16[8,16,1024]{2,1,0:T(8,128)(2,1)S(1)} async-done(((bf16[8,16,1024]{2,1,0:T(8,128)(2,1)}), bf16[8,16,1024]{2,1,0:T(8,128)(2,1)S(1)}, u32[]{:S(2)}, u32[]{:S(2)}) %all-to-all-start.5) | async-done | bytes 262176 | tf_op jit(solution)/shard_map/all_to_all | solution.py:418
  109.8 3.4 %all-to-all-start.6 = ((bf16[8,16,1024]{2,1,0:T(8,128)(2,1)}), bf16[8,16,1024]{2,1,0:T(8,128)(2,1)S(1)}, u32[]{:S(2)}, u32[]{:S(2)}) async-start(bf16[8,16,1024]{2,1,0:T(8,128)(2,1)} %shard_map.85), calls=%async_computation.6 | async-start | bytes 524288 | tf_op jit(solution)/shard_map/all_to_all | solution.py:422
  113.3 7.4 %all-to-all-done.6.recv = bf16[8,16,1024]{2,1,0:T(8,128)(2,1)S(1)} async-done(((bf16[8,16,1024]{2,1,0:T(8,128)(2,1)}), bf16[8,16,1024]{2,1,0:T(8,128)(2,1)S(1)}, u32[]{:S(2)}, u32[]{:S(2)}) %all-to-all-start.6) | async-done | bytes 262176 | tf_op jit(solution)/shard_map/all_to_all | solution.py:422
  120.7 3.6 %shard_map.86.s1 = bf16[8,16,1024]{2,1,0:T(8,128)(2,1)} custom-call(s32[2,64]{1,0:T(2,128)S(1)} %copy-done.3, s32[2,64]{1,0:T(2,128)S(1)} %copy-done.4, bf16[8,16,1024]{2,1,0:T(8,128)(2,1)S(1)} %all-to-all-done.6.recv, bf16[16,1024]{1,0:T(8,128)(2,1)S(1)} %get-tuple-element.105.f.f1, s32[2,64,512]{2,1,0:T(8,128)S(1)} %copy-done, bf16[4,256,1536]{2,1,0:T(8,128)(2,1)} %copy-done.1), custom_call_target="tpu_custom_call" | custom-call | tf_op jit(solution)/shard_map/pallas_call | solution.py:32
  124.3 3.4 %all-to-all-start.7 = ((bf16[8,16,1024]{2,1,0:T(8,128)(2,1)}), bf16[8,16,1024]{2,1,0:T(8,128)(2,1)S(1)}, u32[]{:S(2)}, u32[]{:S(2)}) async-start(bf16[8,16,1024]{2,1,0:T(8,128)(2,1)} %shard_map.86.s1), calls=%async_computation.7 | async-start | bytes 524288 | tf_op jit(solution)/shard_map/all_to_all | solution.py:434
  127.7 2.1 %collective-permute-start.14 = (bf16[256,768]{1,0:T(8,128)(2,1)S(1)}, bf16[256,768]{1,0:T(8,128)(2,1)S(1)}, u32[]{:S(2)}, u32[]{:S(2)}) collective-permute-start(bf16[256,768]{1,0:T(8,128)(2,1)S(1)} %get-tuple-element.111), channel_id=1, source_target_pairs={{0,2},{1,3},{2,0},{3,1},{4,6},{5,7},{6,4},{7,5},{8,10},{9,11},{10,... | collective-permute-start | bytes 1179656 | tf_op jit(solution)/shard_map/ppermute | solution.py:351
  129.8 9.6 %all-to-all-done.7.blocks = bf16[8,16,1024]{2,1,0:T(8,128)(2,1)S(1)} async-done(((bf16[8,16,1024]{2,1,0:T(8,128)(2,1)}), bf16[8,16,1024]{2,1,0:T(8,128)(2,1)S(1)}, u32[]{:S(2)}, u32[]{:S(2)}) %all-to-all-start.7) | async-done | bytes 262176 | tf_op jit(solution)/shard_map/all_to_all | solution.py:434
  140.7 3.4 %all-to-all-start.8 = ((bf16[8,16,1024]{2,1,0:T(8,128)(2,1)}), bf16[8,16,1024]{2,1,0:T(8,128)(2,1)S(1)}, u32[]{:S(2)}, u32[]{:S(2)}) async-start(bf16[8,16,1024]{2,1,0:T(8,128)(2,1)} %shard_map.87), calls=%async_computation.8 | async-start | bytes 524288 | tf_op jit(solution)/shard_map/all_to_all | solution.py:437
  144.1 7.4 %all-to-all-done.8.recv = bf16[8,16,1024]{2,1,0:T(8,128)(2,1)S(1)} async-done(((bf16[8,16,1024]{2,1,0:T(8,128)(2,1)}), bf16[8,16,1024]{2,1,0:T(8,128)(2,1)S(1)}, u32[]{:S(2)}, u32[]{:S(2)}) %all-to-all-start.8) | async-done | bytes 262176 | tf_op jit(solution)/shard_map/all_to_all | solution.py:437
  151.6 1.7 %shard_map.88 = (bf16[16,2304]{1,0:T(8,128)(2,1)S(1)}, bf16[16,2304]{1,0:T(8,128)(2,1)S(1)}, bf16[16,2304]{1,0:T(8,128)(2,1)S(1)}, bf16[16,2304]{1,0:T(8,128)(2,1)S(1)}) custom-call(s32[2,64]{1,0:T(2,128)S(1)} %copy-done.3, s32[2,64]{1,0:T(2,128)S(1)} %copy-done.4, bf16[8,16,1024]{2,1,0:T(8,128)(2,1)S(1)} %all-to-all-done.8.recv, ...), custom_call_target="tpu_custom_call" | custom-call | tf_op jit(solution)/shard_map/pallas_call | solution.py:32
  153.2 2.4 %collective-permute-start.15 = (bf16[16,2304]{1,0:T(8,128)(2,1)S(1)}, bf16[16,2304]{1,0:T(8,128)(2,1)S(1)}, u32[]{:S(2)}, u32[]{:S(2)}) collective-permute-start(bf16[16,2304]{1,0:T(8,128)(2,1)S(1)} %get-tuple-element.115), channel_id=1, source_target_pairs={{0,1},{1,2},{2,3},{3,0},{4,5},{5,6},{6,7},{7,4},{8,9},{9,10},{10,1... | collective-permute-start | bytes 221192 | tf_op jit(solution)/shard_map/ppermute | solution.py:351
  155.6 2.0 %collective-permute-start.16 = (bf16[16,2304]{1,0:T(8,128)(2,1)S(1)}, bf16[16,2304]{1,0:T(8,128)(2,1)S(1)}, u32[]{:S(2)}, u32[]{:S(2)}) collective-permute-start(bf16[16,2304]{1,0:T(8,128)(2,1)S(1)} %get-tuple-element.116), channel_id=1, source_target_pairs={{0,2},{1,3},{2,0},{3,1},{4,6},{5,7},{6,4},{7,5},{8,10},{9,11},{10,... | collective-permute-start | bytes 221192 | tf_op jit(solution)/shard_map/ppermute | solution.py:351
  158.4 3.2 %collective-permute-done.16.refs_2_ = bf16[16,2304]{1,0:T(8,128)(2,1)S(1)} collective-permute-done((bf16[16,2304]{1,0:T(8,128)(2,1)S(1)}, bf16[16,2304]{1,0:T(8,128)(2,1)S(1)}, u32[]{:S(2)}, u32[]{:S(2)}) %collective-permute-start.16) | collective-permute-done | bytes 73760 | tf_op jit(solution)/shard_map/ppermute | solution.py:351
  161.6 1.6 collective-permute-done.17.refs_3_
  (41 shorter events, 11.1 us)
Async XLA Ops:
  1.9 5.7 %collective-permute-start = (bf16[384,128]{1,0:T(8,128)(2,1)S(1)}, bf16[384,128]{1,0:T(8,128)(2,1)S(1)}, u32[]{:S(2)}, u32[]{:S(2)}) collective-permute-start(bf16[384,128]{1,0:T(8,128)(2,1)S(1)} %get-tuple-element.61), channel_id=1, source_target_pairs={{0,1},{1,2},{2,3},{3,0},{4,5},{5,6},{6,7},{7,4},{8,9},{9,10},{10,1... | collective-permute-start | bytes 294920 | tf_op jit(solution)/shard_map/ppermute | solution.py:351
  4.0 10.6 %collective-permute-start.1 = (bf16[384,128]{1,0:T(8,128)(2,1)S(1)}, bf16[384,128]{1,0:T(8,128)(2,1)S(1)}, u32[]{:S(2)}, u32[]{:S(2)}) collective-permute-start(bf16[384,128]{1,0:T(8,128)(2,1)S(1)} %get-tuple-element.64), channel_id=1, source_target_pairs={{0,2},{1,3},{2,0},{3,1},{4,6},{5,7},{6,4},{7,5},{8,10},{9,11},{10,... | collective-permute-start | bytes 294920 | tf_op jit(solution)/shard_map/ppermute | solution.py:351
  4.8 9.7 %collective-permute-start.2 = (bf16[384,128]{1,0:T(8,128)(2,1)S(1)}, bf16[384,128]{1,0:T(8,128)(2,1)S(1)}, u32[]{:S(2)}, u32[]{:S(2)}) collective-permute-start(bf16[384,128]{1,0:T(8,128)(2,1)S(1)} %get-tuple-element.65), channel_id=1, source_target_pairs={{0,3},{1,0},{2,1},{3,2},{4,7},{5,4},{6,5},{7,6},{8,11},{9,8},{10,9... | collective-permute-start | bytes 294920 | tf_op jit(solution)/shard_map/ppermute | solution.py:351
  7.6 7.0 %copy-start.2 = (bf16[3,1,64,256]{3,2,1,0:T(8,128)(2,1)S(1)}, bf16[3,1,64,256]{3,2,1,0:T(8,128)(2,1)}, u32[]{:S(2)}) copy-start(bf16[3,1,64,256]{3,2,1,0:T(8,128)(2,1)} %rhs.3) | copy-start | bytes 294916
  7.6 17.7 %collective-permute-start.5 = (bf16[256,512]{1,0:T(8,128)(2,1)S(1)}, bf16[256,512]{1,0:T(8,128)(2,1)S(1)}, u32[]{:S(2)}, u32[]{:S(2)}) collective-permute-start(bf16[256,512]{1,0:T(8,128)(2,1)S(1)} %get-tuple-element.67.c0), channel_id=1, source_target_pairs={{0,3},{1,0},{2,1},{3,2},{4,7},{5,4},{6,5},{7,6},{8,11},{9,8},{10,9... | collective-permute-start | bytes 786440 | tf_op jit(solution)/shard_map/ppermute | solution.py:351
  7.6 17.7 %collective-permute-start.4 = (bf16[256,512]{1,0:T(8,128)(2,1)S(1)}, bf16[256,512]{1,0:T(8,128)(2,1)S(1)}, u32[]{:S(2)}, u32[]{:S(2)}) collective-permute-start(bf16[256,512]{1,0:T(8,128)(2,1)S(1)} %get-tuple-element.67.c0), channel_id=1, source_target_pairs={{0,2},{1,3},{2,0},{3,1},{4,6},{5,7},{6,4},{7,5},{8,10},{9,11},{10,... | collective-permute-start | bytes 786440 | tf_op jit(solution)/shard_map/ppermute | solution.py:351
  13.0 12.3 %collective-permute-start.3 = (bf16[256,512]{1,0:T(8,128)(2,1)S(1)}, bf16[256,512]{1,0:T(8,128)(2,1)S(1)}, u32[]{:S(2)}, u32[]{:S(2)}) collective-permute-start(bf16[256,512]{1,0:T(8,128)(2,1)S(1)} %get-tuple-element.67.c0), channel_id=1, source_target_pairs={{0,1},{1,2},{2,3},{3,0},{4,5},{5,6},{6,7},{7,4},{8,9},{9,10},{10,1... | collective-permute-start | bytes 786440 | tf_op jit(solution)/shard_map/ppermute | solution.py:351
  14.5 10.8 %copy-start = (s32[2,64,512]{2,1,0:T(8,128)S(1)}, s32[2,64,512]{2,1,0:T(8,128)}, u32[]{:S(2)}) copy-start(s32[2,64,512]{2,1,0:T(8,128)} %lists.7) | copy-start | bytes 786436
  14.5 10.8 %copy-start.4 = (s32[2,64]{1,0:T(2,128)S(1)}, s32[2,64]{1,0:T(2,128)}, u32[]{:S(2)}) copy-start(s32[2,64]{1,0:T(2,128)} %counts.7) | copy-start | bytes 1540
  14.5 31.7 %copy-start.3 = (s32[2,64]{1,0:T(2,128)S(1)}, s32[2,64]{1,0:T(2,128)}, u32[]{:S(2)}) copy-start(s32[2,64]{1,0:T(2,128)} %parents.11) | copy-start | bytes 1540
  26.3 19.8 %collective-permute-start.6 = (bf16[256,1024]{1,0:T(8,128)(2,1)S(1)}, bf16[256,1024]{1,0:T(8,128)(2,1)S(1)}, u32[]{:S(2)}, u32[]{:S(2)}) collective-permute-start(bf16[256,1024]{1,0:T(8,128)(2,1)S(1)} %get-tuple-element.75.i0), channel_id=1, source_target_pairs={{0,1},{1,2},{2,3},{3,0},{4,5},{5,6},{6,7},{7,4},{8,9},{9,10},{10,1... | collective-permute-start | bytes 1572872 | tf_op jit(solution)/shard_map/ppermute | solution.py:351
  28.5 17.7 %collective-permute-start.7 = (bf16[256,1024]{1,0:T(8,128)(2,1)S(1)}, bf16[256,1024]{1,0:T(8,128)(2,1)S(1)}, u32[]{:S(2)}, u32[]{:S(2)}) collective-permute-start(bf16[256,1024]{1,0:T(8,128)(2,1)S(1)} %get-tuple-element.75.i0), channel_id=1, source_target_pairs={{0,3},{1,0},{2,1},{3,2},{4,7},{5,4},{6,5},{7,6},{8,11},{9,8},{10,9... | collective-permute-start | bytes 1572872 | tf_op jit(solution)/shard_map/ppermute | solution.py:351
  46.9 13.9 %collective-permute-start.8 = (bf16[256,1024]{1,0:T(8,128)(2,1)S(1)}, bf16[256,1024]{1,0:T(8,128)(2,1)S(1)}, u32[]{:S(2)}, u32[]{:S(2)}) collective-permute-start(bf16[256,1024]{1,0:T(8,128)(2,1)S(1)} %get-tuple-element.75.i0), channel_id=1, source_target_pairs={{0,2},{1,3},{2,0},{3,1},{4,6},{5,7},{6,4},{7,5},{8,10},{9,11},{10,... | collective-permute-start | bytes 1572872 | tf_op jit(solution)/shard_map/ppermute | solution.py:351
  62.8 31.2 %copy-start.1 = (bf16[4,256,1536]{2,1,0:T(8,128)(2,1)}, bf16[4,256,1536]{2,1,0:T(8,128)(2,1)S(1)}, u32[]{:S(2)}) copy-start(bf16[4,256,1536]{2,1,0:T(8,128)(2,1)S(1)} %get-tuple-element.106.keep) | copy-start | bytes 9437188
  62.9 15.8 %collective-permute-start.9 = (bf16[256,1024]{1,0:T(8,128)(2,1)S(1)}, bf16[256,1024]{1,0:T(8,128)(2,1)S(1)}, u32[]{:S(2)}, u32[]{:S(2)}) collective-permute-start(bf16[256,1024]{1,0:T(8,128)(2,1)S(1)} %get-tuple-element.90.i0), channel_id=1, source_target_pairs={{0,1},{1,2},{2,3},{3,0},{4,5},{5,6},{6,7},{7,4},{8,9},{9,10},{10,1... | collective-permute-start | bytes 1572872 | tf_op jit(solution)/shard_map/ppermute | solution.py:351
  64.6 14.1 %collective-permute-start.10 = (bf16[256,1024]{1,0:T(8,128)(2,1)S(1)}, bf16[256,1024]{1,0:T(8,128)(2,1)S(1)}, u32[]{:S(2)}, u32[]{:S(2)}) collective-permute-start(bf16[256,1024]{1,0:T(8,128)(2,1)S(1)} %get-tuple-element.90.i0), channel_id=1, source_target_pairs={{0,3},{1,0},{2,1},{3,2},{4,7},{5,4},{6,5},{7,6},{8,11},{9,8},{10,9... | collective-permute-start | bytes 1572872 | tf_op jit(solution)/shard_map/ppermute | solution.py:351
  79.3 13.0 %collective-permute-start.11 = (bf16[256,1024]{1,0:T(8,128)(2,1)S(1)}, bf16[256,1024]{1,0:T(8,128)(2,1)S(1)}, u32[]{:S(2)}, u32[]{:S(2)}) collective-permute-start(bf16[256,1024]{1,0:T(8,128)(2,1)S(1)} %get-tuple-element.90.i0), channel_id=1, source_target_pairs={{0,2},{1,3},{2,0},{3,1},{4,6},{5,7},{6,4},{7,5},{8,10},{9,11},{10,... | collective-permute-start | bytes 1572872 | tf_op jit(solution)/shard_map/ppermute | solution.py:351
  94.1 14.5 %all-to-all-start.5 = ((bf16[8,16,1024]{2,1,0:T(8,128)(2,1)}), bf16[8,16,1024]{2,1,0:T(8,128)(2,1)S(1)}, u32[]{:S(2)}, u32[]{:S(2)}) async-start(bf16[8,16,1024]{2,1,0:T(8,128)(2,1)} %get-tuple-element.96.s2), calls=%async_computation.5 | async-start | bytes 524288 | tf_op jit(solution)/shard_map/all_to_all | solution.py:418
  99.4 13.9 %collective-permute-start.12 = (bf16[256,768]{1,0:T(8,128)(2,1)S(1)}, bf16[256,768]{1,0:T(8,128)(2,1)S(1)}, u32[]{:S(2)}, u32[]{:S(2)}) collective-permute-start(bf16[256,768]{1,0:T(8,128)(2,1)S(1)} %get-tuple-element.102), channel_id=1, source_target_pairs={{0,1},{1,2},{2,3},{3,0},{4,5},{5,6},{6,7},{7,4},{8,9},{9,10},{10,1... | collective-permute-start | bytes 1179656 | tf_op jit(solution)/shard_map/ppermute | solution.py:351
  101.3 12.0 %collective-permute-start.13 = (bf16[256,768]{1,0:T(8,128)(2,1)S(1)}, bf16[256,768]{1,0:T(8,128)(2,1)S(1)}, u32[]{:S(2)}, u32[]{:S(2)}) collective-permute-start(bf16[256,768]{1,0:T(8,128)(2,1)S(1)} %get-tuple-element.103), channel_id=1, source_target_pairs={{0,3},{1,0},{2,1},{3,2},{4,7},{5,4},{6,5},{7,6},{8,11},{9,8},{10,9... | collective-permute-start | bytes 1179656 | tf_op jit(solution)/shard_map/ppermute | solution.py:351
  109.8 10.9 %all-to-all-start.6 = ((bf16[8,16,1024]{2,1,0:T(8,128)(2,1)}), bf16[8,16,1024]{2,1,0:T(8,128)(2,1)S(1)}, u32[]{:S(2)}, u32[]{:S(2)}) async-start(bf16[8,16,1024]{2,1,0:T(8,128)(2,1)} %shard_map.85), calls=%async_computation.6 | async-start | bytes 524288 | tf_op jit(solution)/shard_map/all_to_all | solution.py:422
  124.3 15.1 %all-to-all-start.7 = ((bf16[8,16,1024]{2,1,0:T(8,128)(2,1)}), bf16[8,16,1024]{2,1,0:T(8,128)(2,1)S(1)}, u32[]{:S(2)}, u32[]{:S(2)}) async-start(bf16[8,16,1024]{2,1,0:T(8,128)(2,1)} %shard_map.86.s1), calls=%async_computation.7 | async-start | bytes 524288 | tf_op jit(solution)/shard_map/all_to_all | solution.py:434
  127.7 16.4 %collective-permute-start.14 = (bf16[256,768]{1,0:T(8,128)(2,1)S(1)}, bf16[256,768]{1,0:T(8,128)(2,1)S(1)}, u32[]{:S(2)}, u32[]{:S(2)}) collective-permute-start(bf16[256,768]{1,0:T(8,128)(2,1)S(1)} %get-tuple-element.111), channel_id=1, source_target_pairs={{0,2},{1,3},{2,0},{3,1},{4,6},{5,7},{6,4},{7,5},{8,10},{9,11},{10,... | collective-permute-start | bytes 1179656 | tf_op jit(solution)/shard_map/ppermute | solution.py:351
  140.7 10.9 %all-to-all-start.8 = ((bf16[8,16,1024]{2,1,0:T(8,128)(2,1)}), bf16[8,16,1024]{2,1,0:T(8,128)(2,1)S(1)}, u32[]{:S(2)}, u32[]{:S(2)}) async-start(bf16[8,16,1024]{2,1,0:T(8,128)(2,1)} %shard_map.87), calls=%async_computation.8 | async-start | bytes 524288 | tf_op jit(solution)/shard_map/all_to_all | solution.py:437
  153.2 5.1 %collective-permute-start.15 = (bf16[16,2304]{1,0:T(8,128)(2,1)S(1)}, bf16[16,2304]{1,0:T(8,128)(2,1)S(1)}, u32[]{:S(2)}, u32[]{:S(2)}) collective-permute-start(bf16[16,2304]{1,0:T(8,128)(2,1)S(1)} %get-tuple-element.115), channel_id=1, source_target_pairs={{0,1},{1,2},{2,3},{3,0},{4,5},{5,6},{6,7},{7,4},{8,9},{9,10},{10,1... | collective-permute-start | bytes 221192 | tf_op jit(solution)/shard_map/ppermute | solution.py:351
  155.6 6.0 %collective-permute-start.16 = (bf16[16,2304]{1,0:T(8,128)(2,1)S(1)}, bf16[16,2304]{1,0:T(8,128)(2,1)S(1)}, u32[]{:S(2)}, u32[]{:S(2)}) collective-permute-start(bf16[16,2304]{1,0:T(8,128)(2,1)S(1)} %get-tuple-element.116), channel_id=1, source_target_pairs={{0,2},{1,3},{2,0},{3,1},{4,6},{5,7},{6,4},{7,5},{8,10},{9,11},{10,... | collective-permute-start | bytes 221192 | tf_op jit(solution)/shard_map/ppermute | solution.py:351
  157.6 5.6 %collective-permute-start.17 = (bf16[16,2304]{1,0:T(8,128)(2,1)S(1)}, bf16[16,2304]{1,0:T(8,128)(2,1)S(1)}, u32[]{:S(2)}, u32[]{:S(2)}) collective-permute-start(bf16[16,2304]{1,0:T(8,128)(2,1)S(1)} %get-tuple-element.117), channel_id=1, source_target_pairs={{0,3},{1,0},{2,1},{3,2},{4,7},{5,4},{6,5},{7,6},{8,11},{9,8},{10,9... | collective-permute-start | bytes 221192 | tf_op jit(solution)/shard_map/ppermute | solution.py:351

commit v6 on v5

--- a/solution.py
+++ b/solution.py
@@ -96,7 +96,8 @@
             source = coupling.at[0, 0, pl.ds(part * rows, rows)]
             copies.append((source, out.at[:, pl.ds(part * width, width)]))
         cols = pl.ds(pl.multiple_of(target * rows, rows), rows)
-        copies.append((inv.at[0, 0, :, cols], out.at[:, pl.ds(parts * width, rows)]))
+        for start in range(parts * width, out.shape[1], rows):
+            copies.append((inv.at[0, 0, :, cols], out.at[:, pl.ds(start, rows)]))
     copies = [pltpu.make_async_copy(a, b, sems.at[i]) for i, (a, b) in enumerate(copies)]
     for copy in copies:
         copy.start()
@@ -207,7 +208,7 @@
         out[:, pl.ds(pl.multiple_of(order(k, len(blocks)) * width, width), width)] = total
 
 
-def lessened(level, f, recv, parents, placed, blocks, first, picked):
+def lessened(level, f, recv, parents, placed, blocks, first, picked, place_of):
     _, _, leaf = leaf_place()
     above = recv[lax.rem(parents[level, leaf], GROUP)]
     picked[...] = mul(above, placed).astype(BF)
@@ -218,7 +219,7 @@
         lanes = slice(first + part * width, first + (part + 1) * width)
         total = None
         for k, ref in enumerate(blocks):
-            start = pl.multiple_of(order(k, len(blocks)) * width, width)
+            start = pl.multiple_of(place_of(k) * width, width)
             term = mul_t(picked[:, pl.ds(start, width)], ref[:, lanes])
             total = term if total is None else total + term
         pieces.append(total)
@@ -238,7 +239,8 @@
         for part, (source, span) in enumerate(
             ((inverse[k], pl.ds(0, cols)), (blocks[k], pl.ds(cols, c0.shape[1])))
         ):
-            copies.append(pltpu.make_async_copy(source, keep.at[k, :, span], sems.at[k, part]))
+            target = keep.at[order(k, len(blocks)), :, span]
+            copies.append(pltpu.make_async_copy(source, target, sems.at[k, part]))
     for copy in copies:
         copy.start()
     resid = (whole(got, 1).astype(F32) - summed(recv)).astype(BF)
@@ -276,24 +278,32 @@
 
 def down1_body(parents, counts, recv, f, lists, keep, out, picked, red, held, sems):
     cols = red.shape[1]
-    parts = (pl.ds(cols, held.shape[2] - cols), pl.ds(0, cols))
-    copies = [
-        [
-            pltpu.make_async_copy(keep.at[k, :, span], held.at[k, :, span], sems.at[k, part])
-            for k in range(keep.shape[0])
-        ]
-        for part, span in enumerate(parts)
-    ]
-    for copy in copies[0] + copies[1]:
-        copy.start()
-    blocks = [held.at[k] for k in range(keep.shape[0])]
+    rows = keep.shape[1]
+    panels = keep.shape[0]
+
+    def copy(q, part, span):
+        return pltpu.make_async_copy(keep.at[q, :, span], held.at[q, :, span], sems.at[q, part])
+
+    couplings = [copy(q, 0, pl.ds(cols, held.shape[2] - cols)) for q in range(panels)]
+    inverse = [copy(q, 1, pl.ds(0, (q + 1) * rows)) for q in range(panels)]
+    for started in couplings + inverse:
+        started.start()
+    blocks = [held.at[q] for q in range(panels)]
     placed = place(1, counts, lists, cols)
-    for copy in copies[0]:
-        copy.wait()
-    red[...] = lessened(1, f[...], recv, parents, placed, blocks, cols, picked)
-    for copy in copies[1]:
-        copy.wait()
-    to_all(out, backward(red, blocks))
+    for started in couplings:
+        started.wait()
+    red[...] = lessened(1, f[...], recv, parents, placed, blocks, cols, picked, lambda q: q)
+    for started in inverse:
+        started.wait()
+    pieces = []
+    for part in range(panels):
+        lanes = slice(part * rows, (part + 1) * rows)
+        total = None
+        for q in range(part, panels):
+            term = mul(red[:, q * rows : (q + 1) * rows], held[q, :, lanes])
+            total = term if total is None else total + term
+        pieces.append(total)
+    to_all(out, jnp.concatenate(pieces, axis=1).astype(BF))
 
 
 def down0_body(
@@ -305,7 +315,9 @@
     quarter = width // len(outs)
     f0[...] = whole(got, 0)
     placed = place(0, counts, lists, width)
-    red = lessened(0, f0[...], recv, parents, placed, (b0, b1, b2, b3), 0, scratch)
+    red = lessened(0, f0[...], recv, parents, placed, (b0, b1, b2, b3), 0, scratch,
+        lambda k: order(k, 4),
+    )
     for k, out in enumerate(outs):
         target = lax.rem(lax.axis_index("panel") + k, len(outs))
         cols = pl.ds(pl.multiple_of(target * quarter, quarter), quarter)
@@ -319,6 +331,7 @@
 def last_body(*refs):
     panels = (len(refs) - 3) // 2
     ends, cols = refs[:panels], refs[panels : 2 * panels]
+    first = cols[0].shape[1] - cols[0].shape[0]
     fwd, sol, reds = refs[2 * panels :]
     width = reds.shape[1]
     quarter = width // panels
@@ -335,7 +348,7 @@
     for k in range(panels):
         q = order(k, panels)
         part = mul(
-            reds[:, pl.ds(pl.multiple_of(q * quarter, quarter), quarter)], cols[k][:, -quarter:]
+            reds[:, pl.ds(pl.multiple_of(q * quarter, quarter), quarter)], cols[k][:, first : first + quarter]
         )
         total = part if total is None else total + part
     sol[0, 0] = total.astype(BF)
@@ -410,9 +423,11 @@
     )
     s, inv_late, near_coupling = after((s2, inv_diag, coupling))
     w0 = call(
-        last_weights_body, [sds(tall, panels * half + tall)] * panels, near_coupling, inv_late,
+        last_weights_body,
+        [sds(tall, panels * half + (2 if k == 2 else 1) * tall) for k in range(panels)],
+        near_coupling, inv_late,
         specs=[HBM] * 2, outs_at=HBM,
-        scratch=[pltpu.SemaphoreType.DMA((panels * (panels + 1),))],
+        scratch=[pltpu.SemaphoreType.DMA((panels * (panels + 1) + 1,))],
     )
     w0 = [*w0]
     s = lax.all_to_all(s, "z", 0, 0)
@@ -429,9 +444,7 @@
             pltpu.SemaphoreType.DMA((panels, 2)),
         ],
     )
-    s, far2 = after((s1, w0[2]))
-    w02 = shifted(far2, 2)
-    s = lax.all_to_all(s, "z", 0, 0)
+    s, w02 = exchange(s1, "z", [w0[2]], [2])
     w0 = (w0[0], w01, w02, w03)
     s = route(s, 0, parents)
     s = lax.all_to_all(s, ("x", "core"), 0, 0)

time: 165 us -> 163 us (0.988)
  blocking collectives: 63.2 us -> 87 us
  waiting for transfers between devices: 40.6 us -> 23.6 us
  starting transfers between devices: 39.4 us -> 32.1 us
    all_to_all x4 -> x5, blocking collectives: 53 us -> 66.9 us  [exchange(): x = lax.all_to_all(x, axes, 0, 0)]
    all_to_all x0 -> x1, blocking collectives: none -> 9.95 us  [local(): s = lax.all_to_all(s, ('x', 'core'), 0, 0)]
    all_to_all x2 -> x1, waiting for transfers between devices: 16.5 us -> 6.79 us  [local(): s = lax.all_to_all(s, 'z', 0, 0)]
    all_to_all x2 -> x1, waiting for transfers between devices: 14.9 us -> 7.44 us  [local(): s = lax.all_to_all(s, ('x', 'core'), 0, 0)]
    all_to_all x2 -> x1, starting transfers between devices: 6.83 us -> 3.41 us  [local(): s = lax.all_to_all(s, 'z', 0, 0)]
    all_to_all x2 -> x1, starting transfers between devices: 6.82 us -> 3.41 us  [local(): s = lax.all_to_all(s, ('x', 'core'), 0, 0)]
  transfers between devices with their start and end apart: 22 -> 20, of which waited for: 9 -> 7; matrix products, arithmetic and copies ran while one was open for 1% -> 1% of each run, Pallas kernels for 3% -> 2%
where the time goes in v6:
time: 163 us; the launch traced here: 162 us
  blocking collectives  87 us (53%)
  starting transfers between devices  32.1 us (20%)
  waiting for transfers between devices  23.6 us (14%)
  Pallas kernels  17 us (10%)
    all_to_all x5, blocking collectives, exchange(): x = lax.all_to_all(x, axes, 0, 0)  66.9 us
    ppermute x18, starting transfers between devices, shifted(): lax.ppermute(x, 'panel', [(i, (i + k) % panels) for i in range(panels)])  25.3 us
    pallas_call x13, Pallas kernels, call(): pl.pallas_call(body, out_shape=tuple(outs) if isinstance(outs, list) else...  17 us
    all_to_all x1, blocking collectives, local(): got = lax.all_to_all(send, 'panel', 0, 0)  10.2 us
    all_to_all x1, blocking collectives, local(): s = lax.all_to_all(s, ('x', 'core'), 0, 0)  9.95 us
    ppermute x18, waiting for transfers between devices, shifted(): lax.ppermute(x, 'panel', [(i, (i + k) % panels) for i in range(panels)])  9.33 us
    all_to_all x1, waiting for transfers between devices, local(): s = lax.all_to_all(s, ('x', 'core'), 0, 0)  7.44 us
    all_to_all x1, waiting for transfers between devices, local(): s = lax.all_to_all(s, 'z', 0, 0)  6.79 us
  transfers between devices with their start and end apart: 20, of which 7 were waited for; matrix products, arithmetic and copies ran while one was open for 1% of the time, Pallas kernels for 2%

profile of v6, /device:TPU:24, one launch (start us, length us, event | category | flops | bytes accessed | tf_op | source)
XLA Modules:
  0.0 162.1 jit_solution(6578853189583732507)
XLA Ops:
  0.6 1.3 shard_map.77
  1.9 2.0 %collective-permute-start = (bf16[384,128]{1,0:T(8,128)(2,1)S(1)}, bf16[384,128]{1,0:T(8,128)(2,1)S(1)}, u32[]{:S(2)}, u32[]{:S(2)}) collective-permute-start(bf16[384,128]{1,0:T(8,128)(2,1)S(1)} %get-tuple-element.63), channel_id=1, source_target_pairs={{0,1},{1,2},{2,3},{3,0},{4,5},{5,6},{6,7},{7,4},{8,9},{9,10},{10,1... | collective-permute-start | bytes 294920 | tf_op jit(solution)/shard_map/ppermute | solution.py:364
  4.9 2.7 %collective-permute-done.m1 = bf16[384,128]{1,0:T(8,128)(2,1)S(1)} collective-permute-done((bf16[384,128]{1,0:T(8,128)(2,1)S(1)}, bf16[384,128]{1,0:T(8,128)(2,1)S(1)}, u32[]{:S(2)}, u32[]{:S(2)}) %collective-permute-start) | collective-permute-done | bytes 98336 | tf_op jit(solution)/shard_map/ppermute | solution.py:364
  7.6 5.4 %collective-permute-start.4 = (bf16[256,512]{1,0:T(8,128)(2,1)S(1)}, bf16[256,512]{1,0:T(8,128)(2,1)S(1)}, u32[]{:S(2)}, u32[]{:S(2)}) collective-permute-start(bf16[256,512]{1,0:T(8,128)(2,1)S(1)} %get-tuple-element.69.c0), channel_id=1, source_target_pairs={{0,2},{1,3},{2,0},{3,1},{4,6},{5,7},{6,4},{7,5},{8,10},{9,11},{10,... | collective-permute-start | bytes 786440 | tf_op jit(solution)/shard_map/ppermute | solution.py:364
  13.0 1.5 slice_bitcast_fusion
  15.1 10.2 %all_to_all.45.got = bf16[4,14,16,128]{3,2,1,0:T(8,128)(2,1)S(1)} all-to-all(bf16[4,14,16,128]{3,2,1,0:T(8,128)(2,1)S(1)} %shard_map.78), channel_id=1, replica_groups=mesh['z'=8,'x'=4,'core'=2,'panel'=4] {'panel'}, dimensions={0} | all-to-all | bytes 458752 | tf_op jit(solution)/shard_map/all_to_all | solution.py:393
  25.3 1.0 shard_map.79
  26.3 2.1 %collective-permute-start.6 = (bf16[256,1024]{1,0:T(8,128)(2,1)S(1)}, bf16[256,1024]{1,0:T(8,128)(2,1)S(1)}, u32[]{:S(2)}, u32[]{:S(2)}) collective-permute-start(bf16[256,1024]{1,0:T(8,128)(2,1)S(1)} %get-tuple-element.77.i0), channel_id=1, source_target_pairs={{0,1},{1,2},{2,3},{3,0},{4,5},{5,6},{6,7},{7,4},{8,9},{9,10},{10,1... | collective-permute-start | bytes 1572872 | tf_op jit(solution)/shard_map/ppermute | solution.py:364
  28.5 17.7 %all_to_all.46.blocks = bf16[8,16,1024]{2,1,0:T(8,128)(2,1)S(1)} all-to-all(bf16[8,16,1024]{2,1,0:T(8,128)(2,1)S(1)} %shard_map.79), channel_id=1, replica_groups=mesh['z'=8,'x'=4,'core'=2,'panel'=4] {'z'}, dimensions={0} | all-to-all | bytes 524288 | tf_op jit(solution)/shard_map/all_to_all | solution.py:375
  46.9 2.2 %collective-permute-start.8 = (bf16[256,1024]{1,0:T(8,128)(2,1)S(1)}, bf16[256,1024]{1,0:T(8,128)(2,1)S(1)}, u32[]{:S(2)}, u32[]{:S(2)}) collective-permute-start(bf16[256,1024]{1,0:T(8,128)(2,1)S(1)} %get-tuple-element.77.i0), channel_id=1, source_target_pairs={{0,2},{1,3},{2,0},{3,1},{4,6},{5,7},{6,4},{7,5},{8,10},{9,11},{10,... | collective-permute-start | bytes 1572872 | tf_op jit(solution)/shard_map/ppermute | solution.py:364
  49.1 11.6 %all_to_all.47.recv = bf16[8,16,1024]{2,1,0:T(8,128)(2,1)S(1)} all-to-all(bf16[8,16,1024]{2,1,0:T(8,128)(2,1)S(1)} %shard_map.80), channel_id=1, replica_groups=mesh['z'=8,'x'=4,'core'=2,'panel'=4] {'x','core'}, dimensions={0} | all-to-all | bytes 524288 | tf_op jit(solution)/shard_map/all_to_all | solution.py:375
  60.7 2.1 %shard_map.81 = (bf16[16,1024]{1,0:T(8,128)(2,1)S(1)}, bf16[8,16,1024]{2,1,0:T(8,128)(2,1)S(1)}, bf16[4,256,1536]{2,1,0:T(8,128)(2,1)S(1)}) custom-call(s32[2,64]{1,0:T(2,128)S(1)} %copy-done.4, bf16[8,16,1024]{2,1,0:T(8,128)(2,1)S(1)} %all_to_all.47.recv, bf16[4,14,16,128]{3,2,1,0:T(8,128)(2,1)S(1)} %all_to_all.45.got, s32[2,64,512]{2,1,0:T(8,128)S(1)} %copy-done, ...), custom_call_target="tpu_custom_call" | custom-call | tf_op jit(solution)/shard_map/pallas_call | solution.py:32
  62.9 1.7 %collective-permute-start.9 = (bf16[256,1024]{1,0:T(8,128)(2,1)S(1)}, bf16[256,1024]{1,0:T(8,128)(2,1)S(1)}, u32[]{:S(2)}, u32[]{:S(2)}) collective-permute-start(bf16[256,1024]{1,0:T(8,128)(2,1)S(1)} %get-tuple-element.92.i0), channel_id=1, source_target_pairs={{0,1},{1,2},{2,3},{3,0},{4,5},{5,6},{6,7},{7,4},{8,9},{9,10},{10,1... | collective-permute-start | bytes 1572872 | tf_op jit(solution)/shard_map/ppermute | solution.py:364
  65.0 13.7 %all_to_all.48.blocks = bf16[8,16,1024]{2,1,0:T(8,128)(2,1)S(1)} all-to-all(bf16[8,16,1024]{2,1,0:T(8,128)(2,1)S(1)} %get-tuple-element.87), channel_id=1, replica_groups=mesh['z'=8,'x'=4,'core'=2,'panel'=4] {'z'}, dimensions={0} | all-to-all | bytes 524288 | tf_op jit(solution)/shard_map/all_to_all | solution.py:375
  79.3 2.1 %collective-permute-start.11 = (bf16[256,1024]{1,0:T(8,128)(2,1)S(1)}, bf16[256,1024]{1,0:T(8,128)(2,1)S(1)}, u32[]{:S(2)}, u32[]{:S(2)}) collective-permute-start(bf16[256,1024]{1,0:T(8,128)(2,1)S(1)} %get-tuple-element.92.i0), channel_id=1, source_target_pairs={{0,2},{1,3},{2,0},{3,1},{4,6},{5,7},{6,4},{7,5},{8,10},{9,11},{10,... | collective-permute-start | bytes 1572872 | tf_op jit(solution)/shard_map/ppermute | solution.py:364
  81.4 10.0 %all_to_all.49.recv = bf16[8,16,1024]{2,1,0:T(8,128)(2,1)S(1)} all-to-all(bf16[8,16,1024]{2,1,0:T(8,128)(2,1)S(1)} %shard_map.82), channel_id=1, replica_groups=mesh['z'=8,'x'=4,'core'=2,'panel'=4] {'x','core'}, dimensions={0} | all-to-all | bytes 524288 | tf_op jit(solution)/shard_map/all_to_all | solution.py:375
  92.3 1.7 %shard_map.83 = (bf16[16,1024]{1,0:T(8,128)(2,1)S(1)}, bf16[8,16,1024]{2,1,0:T(8,128)(2,1)}) custom-call(bf16[8,16,1024]{2,1,0:T(8,128)(2,1)S(1)} %all_to_all.49.recv, bf16[4,14,16,128]{3,2,1,0:T(8,128)(2,1)S(1)} %all_to_all.45.got, bf16[256,1024]{1,0:T(8,128)(2,1)S(1)} %get-tuple-element.92.i0, bf16[256,1024]{1,0:T(8,128)(2,1)S(1)} %collective-permute-done.9.i1, ...), custom_call_target="tpu_custom_call" | custom-call | tf_op jit(solution)/shard_map/pallas_call | solution.py:32
  94.1 3.4 %all-to-all-start.5 = ((bf16[8,16,1024]{2,1,0:T(8,128)(2,1)}), bf16[8,16,1024]{2,1,0:T(8,128)(2,1)S(1)}, u32[]{:S(2)}, u32[]{:S(2)}) async-start(bf16[8,16,1024]{2,1,0:T(8,128)(2,1)} %get-tuple-element.98.s2), calls=%async_computation.5 | async-start | bytes 524288 | tf_op jit(solution)/shard_map/all_to_all | solution.py:433
  97.5 2.0 %shard_map.84 = (bf16[256,768]{1,0:T(8,128)(2,1)S(1)}, bf16[256,768]{1,0:T(8,128)(2,1)S(1)}, bf16[256,1024]{1,0:T(8,128)(2,1)S(1)}, bf16[256,768]{1,0:T(8,128)(2,1)S(1)}) custom-call(bf16[2,1,1024,128]{3,2,1,0:T(8,128)(2,1)} %coupling.2, bf16[3,1,256,1024]{3,2,1,0:T(8,128)(2,1)} %inv), custom_call_target="tpu_custom_call" | custom-call | tf_op jit(solution)/shard_map/pallas_call | solution.py:32
  99.5 1.9 %collective-permute-start.12 = (bf16[256,768]{1,0:T(8,128)(2,1)S(1)}, bf16[256,768]{1,0:T(8,128)(2,1)S(1)}, u32[]{:S(2)}, u32[]{:S(2)}) collective-permute-start(bf16[256,768]{1,0:T(8,128)(2,1)S(1)} %get-tuple-element.104), channel_id=1, source_target_pairs={{0,1},{1,2},{2,3},{3,0},{4,5},{5,6},{6,7},{7,4},{8,9},{9,10},{10,1... | collective-permute-start | bytes 1179656 | tf_op jit(solution)/shard_map/ppermute | solution.py:364
  101.8 6.8 %all-to-all-done.5.blocks = bf16[8,16,1024]{2,1,0:T(8,128)(2,1)S(1)} async-done(((bf16[8,16,1024]{2,1,0:T(8,128)(2,1)}), bf16[8,16,1024]{2,1,0:T(8,128)(2,1)S(1)}, u32[]{:S(2)}, u32[]{:S(2)}) %all-to-all-start.5) | async-done | bytes 262176 | tf_op jit(solution)/shard_map/all_to_all | solution.py:433
  108.6 1.3 shard_map.85
  109.9 3.4 %all-to-all-start.6 = ((bf16[8,16,1024]{2,1,0:T(8,128)(2,1)}), bf16[8,16,1024]{2,1,0:T(8,128)(2,1)S(1)}, u32[]{:S(2)}, u32[]{:S(2)}) async-start(bf16[8,16,1024]{2,1,0:T(8,128)(2,1)} %shard_map.85), calls=%async_computation.6 | async-start | bytes 524288 | tf_op jit(solution)/shard_map/all_to_all | solution.py:437
  113.3 7.4 %all-to-all-done.6.recv = bf16[8,16,1024]{2,1,0:T(8,128)(2,1)S(1)} async-done(((bf16[8,16,1024]{2,1,0:T(8,128)(2,1)}), bf16[8,16,1024]{2,1,0:T(8,128)(2,1)S(1)}, u32[]{:S(2)}, u32[]{:S(2)}) %all-to-all-start.6) | async-done | bytes 262176 | tf_op jit(solution)/shard_map/all_to_all | solution.py:437
  120.7 2.7 %shard_map.86.s1 = bf16[8,16,1024]{2,1,0:T(8,128)(2,1)S(1)} custom-call(s32[2,64]{1,0:T(2,128)S(1)} %copy-done.3, s32[2,64]{1,0:T(2,128)S(1)} %copy-done.4, bf16[8,16,1024]{2,1,0:T(8,128)(2,1)S(1)} %all-to-all-done.6.recv, bf16[16,1024]{1,0:T(8,128)(2,1)S(1)} %get-tuple-element.107.f.f1, s32[2,64,512]{2,1,0:T(8,128)S(1)} %copy-done, ...), custom_call_target="tpu_custom_call" | custom-call | tf_op jit(solution)/shard_map/pallas_call | solution.py:32
  123.4 2.1 %collective-permute-start.14 = (bf16[256,1024]{1,0:T(8,128)(2,1)S(1)}, bf16[256,1024]{1,0:T(8,128)(2,1)S(1)}, u32[]{:S(2)}, u32[]{:S(2)}) collective-permute-start(bf16[256,1024]{1,0:T(8,128)(2,1)S(1)} %get-tuple-element.111), channel_id=1, source_target_pairs={{0,2},{1,3},{2,0},{3,1},{4,6},{5,7},{6,4},{7,5},{8,10},{9,11},{10,... | collective-permute-start | bytes 1572872 | tf_op jit(solution)/shard_map/ppermute | solution.py:364
  125.5 13.9 %all_to_all.50.blocks = bf16[8,16,1024]{2,1,0:T(8,128)(2,1)S(1)} all-to-all(bf16[8,16,1024]{2,1,0:T(8,128)(2,1)S(1)} %shard_map.86.s1), channel_id=1, replica_groups=mesh['z'=8,'x'=4,'core'=2,'panel'=4] {'z'}, dimensions={0} | all-to-all | bytes 524288 | tf_op jit(solution)/shard_map/all_to_all | solution.py:375
  140.0 9.9 %all_to_all.51.recv = bf16[8,16,1024]{2,1,0:T(8,128)(2,1)S(1)} all-to-all(bf16[8,16,1024]{2,1,0:T(8,128)(2,1)S(1)} %shard_map.87), channel_id=1, replica_groups=mesh['z'=8,'x'=4,'core'=2,'panel'=4] {'x','core'}, dimensions={0} | all-to-all | bytes 524288 | tf_op jit(solution)/shard_map/all_to_all | solution.py:450
  150.0 1.6 shard_map.88
  151.5 3.0 %collective-permute-start.15 = (bf16[16,2304]{1,0:T(8,128)(2,1)S(1)}, bf16[16,2304]{1,0:T(8,128)(2,1)S(1)}, u32[]{:S(2)}, u32[]{:S(2)}) collective-permute-start(bf16[16,2304]{1,0:T(8,128)(2,1)S(1)} %get-tuple-element.119), channel_id=1, source_target_pairs={{0,1},{1,2},{2,3},{3,0},{4,5},{5,6},{6,7},{7,4},{8,9},{9,10},{10,1... | collective-permute-start | bytes 221192 | tf_op jit(solution)/shard_map/ppermute | solution.py:364
  155.5 1.8 %collective-permute-done.15.refs_1_ = bf16[16,2304]{1,0:T(8,128)(2,1)S(1)} collective-permute-done((bf16[16,2304]{1,0:T(8,128)(2,1)S(1)}, bf16[16,2304]{1,0:T(8,128)(2,1)S(1)}, u32[]{:S(2)}, u32[]{:S(2)}) %collective-permute-start.15) | collective-permute-done | bytes 73760 | tf_op jit(solution)/shard_map/ppermute | solution.py:364
  157.3 3.1 %collective-permute-done.16.refs_2_ = bf16[16,2304]{1,0:T(8,128)(2,1)S(1)} collective-permute-done((bf16[16,2304]{1,0:T(8,128)(2,1)S(1)}, bf16[16,2304]{1,0:T(8,128)(2,1)S(1)}, u32[]{:S(2)}, u32[]{:S(2)}) %collective-permute-start.16) | collective-permute-done | bytes 73760 | tf_op jit(solution)/shard_map/ppermute | solution.py:364
  (39 shorter events, 7.8 us)
Async XLA Ops:
  1.9 5.7 %collective-permute-start = (bf16[384,128]{1,0:T(8,128)(2,1)S(1)}, bf16[384,128]{1,0:T(8,128)(2,1)S(1)}, u32[]{:S(2)}, u32[]{:S(2)}) collective-permute-start(bf16[384,128]{1,0:T(8,128)(2,1)S(1)} %get-tuple-element.63), channel_id=1, source_target_pairs={{0,1},{1,2},{2,3},{3,0},{4,5},{5,6},{6,7},{7,4},{8,9},{9,10},{10,1... | collective-permute-start | bytes 294920 | tf_op jit(solution)/shard_map/ppermute | solution.py:364
  4.0 10.6 %collective-permute-start.1 = (bf16[384,128]{1,0:T(8,128)(2,1)S(1)}, bf16[384,128]{1,0:T(8,128)(2,1)S(1)}, u32[]{:S(2)}, u32[]{:S(2)}) collective-permute-start(bf16[384,128]{1,0:T(8,128)(2,1)S(1)} %get-tuple-element.66), channel_id=1, source_target_pairs={{0,2},{1,3},{2,0},{3,1},{4,6},{5,7},{6,4},{7,5},{8,10},{9,11},{10,... | collective-permute-start | bytes 294920 | tf_op jit(solution)/shard_map/ppermute | solution.py:364
  4.8 9.7 %collective-permute-start.2 = (bf16[384,128]{1,0:T(8,128)(2,1)S(1)}, bf16[384,128]{1,0:T(8,128)(2,1)S(1)}, u32[]{:S(2)}, u32[]{:S(2)}) collective-permute-start(bf16[384,128]{1,0:T(8,128)(2,1)S(1)} %get-tuple-element.67), channel_id=1, source_target_pairs={{0,3},{1,0},{2,1},{3,2},{4,7},{5,4},{6,5},{7,6},{8,11},{9,8},{10,9... | collective-permute-start | bytes 294920 | tf_op jit(solution)/shard_map/ppermute | solution.py:364
  7.6 7.0 %copy-start.2 = (bf16[3,1,64,256]{3,2,1,0:T(8,128)(2,1)S(1)}, bf16[3,1,64,256]{3,2,1,0:T(8,128)(2,1)}, u32[]{:S(2)}) copy-start(bf16[3,1,64,256]{3,2,1,0:T(8,128)(2,1)} %rhs.3) | copy-start | bytes 294916
  7.6 17.7 %collective-permute-start.5 = (bf16[256,512]{1,0:T(8,128)(2,1)S(1)}, bf16[256,512]{1,0:T(8,128)(2,1)S(1)}, u32[]{:S(2)}, u32[]{:S(2)}) collective-permute-start(bf16[256,512]{1,0:T(8,128)(2,1)S(1)} %get-tuple-element.69.c0), channel_id=1, source_target_pairs={{0,3},{1,0},{2,1},{3,2},{4,7},{5,4},{6,5},{7,6},{8,11},{9,8},{10,9... | collective-permute-start | bytes 786440 | tf_op jit(solution)/shard_map/ppermute | solution.py:364
  7.6 17.7 %collective-permute-start.4 = (bf16[256,512]{1,0:T(8,128)(2,1)S(1)}, bf16[256,512]{1,0:T(8,128)(2,1)S(1)}, u32[]{:S(2)}, u32[]{:S(2)}) collective-permute-start(bf16[256,512]{1,0:T(8,128)(2,1)S(1)} %get-tuple-element.69.c0), channel_id=1, source_target_pairs={{0,2},{1,3},{2,0},{3,1},{4,6},{5,7},{6,4},{7,5},{8,10},{9,11},{10,... | collective-permute-start | bytes 786440 | tf_op jit(solution)/shard_map/ppermute | solution.py:364
  13.0 12.3 %collective-permute-start.3 = (bf16[256,512]{1,0:T(8,128)(2,1)S(1)}, bf16[256,512]{1,0:T(8,128)(2,1)S(1)}, u32[]{:S(2)}, u32[]{:S(2)}) collective-permute-start(bf16[256,512]{1,0:T(8,128)(2,1)S(1)} %get-tuple-element.69.c0), channel_id=1, source_target_pairs={{0,1},{1,2},{2,3},{3,0},{4,5},{5,6},{6,7},{7,4},{8,9},{9,10},{10,1... | collective-permute-start | bytes 786440 | tf_op jit(solution)/shard_map/ppermute | solution.py:364
  14.5 10.8 %copy-start = (s32[2,64,512]{2,1,0:T(8,128)S(1)}, s32[2,64,512]{2,1,0:T(8,128)}, u32[]{:S(2)}) copy-start(s32[2,64,512]{2,1,0:T(8,128)} %lists.7) | copy-start | bytes 786436
  14.5 10.8 %copy-start.4 = (s32[2,64]{1,0:T(2,128)S(1)}, s32[2,64]{1,0:T(2,128)}, u32[]{:S(2)}) copy-start(s32[2,64]{1,0:T(2,128)} %counts.7) | copy-start | bytes 1540
  14.5 31.7 %copy-start.3 = (s32[2,64]{1,0:T(2,128)S(1)}, s32[2,64]{1,0:T(2,128)}, u32[]{:S(2)}) copy-start(s32[2,64]{1,0:T(2,128)} %parents.11) | copy-start | bytes 1540
  26.3 19.8 %collective-permute-start.6 = (bf16[256,1024]{1,0:T(8,128)(2,1)S(1)}, bf16[256,1024]{1,0:T(8,128)(2,1)S(1)}, u32[]{:S(2)}, u32[]{:S(2)}) collective-permute-start(bf16[256,1024]{1,0:T(8,128)(2,1)S(1)} %get-tuple-element.77.i0), channel_id=1, source_target_pairs={{0,1},{1,2},{2,3},{3,0},{4,5},{5,6},{6,7},{7,4},{8,9},{9,10},{10,1... | collective-permute-start | bytes 1572872 | tf_op jit(solution)/shard_map/ppermute | solution.py:364
  28.5 17.7 %collective-permute-start.7 = (bf16[256,1024]{1,0:T(8,128)(2,1)S(1)}, bf16[256,1024]{1,0:T(8,128)(2,1)S(1)}, u32[]{:S(2)}, u32[]{:S(2)}) collective-permute-start(bf16[256,1024]{1,0:T(8,128)(2,1)S(1)} %get-tuple-element.77.i0), channel_id=1, source_target_pairs={{0,3},{1,0},{2,1},{3,2},{4,7},{5,4},{6,5},{7,6},{8,11},{9,8},{10,9... | collective-permute-start | bytes 1572872 | tf_op jit(solution)/shard_map/ppermute | solution.py:364
  46.9 13.9 %collective-permute-start.8 = (bf16[256,1024]{1,0:T(8,128)(2,1)S(1)}, bf16[256,1024]{1,0:T(8,128)(2,1)S(1)}, u32[]{:S(2)}, u32[]{:S(2)}) collective-permute-start(bf16[256,1024]{1,0:T(8,128)(2,1)S(1)} %get-tuple-element.77.i0), channel_id=1, source_target_pairs={{0,2},{1,3},{2,0},{3,1},{4,6},{5,7},{6,4},{7,5},{8,10},{9,11},{10,... | collective-permute-start | bytes 1572872 | tf_op jit(solution)/shard_map/ppermute | solution.py:364
  62.9 31.2 %copy-start.1 = (bf16[4,256,1536]{2,1,0:T(8,128)(2,1)}, bf16[4,256,1536]{2,1,0:T(8,128)(2,1)S(1)}, u32[]{:S(2)}) copy-start(bf16[4,256,1536]{2,1,0:T(8,128)(2,1)S(1)} %get-tuple-element.108.keep) | copy-start | bytes 9437188
  62.9 15.8 %collective-permute-start.9 = (bf16[256,1024]{1,0:T(8,128)(2,1)S(1)}, bf16[256,1024]{1,0:T(8,128)(2,1)S(1)}, u32[]{:S(2)}, u32[]{:S(2)}) collective-permute-start(bf16[256,1024]{1,0:T(8,128)(2,1)S(1)} %get-tuple-element.92.i0), channel_id=1, source_target_pairs={{0,1},{1,2},{2,3},{3,0},{4,5},{5,6},{6,7},{7,4},{8,9},{9,10},{10,1... | collective-permute-start | bytes 1572872 | tf_op jit(solution)/shard_map/ppermute | solution.py:364
  64.6 14.1 %collective-permute-start.10 = (bf16[256,1024]{1,0:T(8,128)(2,1)S(1)}, bf16[256,1024]{1,0:T(8,128)(2,1)S(1)}, u32[]{:S(2)}, u32[]{:S(2)}) collective-permute-start(bf16[256,1024]{1,0:T(8,128)(2,1)S(1)} %get-tuple-element.92.i0), channel_id=1, source_target_pairs={{0,3},{1,0},{2,1},{3,2},{4,7},{5,4},{6,5},{7,6},{8,11},{9,8},{10,9... | collective-permute-start | bytes 1572872 | tf_op jit(solution)/shard_map/ppermute | solution.py:364
  79.3 13.0 %collective-permute-start.11 = (bf16[256,1024]{1,0:T(8,128)(2,1)S(1)}, bf16[256,1024]{1,0:T(8,128)(2,1)S(1)}, u32[]{:S(2)}, u32[]{:S(2)}) collective-permute-start(bf16[256,1024]{1,0:T(8,128)(2,1)S(1)} %get-tuple-element.92.i0), channel_id=1, source_target_pairs={{0,2},{1,3},{2,0},{3,1},{4,6},{5,7},{6,4},{7,5},{8,10},{9,11},{10,... | collective-permute-start | bytes 1572872 | tf_op jit(solution)/shard_map/ppermute | solution.py:364
  94.1 14.5 %all-to-all-start.5 = ((bf16[8,16,1024]{2,1,0:T(8,128)(2,1)}), bf16[8,16,1024]{2,1,0:T(8,128)(2,1)S(1)}, u32[]{:S(2)}, u32[]{:S(2)}) async-start(bf16[8,16,1024]{2,1,0:T(8,128)(2,1)} %get-tuple-element.98.s2), calls=%async_computation.5 | async-start | bytes 524288 | tf_op jit(solution)/shard_map/all_to_all | solution.py:433
  99.5 13.8 %collective-permute-start.12 = (bf16[256,768]{1,0:T(8,128)(2,1)S(1)}, bf16[256,768]{1,0:T(8,128)(2,1)S(1)}, u32[]{:S(2)}, u32[]{:S(2)}) collective-permute-start(bf16[256,768]{1,0:T(8,128)(2,1)S(1)} %get-tuple-element.104), channel_id=1, source_target_pairs={{0,1},{1,2},{2,3},{3,0},{4,5},{5,6},{6,7},{7,4},{8,9},{9,10},{10,1... | collective-permute-start | bytes 1179656 | tf_op jit(solution)/shard_map/ppermute | solution.py:364
  101.3 11.9 %collective-permute-start.13 = (bf16[256,768]{1,0:T(8,128)(2,1)S(1)}, bf16[256,768]{1,0:T(8,128)(2,1)S(1)}, u32[]{:S(2)}, u32[]{:S(2)}) collective-permute-start(bf16[256,768]{1,0:T(8,128)(2,1)S(1)} %get-tuple-element.105), channel_id=1, source_target_pairs={{0,3},{1,0},{2,1},{3,2},{4,7},{5,4},{6,5},{7,6},{8,11},{9,8},{10,9... | collective-permute-start | bytes 1179656 | tf_op jit(solution)/shard_map/ppermute | solution.py:364
  109.9 10.9 %all-to-all-start.6 = ((bf16[8,16,1024]{2,1,0:T(8,128)(2,1)}), bf16[8,16,1024]{2,1,0:T(8,128)(2,1)S(1)}, u32[]{:S(2)}, u32[]{:S(2)}) async-start(bf16[8,16,1024]{2,1,0:T(8,128)(2,1)} %shard_map.85), calls=%async_computation.6 | async-start | bytes 524288 | tf_op jit(solution)/shard_map/all_to_all | solution.py:437
  123.4 16.0 %collective-permute-start.14 = (bf16[256,1024]{1,0:T(8,128)(2,1)S(1)}, bf16[256,1024]{1,0:T(8,128)(2,1)S(1)}, u32[]{:S(2)}, u32[]{:S(2)}) collective-permute-start(bf16[256,1024]{1,0:T(8,128)(2,1)S(1)} %get-tuple-element.111), channel_id=1, source_target_pairs={{0,2},{1,3},{2,0},{3,1},{4,6},{5,7},{6,4},{7,5},{8,10},{9,11},{10,... | collective-permute-start | bytes 1572872 | tf_op jit(solution)/shard_map/ppermute | solution.py:364
  151.5 5.8 %collective-permute-start.15 = (bf16[16,2304]{1,0:T(8,128)(2,1)S(1)}, bf16[16,2304]{1,0:T(8,128)(2,1)S(1)}, u32[]{:S(2)}, u32[]{:S(2)}) collective-permute-start(bf16[16,2304]{1,0:T(8,128)(2,1)S(1)} %get-tuple-element.119), channel_id=1, source_target_pairs={{0,1},{1,2},{2,3},{3,0},{4,5},{5,6},{6,7},{7,4},{8,9},{9,10},{10,1... | collective-permute-start | bytes 221192 | tf_op jit(solution)/shard_map/ppermute | solution.py:364
  154.5 5.9 %collective-permute-start.16 = (bf16[16,2304]{1,0:T(8,128)(2,1)S(1)}, bf16[16,2304]{1,0:T(8,128)(2,1)S(1)}, u32[]{:S(2)}, u32[]{:S(2)}) collective-permute-start(bf16[16,2304]{1,0:T(8,128)(2,1)S(1)} %get-tuple-element.120), channel_id=1, source_target_pairs={{0,2},{1,3},{2,0},{3,1},{4,6},{5,7},{6,4},{7,5},{8,10},{9,11},{10,... | collective-permute-start | bytes 221192 | tf_op jit(solution)/shard_map/ppermute | solution.py:364
  154.8 6.3 %collective-permute-start.17 = (bf16[16,2304]{1,0:T(8,128)(2,1)S(1)}, bf16[16,2304]{1,0:T(8,128)(2,1)S(1)}, u32[]{:S(2)}, u32[]{:S(2)}) collective-permute-start(bf16[16,2304]{1,0:T(8,128)(2,1)S(1)} %get-tuple-element.121), channel_id=1, source_target_pairs={{0,3},{1,0},{2,1},{3,2},{4,7},{5,4},{6,5},{7,6},{8,11},{9,8},{10,9... | collective-permute-start | bytes 221192 | tf_op jit(solution)/shard_map/ppermute | solution.py:364

commit v7 on v6

--- a/solution.py
+++ b/solution.py
@@ -155,7 +155,9 @@
     )
 
 
-def up0_body(counts, got, lists, out):
+def up0_body(counts, got, lists, inv, out, share, sem):
+    copy = pltpu.make_async_copy(inv.at[1, 0], share, sem)
+    copy.start()
     placed = place(0, counts, lists, out.shape[2])
     panels = got.shape[0]
     pieces = []
@@ -168,6 +170,7 @@
     e = laid_out(0, jnp.concatenate(pieces, axis=1), placed, counts)
     for d in range(out.shape[0]):
         out[d] = e
+    copy.wait()
 
 
 def summed(recv):
@@ -383,10 +386,10 @@
         scratch=[pltpu.SemaphoreType.DMA((4 * panels - 2,))],
     )
     packs = [shifted(x, k) for k, x in enumerate(packs, 1)]
-    base, in1, in2 = (inv_diag[level, 0] for level in range(3))
+    base, in2 = inv_diag[0, 0], inv_diag[2, 0]
     packs[0], c1 = after((packs[0], c1))
     c11, c12, c13 = (shifted(c1, k) for k in range(1, panels))
-    base, in1, in2 = after((base, in1, in2))
+    base, in2 = after((base, in2))
     send = call(
         first_body, sds(panels, 14, rows, half), rhs, own, *packs, base,
     )
@@ -394,7 +397,11 @@
     got, c11, c12, c13 = after((got, c11, c12, c13))
     touched = pltpu.VMEM((rows, panels * half), BF)
     wide = pltpu.VMEM((rows, panels * half), F32)
-    e = call(up0_body, sds(*mid), counts, got, row_lists, specs=[SMEM] + [VMEM] * 2)
+    e, in1 = call(
+        up0_body, [sds(*mid), sds(*inv_diag.shape[2:])], counts, got, row_lists, inv_diag,
+        specs=[SMEM] + [VMEM] * 2 + [HBM], outs_at=[VMEM, HBM],
+        scratch=[pltpu.SemaphoreType.DMA],
+    )
 
     def fold(e, level, table):
         return call(

time: 163 us -> 163 us (level)
  no operation moved by 1% of the time
where the time goes in v7:
time: 163 us
  blocking collectives  87.3 us (54%)
  starting transfers between devices  32.1 us (20%)
  waiting for transfers between devices  23.6 us (14%)
  Pallas kernels  17.6 us (11%)
    all_to_all x5, blocking collectives, exchange(): x = lax.all_to_all(x, axes, 0, 0)  67.1 us
    ppermute x18, starting transfers between devices, shifted(): lax.ppermute(x, 'panel', [(i, (i + k) % panels) for i in range(panels)])  25.3 us
    pallas_call x13, Pallas kernels, call(): pl.pallas_call(body, out_shape=tuple(outs) if isinstance(outs, list) else...  17.6 us
    all_to_all x1, blocking collectives, local(): got = lax.all_to_all(send, 'panel', 0, 0)  10.2 us
    all_to_all x1, blocking collectives, local(): s = lax.all_to_all(s, ('x', 'core'), 0, 0)  9.95 us
    ppermute x18, waiting for transfers between devices, shifted(): lax.ppermute(x, 'panel', [(i, (i + k) % panels) for i in range(panels)])  9.31 us
    all_to_all x1, waiting for transfers between devices, local(): s = lax.all_to_all(s, ('x', 'core'), 0, 0)  7.44 us
    all_to_all x1, waiting for transfers between devices, local(): s = lax.all_to_all(s, 'z', 0, 0)  6.81 us
  transfers between devices with their start and end apart: 20, of which 7 were waited for; matrix products, arithmetic and copies ran while one was open for 1% of the time, Pallas kernels for 2%

profile of v7, /device:TPU:24, one launch (start us, length us, event | category | flops | bytes accessed | tf_op | source)
XLA Modules:
  0.0 162.7 jit_solution(18221305645302112751)
XLA Ops:
  0.6 1.3 shard_map.77
  1.9 2.0 %collective-permute-start = (bf16[384,128]{1,0:T(8,128)(2,1)S(1)}, bf16[384,128]{1,0:T(8,128)(2,1)S(1)}, u32[]{:S(2)}, u32[]{:S(2)}) collective-permute-start(bf16[384,128]{1,0:T(8,128)(2,1)S(1)} %get-tuple-element.64), channel_id=1, source_target_pairs={{0,1},{1,2},{2,3},{3,0},{4,5},{5,6},{6,7},{7,4},{8,9},{9,10},{10,1... | collective-permute-start | bytes 294920 | tf_op jit(solution)/shard_map/ppermute | solution.py:367
  4.9 2.7 %collective-permute-done.m1 = bf16[384,128]{1,0:T(8,128)(2,1)S(1)} collective-permute-done((bf16[384,128]{1,0:T(8,128)(2,1)S(1)}, bf16[384,128]{1,0:T(8,128)(2,1)S(1)}, u32[]{:S(2)}, u32[]{:S(2)}) %collective-permute-start) | collective-permute-done | bytes 98336 | tf_op jit(solution)/shard_map/ppermute | solution.py:367
  7.6 5.4 %collective-permute-start.4 = (bf16[256,512]{1,0:T(8,128)(2,1)S(1)}, bf16[256,512]{1,0:T(8,128)(2,1)S(1)}, u32[]{:S(2)}, u32[]{:S(2)}) collective-permute-start(bf16[256,512]{1,0:T(8,128)(2,1)S(1)} %get-tuple-element.70.c0), channel_id=1, source_target_pairs={{0,2},{1,3},{2,0},{3,1},{4,6},{5,7},{6,4},{7,5},{8,10},{9,11},{10,... | collective-permute-start | bytes 786440 | tf_op jit(solution)/shard_map/ppermute | solution.py:367
  13.1 1.3 slice_bitcast_fusion
  14.9 10.2 %all_to_all.45.got = bf16[4,14,16,128]{3,2,1,0:T(8,128)(2,1)S(1)} all-to-all(bf16[4,14,16,128]{3,2,1,0:T(8,128)(2,1)S(1)} %shard_map.78), channel_id=1, replica_groups=mesh['z'=8,'x'=4,'core'=2,'panel'=4] {'panel'}, dimensions={0} | all-to-all | bytes 458752 | tf_op jit(solution)/shard_map/all_to_all | solution.py:396
  25.1 1.6 shard_map.79
  26.8 2.1 %collective-permute-start.6 = (bf16[256,1024]{1,0:T(8,128)(2,1)S(1)}, bf16[256,1024]{1,0:T(8,128)(2,1)S(1)}, u32[]{:S(2)}, u32[]{:S(2)}) collective-permute-start(bf16[256,1024]{1,0:T(8,128)(2,1)S(1)} %get-tuple-element.79.i0), channel_id=1, source_target_pairs={{0,1},{1,2},{2,3},{3,0},{4,5},{5,6},{6,7},{7,4},{8,9},{9,10},{10,1... | collective-permute-start | bytes 1572872 | tf_op jit(solution)/shard_map/ppermute | solution.py:367
  28.9 17.9 %all_to_all.46.blocks = bf16[8,16,1024]{2,1,0:T(8,128)(2,1)S(1)} all-to-all(bf16[8,16,1024]{2,1,0:T(8,128)(2,1)S(1)} %get-tuple-element.74), channel_id=1, replica_groups=mesh['z'=8,'x'=4,'core'=2,'panel'=4] {'z'}, dimensions={0} | all-to-all | bytes 524288 | tf_op jit(solution)/shard_map/all_to_all | solution.py:378
  47.5 2.2 %collective-permute-start.8 = (bf16[256,1024]{1,0:T(8,128)(2,1)S(1)}, bf16[256,1024]{1,0:T(8,128)(2,1)S(1)}, u32[]{:S(2)}, u32[]{:S(2)}) collective-permute-start(bf16[256,1024]{1,0:T(8,128)(2,1)S(1)} %get-tuple-element.79.i0), channel_id=1, source_target_pairs={{0,2},{1,3},{2,0},{3,1},{4,6},{5,7},{6,4},{7,5},{8,10},{9,11},{10,... | collective-permute-start | bytes 1572872 | tf_op jit(solution)/shard_map/ppermute | solution.py:367
  49.7 11.6 %all_to_all.47.recv = bf16[8,16,1024]{2,1,0:T(8,128)(2,1)S(1)} all-to-all(bf16[8,16,1024]{2,1,0:T(8,128)(2,1)S(1)} %shard_map.80), channel_id=1, replica_groups=mesh['z'=8,'x'=4,'core'=2,'panel'=4] {'x','core'}, dimensions={0} | all-to-all | bytes 524288 | tf_op jit(solution)/shard_map/all_to_all | solution.py:378
  61.4 2.1 %shard_map.81 = (bf16[16,1024]{1,0:T(8,128)(2,1)S(1)}, bf16[8,16,1024]{2,1,0:T(8,128)(2,1)S(1)}, bf16[4,256,1536]{2,1,0:T(8,128)(2,1)S(1)}) custom-call(s32[2,64]{1,0:T(2,128)S(1)} %copy-done.4, bf16[8,16,1024]{2,1,0:T(8,128)(2,1)S(1)} %all_to_all.47.recv, bf16[4,14,16,128]{3,2,1,0:T(8,128)(2,1)S(1)} %all_to_all.45.got, s32[2,64,512]{2,1,0:T(8,128)S(1)} %copy-done, ...), custom_call_target="tpu_custom_call" | custom-call | tf_op jit(solution)/shard_map/pallas_call | solution.py:32
  63.5 1.7 %collective-permute-start.9 = (bf16[256,1024]{1,0:T(8,128)(2,1)S(1)}, bf16[256,1024]{1,0:T(8,128)(2,1)S(1)}, u32[]{:S(2)}, u32[]{:S(2)}) collective-permute-start(bf16[256,1024]{1,0:T(8,128)(2,1)S(1)} %get-tuple-element.94.i0), channel_id=1, source_target_pairs={{0,1},{1,2},{2,3},{3,0},{4,5},{5,6},{6,7},{7,4},{8,9},{9,10},{10,1... | collective-permute-start | bytes 1572872 | tf_op jit(solution)/shard_map/ppermute | solution.py:367
  65.6 13.7 %all_to_all.48.blocks = bf16[8,16,1024]{2,1,0:T(8,128)(2,1)S(1)} all-to-all(bf16[8,16,1024]{2,1,0:T(8,128)(2,1)S(1)} %get-tuple-element.89), channel_id=1, replica_groups=mesh['z'=8,'x'=4,'core'=2,'panel'=4] {'z'}, dimensions={0} | all-to-all | bytes 524288 | tf_op jit(solution)/shard_map/all_to_all | solution.py:378
  80.0 2.1 %collective-permute-start.11 = (bf16[256,1024]{1,0:T(8,128)(2,1)S(1)}, bf16[256,1024]{1,0:T(8,128)(2,1)S(1)}, u32[]{:S(2)}, u32[]{:S(2)}) collective-permute-start(bf16[256,1024]{1,0:T(8,128)(2,1)S(1)} %get-tuple-element.94.i0), channel_id=1, source_target_pairs={{0,2},{1,3},{2,0},{3,1},{4,6},{5,7},{6,4},{7,5},{8,10},{9,11},{10,... | collective-permute-start | bytes 1572872 | tf_op jit(solution)/shard_map/ppermute | solution.py:367
  82.1 10.0 %all_to_all.49.recv = bf16[8,16,1024]{2,1,0:T(8,128)(2,1)S(1)} all-to-all(bf16[8,16,1024]{2,1,0:T(8,128)(2,1)S(1)} %shard_map.82), channel_id=1, replica_groups=mesh['z'=8,'x'=4,'core'=2,'panel'=4] {'x','core'}, dimensions={0} | all-to-all | bytes 524288 | tf_op jit(solution)/shard_map/all_to_all | solution.py:378
  93.0 1.7 %shard_map.83 = (bf16[16,1024]{1,0:T(8,128)(2,1)S(1)}, bf16[8,16,1024]{2,1,0:T(8,128)(2,1)}) custom-call(bf16[8,16,1024]{2,1,0:T(8,128)(2,1)S(1)} %all_to_all.49.recv, bf16[4,14,16,128]{3,2,1,0:T(8,128)(2,1)S(1)} %all_to_all.45.got, bf16[256,1024]{1,0:T(8,128)(2,1)S(1)} %get-tuple-element.94.i0, bf16[256,1024]{1,0:T(8,128)(2,1)S(1)} %collective-permute-done.9.i1, ...), custom_call_target="tpu_custom_call" | custom-call | tf_op jit(solution)/shard_map/pallas_call | solution.py:32
  94.7 3.4 %all-to-all-start.5 = ((bf16[8,16,1024]{2,1,0:T(8,128)(2,1)}), bf16[8,16,1024]{2,1,0:T(8,128)(2,1)S(1)}, u32[]{:S(2)}, u32[]{:S(2)}) async-start(bf16[8,16,1024]{2,1,0:T(8,128)(2,1)} %get-tuple-element.100.s2), calls=%async_computation.5 | async-start | bytes 524288 | tf_op jit(solution)/shard_map/all_to_all | solution.py:440
  98.1 2.0 %shard_map.84 = (bf16[256,768]{1,0:T(8,128)(2,1)S(1)}, bf16[256,768]{1,0:T(8,128)(2,1)S(1)}, bf16[256,1024]{1,0:T(8,128)(2,1)S(1)}, bf16[256,768]{1,0:T(8,128)(2,1)S(1)}) custom-call(bf16[2,1,1024,128]{3,2,1,0:T(8,128)(2,1)} %coupling.2, bf16[3,1,256,1024]{3,2,1,0:T(8,128)(2,1)} %inv.2), custom_call_target="tpu_custom_call" | custom-call | tf_op jit(solution)/shard_map/pallas_call | solution.py:32
  100.1 1.9 %collective-permute-start.12 = (bf16[256,768]{1,0:T(8,128)(2,1)S(1)}, bf16[256,768]{1,0:T(8,128)(2,1)S(1)}, u32[]{:S(2)}, u32[]{:S(2)}) collective-permute-start(bf16[256,768]{1,0:T(8,128)(2,1)S(1)} %get-tuple-element.106), channel_id=1, source_target_pairs={{0,1},{1,2},{2,3},{3,0},{4,5},{5,6},{6,7},{7,4},{8,9},{9,10},{10,1... | collective-permute-start | bytes 1179656 | tf_op jit(solution)/shard_map/ppermute | solution.py:367
  102.4 6.8 %all-to-all-done.5.blocks = bf16[8,16,1024]{2,1,0:T(8,128)(2,1)S(1)} async-done(((bf16[8,16,1024]{2,1,0:T(8,128)(2,1)}), bf16[8,16,1024]{2,1,0:T(8,128)(2,1)S(1)}, u32[]{:S(2)}, u32[]{:S(2)}) %all-to-all-start.5) | async-done | bytes 262176 | tf_op jit(solution)/shard_map/all_to_all | solution.py:440
  109.2 1.3 shard_map.85
  110.5 3.4 %all-to-all-start.6 = ((bf16[8,16,1024]{2,1,0:T(8,128)(2,1)}), bf16[8,16,1024]{2,1,0:T(8,128)(2,1)S(1)}, u32[]{:S(2)}, u32[]{:S(2)}) async-start(bf16[8,16,1024]{2,1,0:T(8,128)(2,1)} %shard_map.85), calls=%async_computation.6 | async-start | bytes 524288 | tf_op jit(solution)/shard_map/all_to_all | solution.py:444
  113.9 7.4 %all-to-all-done.6.recv = bf16[8,16,1024]{2,1,0:T(8,128)(2,1)S(1)} async-done(((bf16[8,16,1024]{2,1,0:T(8,128)(2,1)}), bf16[8,16,1024]{2,1,0:T(8,128)(2,1)S(1)}, u32[]{:S(2)}, u32[]{:S(2)}) %all-to-all-start.6) | async-done | bytes 262176 | tf_op jit(solution)/shard_map/all_to_all | solution.py:444
  121.4 2.7 %shard_map.86.s1 = bf16[8,16,1024]{2,1,0:T(8,128)(2,1)S(1)} custom-call(s32[2,64]{1,0:T(2,128)S(1)} %copy-done.3, s32[2,64]{1,0:T(2,128)S(1)} %copy-done.4, bf16[8,16,1024]{2,1,0:T(8,128)(2,1)S(1)} %all-to-all-done.6.recv, bf16[16,1024]{1,0:T(8,128)(2,1)S(1)} %get-tuple-element.109.f.f1, s32[2,64,512]{2,1,0:T(8,128)S(1)} %copy-done, ...), custom_call_target="tpu_custom_call" | custom-call | tf_op jit(solution)/shard_map/pallas_call | solution.py:32
  124.1 2.1 %collective-permute-start.14 = (bf16[256,1024]{1,0:T(8,128)(2,1)S(1)}, bf16[256,1024]{1,0:T(8,128)(2,1)S(1)}, u32[]{:S(2)}, u32[]{:S(2)}) collective-permute-start(bf16[256,1024]{1,0:T(8,128)(2,1)S(1)} %get-tuple-element.113), channel_id=1, source_target_pairs={{0,2},{1,3},{2,0},{3,1},{4,6},{5,7},{6,4},{7,5},{8,10},{9,11},{10,... | collective-permute-start | bytes 1572872 | tf_op jit(solution)/shard_map/ppermute | solution.py:367
  126.2 13.9 %all_to_all.50.blocks = bf16[8,16,1024]{2,1,0:T(8,128)(2,1)S(1)} all-to-all(bf16[8,16,1024]{2,1,0:T(8,128)(2,1)S(1)} %shard_map.86.s1), channel_id=1, replica_groups=mesh['z'=8,'x'=4,'core'=2,'panel'=4] {'z'}, dimensions={0} | all-to-all | bytes 524288 | tf_op jit(solution)/shard_map/all_to_all | solution.py:378
  140.7 9.9 %all_to_all.51.recv = bf16[8,16,1024]{2,1,0:T(8,128)(2,1)S(1)} all-to-all(bf16[8,16,1024]{2,1,0:T(8,128)(2,1)S(1)} %shard_map.87), channel_id=1, replica_groups=mesh['z'=8,'x'=4,'core'=2,'panel'=4] {'x','core'}, dimensions={0} | all-to-all | bytes 524288 | tf_op jit(solution)/shard_map/all_to_all | solution.py:457
  150.6 1.6 shard_map.88
  152.2 3.0 %collective-permute-start.15 = (bf16[16,2304]{1,0:T(8,128)(2,1)S(1)}, bf16[16,2304]{1,0:T(8,128)(2,1)S(1)}, u32[]{:S(2)}, u32[]{:S(2)}) collective-permute-start(bf16[16,2304]{1,0:T(8,128)(2,1)S(1)} %get-tuple-element.121), channel_id=1, source_target_pairs={{0,1},{1,2},{2,3},{3,0},{4,5},{5,6},{6,7},{7,4},{8,9},{9,10},{10,1... | collective-permute-start | bytes 221192 | tf_op jit(solution)/shard_map/ppermute | solution.py:367
  156.1 1.9 %collective-permute-done.15.refs_1_ = bf16[16,2304]{1,0:T(8,128)(2,1)S(1)} collective-permute-done((bf16[16,2304]{1,0:T(8,128)(2,1)S(1)}, bf16[16,2304]{1,0:T(8,128)(2,1)S(1)}, u32[]{:S(2)}, u32[]{:S(2)}) %collective-permute-start.15) | collective-permute-done | bytes 73760 | tf_op jit(solution)/shard_map/ppermute | solution.py:367
  158.0 3.1 %collective-permute-done.16.refs_2_ = bf16[16,2304]{1,0:T(8,128)(2,1)S(1)} collective-permute-done((bf16[16,2304]{1,0:T(8,128)(2,1)S(1)}, bf16[16,2304]{1,0:T(8,128)(2,1)S(1)}, u32[]{:S(2)}, u32[]{:S(2)}) %collective-permute-start.16) | collective-permute-done | bytes 73760 | tf_op jit(solution)/shard_map/ppermute | solution.py:367
  (39 shorter events, 7.8 us)
Async XLA Ops:
  0.6 13.7 %copy-start.2 = (bf16[3,1,64,256]{3,2,1,0:T(8,128)(2,1)S(1)}, bf16[3,1,64,256]{3,2,1,0:T(8,128)(2,1)}, u32[]{:S(2)}) copy-start(bf16[3,1,64,256]{3,2,1,0:T(8,128)(2,1)} %rhs.3) | copy-start | bytes 294916
  1.9 5.7 %collective-permute-start = (bf16[384,128]{1,0:T(8,128)(2,1)S(1)}, bf16[384,128]{1,0:T(8,128)(2,1)S(1)}, u32[]{:S(2)}, u32[]{:S(2)}) collective-permute-start(bf16[384,128]{1,0:T(8,128)(2,1)S(1)} %get-tuple-element.64), channel_id=1, source_target_pairs={{0,1},{1,2},{2,3},{3,0},{4,5},{5,6},{6,7},{7,4},{8,9},{9,10},{10,1... | collective-permute-start | bytes 294920 | tf_op jit(solution)/shard_map/ppermute | solution.py:367
  4.0 10.3 %collective-permute-start.1 = (bf16[384,128]{1,0:T(8,128)(2,1)S(1)}, bf16[384,128]{1,0:T(8,128)(2,1)S(1)}, u32[]{:S(2)}, u32[]{:S(2)}) collective-permute-start(bf16[384,128]{1,0:T(8,128)(2,1)S(1)} %get-tuple-element.67), channel_id=1, source_target_pairs={{0,2},{1,3},{2,0},{3,1},{4,6},{5,7},{6,4},{7,5},{8,10},{9,11},{10,... | collective-permute-start | bytes 294920 | tf_op jit(solution)/shard_map/ppermute | solution.py:367
  4.8 9.5 %collective-permute-start.2 = (bf16[384,128]{1,0:T(8,128)(2,1)S(1)}, bf16[384,128]{1,0:T(8,128)(2,1)S(1)}, u32[]{:S(2)}, u32[]{:S(2)}) collective-permute-start(bf16[384,128]{1,0:T(8,128)(2,1)S(1)} %get-tuple-element.68), channel_id=1, source_target_pairs={{0,3},{1,0},{2,1},{3,2},{4,7},{5,4},{6,5},{7,6},{8,11},{9,8},{10,9... | collective-permute-start | bytes 294920 | tf_op jit(solution)/shard_map/ppermute | solution.py:367
  7.6 17.5 %copy-start = (s32[2,64,512]{2,1,0:T(8,128)S(1)}, s32[2,64,512]{2,1,0:T(8,128)}, u32[]{:S(2)}) copy-start(s32[2,64,512]{2,1,0:T(8,128)} %lists.7) | copy-start | bytes 786436
  7.6 17.5 %copy-start.4 = (s32[2,64]{1,0:T(2,128)S(1)}, s32[2,64]{1,0:T(2,128)}, u32[]{:S(2)}) copy-start(s32[2,64]{1,0:T(2,128)} %counts.7) | copy-start | bytes 1540
  7.6 17.5 %collective-permute-start.5 = (bf16[256,512]{1,0:T(8,128)(2,1)S(1)}, bf16[256,512]{1,0:T(8,128)(2,1)S(1)}, u32[]{:S(2)}, u32[]{:S(2)}) collective-permute-start(bf16[256,512]{1,0:T(8,128)(2,1)S(1)} %get-tuple-element.70.c0), channel_id=1, source_target_pairs={{0,3},{1,0},{2,1},{3,2},{4,7},{5,4},{6,5},{7,6},{8,11},{9,8},{10,9... | collective-permute-start | bytes 786440 | tf_op jit(solution)/shard_map/ppermute | solution.py:367
  7.6 17.5 %collective-permute-start.4 = (bf16[256,512]{1,0:T(8,128)(2,1)S(1)}, bf16[256,512]{1,0:T(8,128)(2,1)S(1)}, u32[]{:S(2)}, u32[]{:S(2)}) collective-permute-start(bf16[256,512]{1,0:T(8,128)(2,1)S(1)} %get-tuple-element.70.c0), channel_id=1, source_target_pairs={{0,2},{1,3},{2,0},{3,1},{4,6},{5,7},{6,4},{7,5},{8,10},{9,11},{10,... | collective-permute-start | bytes 786440 | tf_op jit(solution)/shard_map/ppermute | solution.py:367
  13.0 12.1 %collective-permute-start.3 = (bf16[256,512]{1,0:T(8,128)(2,1)S(1)}, bf16[256,512]{1,0:T(8,128)(2,1)S(1)}, u32[]{:S(2)}, u32[]{:S(2)}) collective-permute-start(bf16[256,512]{1,0:T(8,128)(2,1)S(1)} %get-tuple-element.70.c0), channel_id=1, source_target_pairs={{0,1},{1,2},{2,3},{3,0},{4,5},{5,6},{6,7},{7,4},{8,9},{9,10},{10,1... | collective-permute-start | bytes 786440 | tf_op jit(solution)/shard_map/ppermute | solution.py:367
  14.9 31.9 %copy-start.3 = (s32[2,64]{1,0:T(2,128)S(1)}, s32[2,64]{1,0:T(2,128)}, u32[]{:S(2)}) copy-start(s32[2,64]{1,0:T(2,128)} %parents.11) | copy-start | bytes 1540
  26.8 20.1 %collective-permute-start.6 = (bf16[256,1024]{1,0:T(8,128)(2,1)S(1)}, bf16[256,1024]{1,0:T(8,128)(2,1)S(1)}, u32[]{:S(2)}, u32[]{:S(2)}) collective-permute-start(bf16[256,1024]{1,0:T(8,128)(2,1)S(1)} %get-tuple-element.79.i0), channel_id=1, source_target_pairs={{0,1},{1,2},{2,3},{3,0},{4,5},{5,6},{6,7},{7,4},{8,9},{9,10},{10,1... | collective-permute-start | bytes 1572872 | tf_op jit(solution)/shard_map/ppermute | solution.py:367
  28.9 17.9 %collective-permute-start.7 = (bf16[256,1024]{1,0:T(8,128)(2,1)S(1)}, bf16[256,1024]{1,0:T(8,128)(2,1)S(1)}, u32[]{:S(2)}, u32[]{:S(2)}) collective-permute-start(bf16[256,1024]{1,0:T(8,128)(2,1)S(1)} %get-tuple-element.79.i0), channel_id=1, source_target_pairs={{0,3},{1,0},{2,1},{3,2},{4,7},{5,4},{6,5},{7,6},{8,11},{9,8},{10,9... | collective-permute-start | bytes 1572872 | tf_op jit(solution)/shard_map/ppermute | solution.py:367
  47.5 13.9 %collective-permute-start.8 = (bf16[256,1024]{1,0:T(8,128)(2,1)S(1)}, bf16[256,1024]{1,0:T(8,128)(2,1)S(1)}, u32[]{:S(2)}, u32[]{:S(2)}) collective-permute-start(bf16[256,1024]{1,0:T(8,128)(2,1)S(1)} %get-tuple-element.79.i0), channel_id=1, source_target_pairs={{0,2},{1,3},{2,0},{3,1},{4,6},{5,7},{6,4},{7,5},{8,10},{9,11},{10,... | collective-permute-start | bytes 1572872 | tf_op jit(solution)/shard_map/ppermute | solution.py:367
  63.5 31.2 %copy-start.1 = (bf16[4,256,1536]{2,1,0:T(8,128)(2,1)}, bf16[4,256,1536]{2,1,0:T(8,128)(2,1)S(1)}, u32[]{:S(2)}) copy-start(bf16[4,256,1536]{2,1,0:T(8,128)(2,1)S(1)} %get-tuple-element.110.keep) | copy-start | bytes 9437188
  63.5 15.8 %collective-permute-start.9 = (bf16[256,1024]{1,0:T(8,128)(2,1)S(1)}, bf16[256,1024]{1,0:T(8,128)(2,1)S(1)}, u32[]{:S(2)}, u32[]{:S(2)}) collective-permute-start(bf16[256,1024]{1,0:T(8,128)(2,1)S(1)} %get-tuple-element.94.i0), channel_id=1, source_target_pairs={{0,1},{1,2},{2,3},{3,0},{4,5},{5,6},{6,7},{7,4},{8,9},{9,10},{10,1... | collective-permute-start | bytes 1572872 | tf_op jit(solution)/shard_map/ppermute | solution.py:367
  65.2 14.1 %collective-permute-start.10 = (bf16[256,1024]{1,0:T(8,128)(2,1)S(1)}, bf16[256,1024]{1,0:T(8,128)(2,1)S(1)}, u32[]{:S(2)}, u32[]{:S(2)}) collective-permute-start(bf16[256,1024]{1,0:T(8,128)(2,1)S(1)} %get-tuple-element.94.i0), channel_id=1, source_target_pairs={{0,3},{1,0},{2,1},{3,2},{4,7},{5,4},{6,5},{7,6},{8,11},{9,8},{10,9... | collective-permute-start | bytes 1572872 | tf_op jit(solution)/shard_map/ppermute | solution.py:367
  80.0 13.0 %collective-permute-start.11 = (bf16[256,1024]{1,0:T(8,128)(2,1)S(1)}, bf16[256,1024]{1,0:T(8,128)(2,1)S(1)}, u32[]{:S(2)}, u32[]{:S(2)}) collective-permute-start(bf16[256,1024]{1,0:T(8,128)(2,1)S(1)} %get-tuple-element.94.i0), channel_id=1, source_target_pairs={{0,2},{1,3},{2,0},{3,1},{4,6},{5,7},{6,4},{7,5},{8,10},{9,11},{10,... | collective-permute-start | bytes 1572872 | tf_op jit(solution)/shard_map/ppermute | solution.py:367
  94.7 14.5 %all-to-all-start.5 = ((bf16[8,16,1024]{2,1,0:T(8,128)(2,1)}), bf16[8,16,1024]{2,1,0:T(8,128)(2,1)S(1)}, u32[]{:S(2)}, u32[]{:S(2)}) async-start(bf16[8,16,1024]{2,1,0:T(8,128)(2,1)} %get-tuple-element.100.s2), calls=%async_computation.5 | async-start | bytes 524288 | tf_op jit(solution)/shard_map/all_to_all | solution.py:440
  100.1 13.8 %collective-permute-start.12 = (bf16[256,768]{1,0:T(8,128)(2,1)S(1)}, bf16[256,768]{1,0:T(8,128)(2,1)S(1)}, u32[]{:S(2)}, u32[]{:S(2)}) collective-permute-start(bf16[256,768]{1,0:T(8,128)(2,1)S(1)} %get-tuple-element.106), channel_id=1, source_target_pairs={{0,1},{1,2},{2,3},{3,0},{4,5},{5,6},{6,7},{7,4},{8,9},{9,10},{10,1... | collective-permute-start | bytes 1179656 | tf_op jit(solution)/shard_map/ppermute | solution.py:367
  102.0 12.0 %collective-permute-start.13 = (bf16[256,768]{1,0:T(8,128)(2,1)S(1)}, bf16[256,768]{1,0:T(8,128)(2,1)S(1)}, u32[]{:S(2)}, u32[]{:S(2)}) collective-permute-start(bf16[256,768]{1,0:T(8,128)(2,1)S(1)} %get-tuple-element.107), channel_id=1, source_target_pairs={{0,3},{1,0},{2,1},{3,2},{4,7},{5,4},{6,5},{7,6},{8,11},{9,8},{10,9... | collective-permute-start | bytes 1179656 | tf_op jit(solution)/shard_map/ppermute | solution.py:367
  110.5 10.9 %all-to-all-start.6 = ((bf16[8,16,1024]{2,1,0:T(8,128)(2,1)}), bf16[8,16,1024]{2,1,0:T(8,128)(2,1)S(1)}, u32[]{:S(2)}, u32[]{:S(2)}) async-start(bf16[8,16,1024]{2,1,0:T(8,128)(2,1)} %shard_map.85), calls=%async_computation.6 | async-start | bytes 524288 | tf_op jit(solution)/shard_map/all_to_all | solution.py:444
  124.1 16.0 %collective-permute-start.14 = (bf16[256,1024]{1,0:T(8,128)(2,1)S(1)}, bf16[256,1024]{1,0:T(8,128)(2,1)S(1)}, u32[]{:S(2)}, u32[]{:S(2)}) collective-permute-start(bf16[256,1024]{1,0:T(8,128)(2,1)S(1)} %get-tuple-element.113), channel_id=1, source_target_pairs={{0,2},{1,3},{2,0},{3,1},{4,6},{5,7},{6,4},{7,5},{8,10},{9,11},{10,... | collective-permute-start | bytes 1572872 | tf_op jit(solution)/shard_map/ppermute | solution.py:367
  152.2 5.8 %collective-permute-start.15 = (bf16[16,2304]{1,0:T(8,128)(2,1)S(1)}, bf16[16,2304]{1,0:T(8,128)(2,1)S(1)}, u32[]{:S(2)}, u32[]{:S(2)}) collective-permute-start(bf16[16,2304]{1,0:T(8,128)(2,1)S(1)} %get-tuple-element.121), channel_id=1, source_target_pairs={{0,1},{1,2},{2,3},{3,0},{4,5},{5,6},{6,7},{7,4},{8,9},{9,10},{10,1... | collective-permute-start | bytes 221192 | tf_op jit(solution)/shard_map/ppermute | solution.py:367
  155.2 5.9 %collective-permute-start.16 = (bf16[16,2304]{1,0:T(8,128)(2,1)S(1)}, bf16[16,2304]{1,0:T(8,128)(2,1)S(1)}, u32[]{:S(2)}, u32[]{:S(2)}) collective-permute-start(bf16[16,2304]{1,0:T(8,128)(2,1)S(1)} %get-tuple-element.122), channel_id=1, source_target_pairs={{0,2},{1,3},{2,0},{3,1},{4,6},{5,7},{6,4},{7,5},{8,10},{9,11},{10,... | collective-permute-start | bytes 221192 | tf_op jit(solution)/shard_map/ppermute | solution.py:367
  155.5 6.3 %collective-permute-start.17 = (bf16[16,2304]{1,0:T(8,128)(2,1)S(1)}, bf16[16,2304]{1,0:T(8,128)(2,1)S(1)}, u32[]{:S(2)}, u32[]{:S(2)}) collective-permute-start(bf16[16,2304]{1,0:T(8,128)(2,1)S(1)} %get-tuple-element.123), channel_id=1, source_target_pairs={{0,3},{1,0},{2,1},{3,2},{4,7},{5,4},{6,5},{7,6},{8,11},{9,8},{10,9... | collective-permute-start | bytes 221192 | tf_op jit(solution)/shard_map/ppermute | solution.py:367
